TPU v7x, 32 devices: a whole 2x2x4 slice. The times are simulated.
32 devices in a mesh: shot: 2 (over x), freq: 16 (over z, y, core).
Axes of the slice: x: 2, y: 2, z: 4, core: 2. Of those that a mesh axis runs over, the one named last changes fastest.
Arguments:
- receiver_data: float32 [64, 2, 32, 1024], P(('shot', 'freq')), parts along dimension 0, may hold values from -6 to 6
- source_spectrum: float32 [32, 2], P('freq'), may hold values from -4 to 4
- filter_taps: float32 [32, 4, 6], P('freq'), may hold values from -1.5 to 1.5, as said below
- slowness: float32 [16, 32, 1024], P('freq'), may hold values from 0.5 to 2
- depth_owner: int32 [6], P('shot'), parts along dimension 0, may hold values from 0 to 15
- source_position: int32 [4], P('shot'), parts along dimension 0, may hold values from 0 to 31
Outputs:
- migrated_image: float32 [32, 32, 1024], P(('shot', 'freq')), parts along dimension 0
There are 2 independent parts, one for each index of `shot`. A program takes and returns all parts, laid end to end along the dimension named above; an argument that names none is the same for every part. Nothing has to cross between parts.
Inputs may be any that keep to these rules, and one draw needn't show every extreme that they name: `filter_taps`: each frequency and direction holds three complex taps.
All inputs are finite; a program needn't handle non-finite values.
Results may differ from a plain program's by a relative error of at most 0.0001.
Values sent between devices are 32-bit elements; how exact they have to be, the bound alone decides.
No kernel may reach another device: no remote copies, remote signals or barrier semaphores. Data moves between devices by JAX's collectives and lax.ppermute only.
A program may use at most 64 MiB of HBM per device.

v0:
```python
import math

import jax
import jax.numpy as jnp
from jax import lax
from jax.sharding import PartitionSpec as P

lens_rate = 3.0
wave_rate = 0.5
directions = ((1, 0), (0, 1), (1, 1), (1, -1))


def broadcast(value, axis, source):
    kept = jnp.where(lax.axis_index(axis) == source, value, 0).astype(value.dtype)
    return lax.psum(kept, axis)


def source_start(spectrum, position, freq_index, freq_total, height, breadth):
    src_row = position[0].astype(jnp.float32)
    src_col = position[1].astype(jnp.float32)
    row_axis = jnp.arange(height, dtype=jnp.float32)[:, None]
    col_axis = jnp.arange(breadth, dtype=jnp.float32)[None, :]
    distance = jnp.sqrt((row_axis - src_row) ** 2 + (col_axis - src_col) ** 2 + 1.0)
    amplitude = 1.0 / (1.0 + distance / (height / 4.0))
    wavenumber = (freq_index.astype(jnp.float32) + 1.0) * (wave_rate / freq_total)
    phase_map = wavenumber[:, None, None] * distance[None]
    base_re = amplitude[None] * jnp.cos(phase_map)
    base_im = -amplitude[None] * jnp.sin(phase_map)
    wave_re = spectrum[:, 0][:, None, None]
    wave_im = spectrum[:, 1][:, None, None]
    return jnp.stack(
        [wave_re * base_re - wave_im * base_im, wave_re * base_im + wave_im * base_re], axis=1
    )


def complex_mul(values, coef_re, coef_im):
    coef_re = coef_re[:, None, None]
    coef_im = coef_im[:, None, None]
    return jnp.stack(
        [
            values[:, 0] * coef_re - values[:, 1] * coef_im,
            values[:, 0] * coef_im + values[:, 1] * coef_re,
        ],
        axis=1,
    )


def thin_lens(wavefield, layer_slab, freq_index, freq_total, handed):
    phases = (
        (freq_index.astype(jnp.float32) + 1.0)[:, None, None]
        * (lens_rate / freq_total)
        * layer_slab[None]
    )
    rot_re = jnp.cos(phases)
    rot_im = handed * jnp.sin(phases)
    part_re = wavefield[:, 0]
    part_im = wavefield[:, 1]
    return jnp.stack(
        [part_re * rot_re - part_im * rot_im, part_re * rot_im + part_im * rot_re], axis=1
    )


def directional(wavefield, coeffs, step_x, step_y, handed):
    height = wavefield.shape[2]
    breadth = wavefield.shape[3]
    padded = jnp.pad(wavefield, ((0, 0), (0, 0), (2, 2), (2, 2)))

    def adjacent(offset):
        return padded[
            :,
            :,
            2 + offset * step_x : 2 + offset * step_x + height,
            2 + offset * step_y : 2 + offset * step_y + breadth,
        ]

    inner_pair = adjacent(1) + adjacent(-1)
    outer_pair = adjacent(2) + adjacent(-2)
    result = complex_mul(wavefield, coeffs[:, 0], handed * coeffs[:, 1])
    result = result + complex_mul(inner_pair, coeffs[:, 2], handed * coeffs[:, 3])
    return result + complex_mul(outer_pair, coeffs[:, 4], handed * coeffs[:, 5])


def depth_step(source, receiver, layer_slab, filter_taps, freq_index, freq_total):
    source = thin_lens(source, layer_slab, freq_index, freq_total, -1.0)
    receiver = thin_lens(receiver, layer_slab, freq_index, freq_total, 1.0)
    for direction, (step_x, step_y) in enumerate(directions):
        source = directional(source, filter_taps[:, direction], step_x, step_y, 1.0)
        receiver = directional(receiver, filter_taps[:, direction], step_x, step_y, -1.0)
    return (source, receiver)


def local(receiver_data, source_spectrum, filter_taps, slowness, depth_owner, source_position):
    freq_local = receiver_data.shape[0]
    height = receiver_data.shape[2]
    breadth = receiver_data.shape[3]
    device_rank = lax.axis_index("freq")
    freq_total = lax.axis_size("freq") * freq_local
    freq_index = device_rank * freq_local + jnp.arange(freq_local, dtype=jnp.int32)
    source = source_start(source_spectrum, source_position, freq_index, freq_total, height, breadth)
    receiver = receiver_data
    migrated = jnp.zeros((1, height, breadth), jnp.float32)
    partials = []
    masks = []
    for level in range(depth_owner.shape[0]):
        owner_now = depth_owner[level]
        layer_slab = broadcast(slowness[0], "freq", owner_now)
        source, receiver = depth_step(
            source, receiver, layer_slab, filter_taps, freq_index, freq_total
        )
        local_term = jnp.sum(
            source[:, 0] * receiver[:, 0] + source[:, 1] * receiver[:, 1], axis=0
        ) / math.sqrt(freq_total)
        owner_mask = (owner_now == device_rank).astype(jnp.float32)
        partials.append(local_term)
        masks.append(owner_mask)
    summed_stack = lax.psum(jnp.stack(partials), "freq")
    for level in range(len(masks)):
        migrated = migrated + masks[level] * summed_stack[level][None]
    return migrated


def solution(mesh):
    return jax.shard_map(
        local,
        mesh=mesh,
        in_specs=(
            P(("shot", "freq"), None, None, None),
            P("freq", None),
            P("freq", None, None),
            P("freq", None, None),
            P("shot"),
            P("shot"),
        ),
        out_specs=P(("shot", "freq"), None, None),
        check_vma=False,
    )
```

profile of v0, /device:TPU:0, one launch (start us, length us, event | category | flops | bytes accessed | tf_op | source)
XLA Modules:
  0.0 238.9 jit_solution(6213239613544791227)
XLA Ops:
  6.5 0.7 copy-done.3
  7.2 0.6 fusion.131
  9.7 1.7 select_bitcast_fusion
  11.5 0.3 slice_reduce_fusion.19
  11.8 0.6 fusion.130
  13.9 0.3 slice_reduce_fusion.13
  14.2 0.3 slice_reduce_fusion.7
  14.5 0.3 slice_reduce_fusion.1
  14.9 90.5 %all-reduce.30.cloned.1.call-done = (f32[32,1024]{1,0:T(8,128)}, f32[32,1024]{1,0:T(8,128)}, f32[32,1024]{1,0:T(8,128)}) async-done(((f32[32,1024]{1,0:T(8,128)}, f32[32,1024]{1,0:T(8,128)}, f32[32,1024]{1,0:T(8,128)}), (f32[32,1024]{1,0:T(8,128)}, f32[32,1024]{1,0:T(8,128)}, f32[32,1024]{1,0:T(8,128)})) %all-reduce.30.cloned.1.call-update) | async-done | bytes 393232 | tf_op jit(solution)/shard_map/psum | solution.py:15
  105.4 3.0 %multiply_subtract_fusion.71 = (f32[2,1,32,1024]{3,2,1,0:T(8,128)S(1)}, f32[2,1,32,1024]{3,2,1,0:T(8,128)S(1)}, f32[2,1,32,1024]{3,2,1,0:T(8,128)S(1)}, f32[2,1,...) fusion(f32[2]{0:T(128)S(1)} %get-tuple-element.29, ...), kind=kLoop, calls=%fused_computation.386 | loop fusion | flops 1900544 | bytes 2621496 | tf_op jit(solution)/shard_map/sub | solution.py:41
  108.4 0.3 select_maximum_fusion.4
  108.7 0.3 select_maximum_fusion.5
  109.1 0.6 slice_add_fusion.8
  109.7 0.6 slice_add_fusion.10
  110.4 0.2 multiply_subtract_fusion.69
  110.6 0.2 multiply_subtract_fusion.70
  110.9 0.6 fusion.10
  111.6 0.6 fusion.4
  112.3 0.2 multiply_subtract_fusion.68
  112.4 0.2 multiply_subtract_fusion.66
  112.6 0.2 multiply_subtract_fusion.67
  113.0 0.7 fusion.12
  113.8 0.7 fusion.6
  114.8 0.2 multiply_subtract_fusion.64
  115.1 0.7 fusion.14
  115.9 0.7 fusion.8
  116.6 0.2 multiply_subtract_fusion.62
  117.4 0.8 copy-done.2
  118.2 1.5 multiply_subtract_fusion.47
  119.7 0.3 select_maximum_fusion.2
  119.9 0.3 select_maximum_fusion.3
  120.4 0.6 slice_add_fusion.4
  121.0 0.6 slice_add_fusion.6
  121.6 0.2 multiply_subtract_fusion.45
  121.8 0.2 multiply_subtract_fusion.46
  122.2 0.6 fusion.22
  122.9 0.6 fusion.16
  123.9 0.2 multiply_subtract_fusion.43
  124.2 0.7 fusion.24
  125.0 0.7 fusion.18
  126.0 0.2 multiply_subtract_fusion.40
  126.4 0.7 fusion.26
  127.1 0.7 fusion.20
  128.2 0.2 multiply_subtract_fusion.37
  128.6 0.8 copy-done.1
  129.4 1.5 multiply_subtract_fusion.23
  131.0 0.3 select_maximum_fusion
  131.2 0.6 slice_add_fusion
  131.9 0.3 select_maximum_fusion.1
  132.1 0.6 slice_add_fusion.2
  132.7 0.2 multiply_subtract_fusion.22
  133.0 0.3 multiply_subtract_fusion.21
  133.4 0.6 fusion.34
  134.1 0.6 fusion.28
  135.1 0.2 multiply_subtract_fusion.19
  135.5 0.7 fusion.36
  136.2 0.7 fusion.30
  137.3 0.2 multiply_subtract_fusion.16
  137.6 0.7 fusion.38
  138.4 0.7 fusion.32
  139.4 0.2 multiply_subtract_fusion.13
  140.0 0.8 pad_maximum_fusion
  142.6 87.7 %all-reduce.28.cloned.1.call-done = f32[3,32,1024]{2,1,0:T(8,128)} async-done(((f32[3,32,1024]{2,1,0:T(8,128)}), f32[3,32,1024]{2,1,0:T(8,128)}) %all-reduce.28.cloned.1.call-update) | async-done | bytes 393232 | tf_op jit(solution)/shard_map/psum | solution.py:116
  230.3 1.7 fusion.112
  (79 shorter events, 6.2 us)
Async XLA Ops:
  6.5 98.9 %all-reduce.30.cloned.1.call-start = ((), (), s32[]{:S(2)}) async-start(), calls=%async_computation.1 | async-start | bytes 786432 | tf_op jit(solution)/shard_map/psum | solution.py:15
  6.5 0.7 copy-start.3
  9.7 1.8 copy-start.5
  9.7 2.1 copy-start.6
  9.7 4.0 %copy-start.4 = (f32[2,2]{1,0:T(2,128)S(1)}, f32[2,2]{1,0:T(2,128)}, u32[]{:S(2)}) copy-start(f32[2,2]{1,0:T(2,128)} %param.7) | copy-start | bytes 52
  11.4 94.1 %copy-start = (f32[2,2,32,1024]{3,2,1,0:T(8,128)S(1)}, f32[2,2,32,1024]{3,2,1,0:T(8,128)}, u32[]{:S(2)}) copy-start(f32[2,2,32,1024]{3,2,1,0:T(8,128)} %param.6) | copy-start | bytes 1572868
  11.4 219.0 %all-reduce.28.cloned.1.call-start = ((), (), s32[]{:S(2)}) async-start(), calls=%async_computation | async-start | bytes 786432 | tf_op jit(solution)/shard_map/psum | solution.py:116
  117.3 0.9 copy-start.2
  128.5 0.9 copy-start.1
Sparse Core Ops, SparseCore 0:
  11.5 93.8 all-reduce.29
  140.9 89.3 all-reduce.27
where the time goes:
time: 239 us
  waiting for transfers between devices  178 us (74%)
  other arithmetic  36.8 us (15%)
  between operations  19.1 us (8%)
  local copies, waits for them, and re-layouts  4.73 us (2%)
    psum x1, waiting for transfers between devices, broadcast(): return lax.psum(kept, axis)  90.5 us
    psum x1, waiting for transfers between devices, local(): summed_stack = lax.psum(jnp.stack(partials), 'freq')  87.7 us
    add x24, other arithmetic, directional(): outer_pair = adjacent(2) + adjacent(-2)  15.3 us
    sub x36, other arithmetic, complex_mul(): values[:, 0] * coef_re - values[:, 1] * coef_im  12.8 us
  transfers between devices with their start and end apart: 2, of which 2 were waited for; matrix products, arithmetic and copies ran while one was open for 1% of the time, Pallas kernels for 0%

commit v1 on v0

v1 whole, which is shorter than its diff:
```python
import functools
import math

import jax
import jax.numpy as jnp
from jax import lax
from jax.experimental import pallas as pl
from jax.experimental.pallas import tpu as pltpu
from jax.sharding import PartitionSpec as P

lens_rate = 3.0
wave_rate = 0.5
directions = ((1, 0), (0, 1), (1, 1), (1, -1))
LANES = 128
SUB = 8
REACH = 2
TWO_OVER_PI = 2.0 / math.pi
PI_2 = (1.5703125, 4.837512969970703125e-4, 7.54978995489188216e-8)


def cos_sin(x):
    turns = jnp.floor(x * TWO_OVER_PI + 0.5)
    r = x - turns * PI_2[0]
    r = r - turns * PI_2[1]
    r = r - turns * PI_2[2]
    r2 = r * r
    s = r + r * r2 * (-1.6666654611e-1 + r2 * (8.3321608736e-3 + r2 * -1.9515295891e-4))
    c = (1.0 - 0.5 * r2) + r2 * r2 * (
        4.166664568298827e-2 + r2 * (-1.388731625493765e-3 + r2 * 2.443315711809948e-5)
    )
    quadrant = turns.astype(jnp.int32)
    odd = (quadrant & 1) == 1
    cos_value = jnp.where(odd, s, c)
    sin_value = jnp.where(odd, c, s)
    cos_value = jnp.where(((quadrant + 1) & 2) == 2, -cos_value, cos_value)
    sin_value = jnp.where((quadrant & 2) == 2, -sin_value, sin_value)
    return cos_value, sin_value


def swap_segments(blocks):
    count = len(blocks)
    width = LANES // count
    lane = lax.broadcasted_iota(jnp.int32, (SUB, LANES), 1)
    step = 1
    while step < count:
        upper = ((lane // (width * step)) & 1) == 1
        swapped = list(blocks)
        for b in range(count):
            if b & step == 0:
                low, high = blocks[b], blocks[b + step]
                swapped[b] = jnp.where(upper, pltpu.roll(high, step * width, 1), low)
                swapped[b + step] = jnp.where(
                    upper, high, pltpu.roll(low, LANES - step * width, 1)
                )
        blocks = swapped
        step *= 2
    return blocks


def interleave(blocks):
    count = len(blocks)
    width = LANES // count
    lane = lax.broadcasted_iota(jnp.int32, (SUB, LANES), 1)
    pick = (lane % width) * count + lane // width
    return swap_segments([jnp.take_along_axis(b, pick, axis=1) for b in blocks])


def deinterleave(blocks):
    count = len(blocks)
    width = LANES // count
    lane = lax.broadcasted_iota(jnp.int32, (SUB, LANES), 1)
    pick = (lane % count) * width + lane // count
    return [jnp.take_along_axis(b, pick, axis=1) for b in swap_segments(blocks)]


def migrate_kernel(
    freq_total, base_ref, position_ref, spectrum_ref, taps_ref, receiver_ref, slab_ref, out_ref, a_ref, b_ref, v_ref, c_ref
):
    freq_local, _, height, breadth = receiver_ref.shape
    levels = slab_ref.shape[0]
    blocks = breadth // LANES
    groups = height // SUB
    lane = lax.broadcasted_iota(jnp.int32, (SUB, LANES), 1)
    row = lax.broadcasted_iota(jnp.int32, (SUB, LANES), 0)
    not_first = lane > 0
    not_last = lane < LANES - 1

    def load(ref, f, field, part, block, group, shift=0):
        return ref[f, field, part, block + REACH, pl.ds(SUB * (group + 1) + shift, SUB), :]

    def store(ref, f, field, part, block, group, value):
        ref[f, field, part, block + REACH, pl.ds(SUB * (group + 1), SUB), :] = value

    zero = jnp.zeros((SUB, LANES), jnp.float32)

    @pl.loop(0, freq_local)
    def _(f):
        for ref in (a_ref, b_ref):
            for field in range(2):
                for part in range(2):
                    for block in range(blocks + 2 * REACH):
                        ref[f, field, part, block, 0:SUB, :] = zero
                        ref[f, field, part, block, SUB * (groups + 1) : SUB * (groups + 2), :] = zero

    @pl.loop(0, freq_local)
    def _(f):
        for part in range(2):
            for g in range(groups):
                loaded = [
                    receiver_ref[f, part, SUB * g : SUB * (g + 1), LANES * b : LANES * (b + 1)]
                    for b in range(blocks)
                ]
                for b, value in enumerate(interleave(loaded)):
                    store(a_ref, f, 1, part, b, g, -value if part else value)

    src_row = position_ref[0].astype(jnp.float32)
    src_col = position_ref[1].astype(jnp.float32)

    def number(f):
        return (base_ref[0] + f).astype(jnp.float32) + 1.0

    for g in range(groups):
        for b in range(blocks):
            d_row = (row + SUB * g).astype(jnp.float32) - src_row
            d_col = (lane * blocks + b).astype(jnp.float32) - src_col
            distance = jnp.sqrt(d_row * d_row + d_col * d_col + 1.0)
            amplitude = 1.0 / (1.0 + distance / (height / 4.0))
            for f in range(freq_local):
                cos_value, sin_value = cos_sin(number(f) * (wave_rate / freq_total) * distance)
                base_re = amplitude * cos_value
                base_im = -amplitude * sin_value
                w_re, w_im = spectrum_ref[f, 0], spectrum_ref[f, 1]
                store(a_ref, f, 0, 0, b, g, w_re * base_re - w_im * base_im)
                store(a_ref, f, 0, 1, b, g, w_re * base_im + w_im * base_re)

    @pl.loop(0, levels)
    def _(t):
        for g in range(groups):
            loaded = [
                slab_ref[t, SUB * g : SUB * (g + 1), LANES * b : LANES * (b + 1)] for b in range(blocks)
            ]
            for b, value in enumerate(interleave(loaded)):
                v_ref[t, b, SUB * g : SUB * (g + 1), :] = value

    def lens(t):
        @pl.loop(0, freq_local)
        def _(f):
            rate = number(f) * (lens_rate / freq_total)
            for g in range(groups):
                for b in range(blocks):
                    cos_value, sin_value = cos_sin(rate * v_ref[t, b, SUB * g : SUB * (g + 1), :])
                    for field in range(2):
                        re = load(a_ref, f, field, 0, b, g)
                        im = load(a_ref, f, field, 1, b, g)
                        store(a_ref, f, field, 0, b, g, re * cos_value + im * sin_value)
                        store(a_ref, f, field, 1, b, g, im * cos_value - re * sin_value)

    def filtered(src, f, field, b, g, d, taps):
        step_x, step_y = directions[d]

        def at(part, k):
            return load(src, f, field, part, b + k * step_y, g, k * step_x)

        c0r, c0i, c1r, c1i, c2r, c2i = taps
        re, im = at(0, 0), at(1, 0)
        p1r, p1i = at(0, 1) + at(0, -1), at(1, 1) + at(1, -1)
        p2r, p2i = at(0, 2) + at(0, -2), at(1, 2) + at(1, -2)
        out_re = (re * c0r - im * c0i) + (p1r * c1r - p1i * c1i) + (p2r * c2r - p2i * c2i)
        out_im = (re * c0i + im * c0r) + (p1r * c1i + p1i * c1r) + (p2r * c2i + p2i * c2r)
        return out_re, out_im

    def sweep(src, dst, d):
        @pl.loop(0, freq_local)
        def _(f):
            taps = [taps_ref[f, d, i] for i in range(6)]

            @pl.loop(0, 2)
            def _(field):
                for g in range(groups):
                    for b in range(blocks):
                        for part, value in enumerate(filtered(src, f, field, b, g, d, taps)):
                            store(dst, f, field, part, b, g, value)
                            if b < REACH:
                                store(dst, f, field, part, b + blocks, g, jnp.where(not_last, pltpu.roll(value, LANES - 1, 1), 0.0))
                            if b >= blocks - REACH:
                                store(dst, f, field, part, b - blocks, g, jnp.where(not_first, pltpu.roll(value, 1, 1), 0.0))

    def last_sweep(src, dst, d, t):
        @pl.loop(0, freq_local)
        def _(f):
            taps = [taps_ref[f, d, i] for i in range(6)]
            for g in range(groups):
                for b in range(blocks):
                    s_re, s_im = filtered(src, f, 0, b, g, d, taps)
                    r_re, r_im = filtered(src, f, 1, b, g, d, taps)
                    store(dst, f, 0, 0, b, g, s_re)
                    store(dst, f, 0, 1, b, g, s_im)
                    store(dst, f, 1, 0, b, g, r_re)
                    store(dst, f, 1, 1, b, g, r_im)
                    term = s_re * r_re - s_im * r_im
                    at = (b, slice(SUB * g, SUB * (g + 1)))
                    c_ref[at] = jnp.where(f == 0, term, c_ref[at] + term)

    @pl.loop(0, levels)
    def _(t):
        lens(t)
        sweep(a_ref, b_ref, 0)
        sweep(b_ref, a_ref, 1)
        sweep(a_ref, b_ref, 2)
        last_sweep(b_ref, a_ref, 3, t)
        for g in range(groups):
            summed = [c_ref[b, SUB * g : SUB * (g + 1)] for b in range(blocks)]
            for b, value in enumerate(deinterleave(summed)):
                out_ref[t, SUB * g : SUB * (g + 1), LANES * b : LANES * (b + 1)] = value * (
                    1.0 / math.sqrt(freq_total)
                )


def migrate(receiver, slabs, spectrum, taps, position, base, freq_total):
    freq_local, _, height, breadth = receiver.shape
    levels = slabs.shape[0]
    blocks = breadth // LANES
    state = pltpu.VMEM((freq_local, 2, 2, blocks + 2 * REACH, height + 2 * SUB, LANES), jnp.float32)
    smem = pl.BlockSpec(memory_space=pltpu.SMEM)
    vmem = pl.BlockSpec(memory_space=pltpu.VMEM)
    return pl.pallas_call(
        functools.partial(migrate_kernel, freq_total),
        out_shape=jax.ShapeDtypeStruct((levels, height, breadth), jnp.float32),
        in_specs=[smem, smem, smem, smem, vmem, vmem],
        out_specs=vmem,
        scratch_shapes=[
            state,
            state,
            pltpu.VMEM((levels, blocks, height, LANES), jnp.float32),
            pltpu.VMEM((blocks, height, LANES), jnp.float32),
        ],
        compiler_params=pltpu.CompilerParams(vmem_limit_bytes=32 * 1024 * 1024),
    )(base, position, spectrum, taps, receiver, slabs)


def across(bit, size):
    return [(i, i ^ bit) for i in range(size)]


def exchange(value, bit, size):
    return lax.ppermute(value, "freq", across(bit, size))


def fetch_slabs(own, owners, rank, size):
    half = own.shape[0] // 2
    parity = rank & 1
    halves = own.reshape(2, half, own.shape[1])
    mine, other = halves[parity], halves[1 - parity]
    got = exchange(other, 1, size)
    mismatch = owners ^ rank
    carried = jnp.where(((mismatch & 1) == 0)[:, None, None], mine[None], got[None])
    bit = 2
    while bit < size:
        got = exchange(carried, bit, size)
        carried = jnp.where(((mismatch & bit) == 0)[:, None, None], carried, got)
        bit *= 2
    got = exchange(carried, 1, size)
    return jnp.where(
        parity == 0, jnp.concatenate([carried, got], axis=1), jnp.concatenate([got, carried], axis=1)
    )


def sum_over(partial, rank, size):
    levels, height, breadth = partial.shape
    parity = rank & 1
    halves = partial.reshape(levels, 2, height // 2, breadth)
    carried = halves[:, parity] + exchange(halves[:, 1 - parity], 1, size)
    bit = 2
    while bit < size:
        carried = carried + exchange(carried, bit, size)
        bit *= 2
    got = exchange(carried, 1, size)
    return jnp.where(
        parity == 0, jnp.concatenate([carried, got], axis=1), jnp.concatenate([got, carried], axis=1)
    )


def local(receiver_data, source_spectrum, filter_taps, slowness, depth_owner, source_position):
    freq_local = receiver_data.shape[0]
    size = lax.axis_size("freq")
    rank = lax.axis_index("freq")
    freq_total = size * freq_local
    slabs = fetch_slabs(slowness[0], depth_owner, rank, size)
    base = (rank * freq_local).astype(jnp.int32).reshape(1)
    partial = migrate(
        receiver_data, slabs, source_spectrum, filter_taps, source_position, base, freq_total
    )
    summed = sum_over(partial, rank, size)
    owned = (depth_owner == rank).astype(jnp.float32)
    return jnp.sum(summed * owned[:, None, None], axis=0)[None]


def solution(mesh):
    return jax.shard_map(
        local,
        mesh=mesh,
        in_specs=(
            P(("shot", "freq"), None, None, None),
            P("freq", None),
            P("freq", None, None),
            P("freq", None, None),
            P("shot"),
            P("shot"),
        ),
        out_specs=P(("shot", "freq"), None, None),
        check_vma=False,
    )
```

time: 239 us -> 69.9 us (0.29)
  waiting for transfers between devices: 178 us -> 43.1 us
  other arithmetic: 36.8 us -> 1.25 us
  between operations: 19.1 us -> 0.13 us
  Pallas kernels: 0 us -> 11.9 us
  starting transfers between devices: 0.04 us -> 11.6 us
  local copies, waits for them, and re-layouts: 4.73 us -> 1.7 us
    psum x2 -> x0, waiting for transfers between devices: 178 us -> none  [the longest x1 90.5 us: broadcast(): return lax.psum(kept, axis)]
    ppermute x0 -> x10, waiting for transfers between devices: none -> 43.1 us  [exchange(): return lax.ppermute(value, 'freq', across(bit, size))]
    add x51 -> x4, other arithmetic: 19.7 us -> 0.1 us  [the longest x3 0.07 us: sum_over(): carried = carried + exchange(carried, bit, size)]
    sub x36 -> x0, other arithmetic: 12.8 us -> none  [complex_mul(): values[:, 0] * coef_re - values[:, 1] * coef_im]
    pallas_call x0 -> x1, Pallas kernels: none -> 11.9 us  [migrate(): pl.pallas_call(functools.partial(migrate_kernel, freq_total), out_shape=j...]
    ppermute x0 -> x10, starting transfers between devices: none -> 11.6 us  [exchange(): return lax.ppermute(value, 'freq', across(bit, size))]
    slice x8 -> x0, local copies, waits for them, and re-layouts: 2.48 us -> none  [the longest x4 1.02 us: directional(): return result + complex_mul(outer_pair, coeffs[:, 4], handed * coeffs[:, 5])]
  transfers between devices with their start and end apart: 2 -> 10, of which waited for: 2 -> 10; matrix products, arithmetic and copies ran while one was open for 1% -> 0% of each run, Pallas kernels for 0% -> 0%
where the time goes in v1:
time: 69.9 us; the launch traced here: 69.7 us
  waiting for transfers between devices  43.1 us (62%)
  Pallas kernels  11.9 us (17%)
  starting transfers between devices  11.6 us (17%)
  local copies, waits for them, and re-layouts  1.7 us (2%)
  other arithmetic  1.25 us (2%)
    ppermute x10, waiting for transfers between devices, exchange(): return lax.ppermute(value, 'freq', across(bit, size))  43.1 us
    pallas_call x1, Pallas kernels, migrate(): pl.pallas_call(functools.partial(migrate_kernel, freq_total), out_shape=j...  11.9 us
    ppermute x10, starting transfers between devices, exchange(): return lax.ppermute(value, 'freq', across(bit, size))  11.6 us
  transfers between devices with their start and end apart: 10, of which 10 were waited for; matrix products, arithmetic and copies ran while one was open for 0% of the time, Pallas kernels for 0%

profile of v1, /device:TPU:0, one launch (start us, length us, event | category | flops | bytes accessed | tf_op | source)
XLA Modules:
  0.0 69.7 jit_solution(15867705381040621163)
XLA Ops:
  0.0 0.9 %dynamic-slice_bitcast_fusion.2 = (f32[16,1024]{1,0:T(8,128)S(1)}, f32[16,1024]{1,0:T(8,128)S(1)}) fusion(f32[2,16,1024]{2,1,0:T(8,128)} %bitcast.18, s32[]{:T(128)S(6)} %select_n.35, s32[]{:T(128)S(6)} %select_n.36), kind=kLoop, calls=%fused_computation.11 | loop fusion | bytes 262152 | tf_op jit(solution)/shard_map/jit(_where)/broadcast_in_dim | solution.py:256
  0.9 0.0 copy-start.4
  0.9 0.5 collective-permute-start
  1.4 0.1 copy-done.4
  1.6 0.8 %collective-permute-done = f32[16,1024]{1,0:T(8,128)S(1)} collective-permute-done((f32[16,1024]{1,0:T(8,128)S(1)}, f32[16,1024]{1,0:T(8,128)S(1)}, u32[]{:S(2)}, u32[]{:S(2)}) %collective-permute-start) | collective-permute-done | bytes 65568 | tf_op jit(solution)/shard_map/ppermute | solution.py:246
  2.3 0.1 broadcast_select_fusion
  2.4 2.9 %collective-permute-start.1 = (f32[3,16,1024]{2,1,0:T(8,128)S(1)}, f32[3,16,1024]{2,1,0:T(8,128)S(1)}, u32[]{:S(2)}, u32[]{:S(2)}) collective-permute-start(f32[3,16,1024]{2,1,0:T(8,128)S(1)} %broadcast_select_fusion), channel_id=1, source_target_pairs={{0,2},{1,3},{2,0},{3,1},{4,6},{5,7},{6,4},{7,5},{8,10},{9,11},{10,... | collective-permute-start | bytes 589832 | tf_op jit(solution)/shard_map/ppermute | solution.py:246
  5.3 5.2 %collective-permute-done.1 = f32[3,16,1024]{2,1,0:T(8,128)S(1)} collective-permute-done((f32[3,16,1024]{2,1,0:T(8,128)S(1)}, f32[3,16,1024]{2,1,0:T(8,128)S(1)}, u32[]{:S(2)}, u32[]{:S(2)}) %collective-permute-start.1) | collective-permute-done | bytes 196640 | tf_op jit(solution)/shard_map/ppermute | solution.py:246
  10.6 0.1 broadcast_select_fusion.1
  10.7 1.9 %collective-permute-start.2 = (f32[3,16,1024]{2,1,0:T(8,128)S(1)}, f32[3,16,1024]{2,1,0:T(8,128)S(1)}, u32[]{:S(2)}, u32[]{:S(2)}) collective-permute-start(f32[3,16,1024]{2,1,0:T(8,128)S(1)} %broadcast_select_fusion.1), channel_id=1, source_target_pairs={{0,4},{1,5},{2,6},{3,7},{4,0},{5,1},{6,2},{7,3},{8,12},{9,13},{10,... | collective-permute-start | bytes 589832 | tf_op jit(solution)/shard_map/ppermute | solution.py:246
  12.5 4.7 %collective-permute-done.2 = f32[3,16,1024]{2,1,0:T(8,128)S(1)} collective-permute-done((f32[3,16,1024]{2,1,0:T(8,128)S(1)}, f32[3,16,1024]{2,1,0:T(8,128)S(1)}, u32[]{:S(2)}, u32[]{:S(2)}) %collective-permute-start.2) | collective-permute-done | bytes 196640 | tf_op jit(solution)/shard_map/ppermute | solution.py:246
  17.2 0.1 broadcast_select_fusion.2
  17.3 2.6 %collective-permute-start.3 = (f32[3,16,1024]{2,1,0:T(8,128)S(1)}, f32[3,16,1024]{2,1,0:T(8,128)S(1)}, u32[]{:S(2)}, u32[]{:S(2)}) collective-permute-start(f32[3,16,1024]{2,1,0:T(8,128)S(1)} %broadcast_select_fusion.2), channel_id=1, source_target_pairs={{0,8},{1,9},{2,10},{3,11},{4,12},{5,13},{6,14},{7,15},{8,0},{9,1},... | collective-permute-start | bytes 589832 | tf_op jit(solution)/shard_map/ppermute | solution.py:246
  19.8 8.2 %collective-permute-done.3 = f32[3,16,1024]{2,1,0:T(8,128)S(1)} collective-permute-done((f32[3,16,1024]{2,1,0:T(8,128)S(1)}, f32[3,16,1024]{2,1,0:T(8,128)S(1)}, u32[]{:S(2)}, u32[]{:S(2)}) %collective-permute-start.3) | collective-permute-done | bytes 196640 | tf_op jit(solution)/shard_map/ppermute | solution.py:246
  28.0 0.1 broadcast_select_fusion.3
  28.1 0.0 copy-start
  28.1 0.1 collective-permute-start.4
  28.2 1.4 %collective-permute-done.4 = f32[3,16,1024]{2,1,0:T(8,128)S(1)} collective-permute-done((f32[3,16,1024]{2,1,0:T(8,128)S(1)}, f32[3,16,1024]{2,1,0:T(8,128)S(1)}, u32[]{:S(2)}, u32[]{:S(2)}) %collective-permute-start.4) | collective-permute-done | bytes 196640 | tf_op jit(solution)/shard_map/ppermute | solution.py:246
  29.6 0.0 copy-start.1
  29.7 0.0 copy-start.2
  29.7 0.0 copy-start.3
  29.7 0.0 copy-done
  29.7 0.6 copy-done.1
  30.3 0.0 copy-done.2
  30.3 0.0 copy-done.3
  30.3 11.9 %shard_map.64 = f32[3,32,1024]{2,1,0:T(8,128)S(1)} custom-call(s32[1]{0:T(128)} %bitcast.base_ref, s32[2]{0:T(128)S(1)} %copy-done.3, f32[2,2]{1,0:T(2,128)S(1)} %copy-done.2, f32[2,4,6]{2,1,0:T(4,128)S(1)} %copy-done.1, f32[2,2,32,1024]{3,2,1,0:T(8,128)S(1)} %copy-done, f32[3,32,1024]{2,1,0:T(8,128)S(1)} %maximum_select_fusion.slab_ref), custom_call_target="tpu_custom_call" | custom-call | tf_op jit(solution)/shard_map/pallas_call | solution.py:226
  42.3 0.2 collective-permute-start.5
  42.5 1.3 %collective-permute-done.5 = f32[3,16,1024]{2,1,0:T(8,128)S(1)} collective-permute-done((f32[3,16,1024]{2,1,0:T(8,128)S(1)}, f32[3,16,1024]{2,1,0:T(8,128)S(1)}, u32[]{:S(2)}, u32[]{:S(2)}) %collective-permute-start.5) | collective-permute-done | bytes 196640 | tf_op jit(solution)/shard_map/ppermute | solution.py:246
  43.8 1.1 %collective-permute-start.6 = (f32[3,16,1024]{2,1,0:T(8,128)S(1)}, f32[3,16,1024]{2,1,0:T(8,128)S(1)}, u32[]{:S(2)}, u32[]{:S(2)}) collective-permute-start(f32[3,16,1024]{2,1,0:T(8,128)S(1)} %bitcast_add_fusion), channel_id=1, source_target_pairs={{0,2},{1,3},{2,0},{3,1},{4,6},{5,7},{6,4},{7,5},{8,10},{9,11},{10,... | collective-permute-start | bytes 589832 | tf_op jit(solution)/shard_map/ppermute | solution.py:246
  44.9 5.9 %collective-permute-done.6 = f32[3,16,1024]{2,1,0:T(8,128)S(1)} collective-permute-done((f32[3,16,1024]{2,1,0:T(8,128)S(1)}, f32[3,16,1024]{2,1,0:T(8,128)S(1)}, u32[]{:S(2)}, u32[]{:S(2)}) %collective-permute-start.6) | collective-permute-done | bytes 196640 | tf_op jit(solution)/shard_map/ppermute | solution.py:246
  50.8 0.3 collective-permute-start.7
  51.1 5.9 %collective-permute-done.7 = f32[3,16,1024]{2,1,0:T(8,128)S(1)} collective-permute-done((f32[3,16,1024]{2,1,0:T(8,128)S(1)}, f32[3,16,1024]{2,1,0:T(8,128)S(1)}, u32[]{:S(2)}, u32[]{:S(2)}) %collective-permute-start.7) | collective-permute-done | bytes 196640 | tf_op jit(solution)/shard_map/ppermute | solution.py:246
  57.0 1.9 %collective-permute-start.8 = (f32[3,16,1024]{2,1,0:T(8,128)S(1)}, f32[3,16,1024]{2,1,0:T(8,128)S(1)}, u32[]{:S(2)}, u32[]{:S(2)}) collective-permute-start(f32[3,16,1024]{2,1,0:T(8,128)S(1)} %add.25), channel_id=1, source_target_pairs={{0,8},{1,9},{2,10},{3,11},{4,12},{5,13},{6,14},{7,15},{8,0},{9,1},... | collective-permute-start | bytes 589832 | tf_op jit(solution)/shard_map/ppermute | solution.py:246
  59.0 8.4 %collective-permute-done.8 = f32[3,16,1024]{2,1,0:T(8,128)S(1)} collective-permute-done((f32[3,16,1024]{2,1,0:T(8,128)S(1)}, f32[3,16,1024]{2,1,0:T(8,128)S(1)}, u32[]{:S(2)}, u32[]{:S(2)}) %collective-permute-start.8) | collective-permute-done | bytes 196640 | tf_op jit(solution)/shard_map/ppermute | solution.py:246
  67.4 0.1 collective-permute-start.9
  67.5 1.4 %collective-permute-done.9 = f32[3,16,1024]{2,1,0:T(8,128)S(1)} collective-permute-done((f32[3,16,1024]{2,1,0:T(8,128)S(1)}, f32[3,16,1024]{2,1,0:T(8,128)S(1)}, u32[]{:S(2)}, u32[]{:S(2)}) %collective-permute-start.9) | collective-permute-done | bytes 196640 | tf_op jit(solution)/shard_map/ppermute | solution.py:246
  68.9 0.7 %fusion.1 = f32[32,1024]{1,0:T(8,128)} fusion(f32[3,16,1024]{2,1,0:T(8,128)S(1)} %collective-permute-done.9, f32[3,16,1024]{2,1,0:T(8,128)S(1)} %add.26, f32[3]{0:T(128)S(1)} %get-tuple-element.9, pred[]{:T(512)S(6)} %eq.20), kind=kLoop, calls=%fused_computation.3 | loop fusion | flops 458752 | bytes 524301 | tf_op jit(solution)/shard_map/reduce_sum | solution.py:295
  (8 shorter events, 0.2 us)
Async XLA Ops:
  0.9 0.7 copy-start.4
  0.9 1.4 %collective-permute-start = (f32[16,1024]{1,0:T(8,128)S(1)}, f32[16,1024]{1,0:T(8,128)S(1)}, u32[]{:S(2)}, u32[]{:S(2)}) collective-permute-start(f32[16,1024]{1,0:T(8,128)S(1)} %get-tuple-element.8), channel_id=1, source_target_pairs={{0,1},{1,0},{2,3},{3,2},{4,5},{5,4},{6,7},{7,6},{8,9},{9,8},{10,11... | collective-permute-start | bytes 196616 | tf_op jit(solution)/shard_map/ppermute | solution.py:246
  2.4 8.2 %collective-permute-start.1 = (f32[3,16,1024]{2,1,0:T(8,128)S(1)}, f32[3,16,1024]{2,1,0:T(8,128)S(1)}, u32[]{:S(2)}, u32[]{:S(2)}) collective-permute-start(f32[3,16,1024]{2,1,0:T(8,128)S(1)} %broadcast_select_fusion), channel_id=1, source_target_pairs={{0,2},{1,3},{2,0},{3,1},{4,6},{5,7},{6,4},{7,5},{8,10},{9,11},{10,... | collective-permute-start | bytes 589832 | tf_op jit(solution)/shard_map/ppermute | solution.py:246
  10.7 6.5 %collective-permute-start.2 = (f32[3,16,1024]{2,1,0:T(8,128)S(1)}, f32[3,16,1024]{2,1,0:T(8,128)S(1)}, u32[]{:S(2)}, u32[]{:S(2)}) collective-permute-start(f32[3,16,1024]{2,1,0:T(8,128)S(1)} %broadcast_select_fusion.1), channel_id=1, source_target_pairs={{0,4},{1,5},{2,6},{3,7},{4,0},{5,1},{6,2},{7,3},{8,12},{9,13},{10,... | collective-permute-start | bytes 589832 | tf_op jit(solution)/shard_map/ppermute | solution.py:246
  17.3 10.7 %collective-permute-start.3 = (f32[3,16,1024]{2,1,0:T(8,128)S(1)}, f32[3,16,1024]{2,1,0:T(8,128)S(1)}, u32[]{:S(2)}, u32[]{:S(2)}) collective-permute-start(f32[3,16,1024]{2,1,0:T(8,128)S(1)} %broadcast_select_fusion.2), channel_id=1, source_target_pairs={{0,8},{1,9},{2,10},{3,11},{4,12},{5,13},{6,14},{7,15},{8,0},{9,1},... | collective-permute-start | bytes 589832 | tf_op jit(solution)/shard_map/ppermute | solution.py:246
  28.1 1.6 %copy-start = (f32[2,2,32,1024]{3,2,1,0:T(8,128)S(1)}, f32[2,2,32,1024]{3,2,1,0:T(8,128)}, u32[]{:S(2)}) copy-start(f32[2,2,32,1024]{3,2,1,0:T(8,128)} %receiver_ref.1) | copy-start | bytes 1572868
  28.1 1.5 %collective-permute-start.4 = (f32[3,16,1024]{2,1,0:T(8,128)S(1)}, f32[3,16,1024]{2,1,0:T(8,128)S(1)}, u32[]{:S(2)}, u32[]{:S(2)}) collective-permute-start(f32[3,16,1024]{2,1,0:T(8,128)S(1)} %broadcast_select_fusion.3), channel_id=1, source_target_pairs={{0,1},{1,0},{2,3},{3,2},{4,5},{5,4},{6,7},{7,6},{8,9},{9,8},{10,11... | collective-permute-start | bytes 589832 | tf_op jit(solution)/shard_map/ppermute | solution.py:246
  29.6 0.7 copy-start.1
  29.7 0.7 copy-start.2
  29.7 0.7 copy-start.3
  42.3 1.5 %collective-permute-start.5 = (f32[3,16,1024]{2,1,0:T(8,128)S(1)}, f32[3,16,1024]{2,1,0:T(8,128)S(1)}, u32[]{:S(2)}, u32[]{:S(2)}) collective-permute-start(f32[3,16,1024]{2,1,0:T(8,128)S(1)} %dynamic-slice_bitcast_fusion), channel_id=1, source_target_pairs={{0,1},{1,0},{2,3},{3,2},{4,5},{5,4},{6,7},{7,6},{8,9},{9,8},{10,11... | collective-permute-start | bytes 589832 | tf_op jit(solution)/shard_map/ppermute | solution.py:246
  43.8 7.0 %collective-permute-start.6 = (f32[3,16,1024]{2,1,0:T(8,128)S(1)}, f32[3,16,1024]{2,1,0:T(8,128)S(1)}, u32[]{:S(2)}, u32[]{:S(2)}) collective-permute-start(f32[3,16,1024]{2,1,0:T(8,128)S(1)} %bitcast_add_fusion), channel_id=1, source_target_pairs={{0,2},{1,3},{2,0},{3,1},{4,6},{5,7},{6,4},{7,5},{8,10},{9,11},{10,... | collective-permute-start | bytes 589832 | tf_op jit(solution)/shard_map/ppermute | solution.py:246
  50.8 6.2 %collective-permute-start.7 = (f32[3,16,1024]{2,1,0:T(8,128)S(1)}, f32[3,16,1024]{2,1,0:T(8,128)S(1)}, u32[]{:S(2)}, u32[]{:S(2)}) collective-permute-start(f32[3,16,1024]{2,1,0:T(8,128)S(1)} %add.24), channel_id=1, source_target_pairs={{0,4},{1,5},{2,6},{3,7},{4,0},{5,1},{6,2},{7,3},{8,12},{9,13},{10,... | collective-permute-start | bytes 589832 | tf_op jit(solution)/shard_map/ppermute | solution.py:246
  57.0 10.4 %collective-permute-start.8 = (f32[3,16,1024]{2,1,0:T(8,128)S(1)}, f32[3,16,1024]{2,1,0:T(8,128)S(1)}, u32[]{:S(2)}, u32[]{:S(2)}) collective-permute-start(f32[3,16,1024]{2,1,0:T(8,128)S(1)} %add.25), channel_id=1, source_target_pairs={{0,8},{1,9},{2,10},{3,11},{4,12},{5,13},{6,14},{7,15},{8,0},{9,1},... | collective-permute-start | bytes 589832 | tf_op jit(solution)/shard_map/ppermute | solution.py:246
  67.4 1.5 %collective-permute-start.9 = (f32[3,16,1024]{2,1,0:T(8,128)S(1)}, f32[3,16,1024]{2,1,0:T(8,128)S(1)}, u32[]{:S(2)}, u32[]{:S(2)}) collective-permute-start(f32[3,16,1024]{2,1,0:T(8,128)S(1)} %add.26), channel_id=1, source_target_pairs={{0,1},{1,0},{2,3},{3,2},{4,5},{5,4},{6,7},{7,6},{8,9},{9,8},{10,11... | collective-permute-start | bytes 589832 | tf_op jit(solution)/shard_map/ppermute | solution.py:246

commit v2 on v1

--- a/solution.py
+++ b/solution.py
@@ -73,34 +73,31 @@
     return [jnp.take_along_axis(b, pick, axis=1) for b in swap_segments(blocks)]
 
 
-def migrate_kernel(
-    freq_total, base_ref, position_ref, spectrum_ref, taps_ref, receiver_ref, slab_ref, out_ref, a_ref, b_ref, v_ref, c_ref
+def tile(ref, f, field, part, block, group, shift=0):
+    return ref.at[f, field, part, block, pl.ds(SUB * group + shift, SUB), :]
+
+
+def prepare_kernel(
+    freq_total,
+    base_ref,
+    position_ref,
+    mismatch_ref,
+    spectrum_ref,
+    taps_ref,
+    receiver_ref,
+    field_ref,
+    taps_out_ref,
+    rate_ref,
+    turn_ref,
 ):
     freq_local, _, height, breadth = receiver_ref.shape
-    levels = slab_ref.shape[0]
     blocks = breadth // LANES
     groups = height // SUB
     lane = lax.broadcasted_iota(jnp.int32, (SUB, LANES), 1)
     row = lax.broadcasted_iota(jnp.int32, (SUB, LANES), 0)
-    not_first = lane > 0
-    not_last = lane < LANES - 1
-
-    def load(ref, f, field, part, block, group, shift=0):
-        return ref[f, field, part, block + REACH, pl.ds(SUB * (group + 1) + shift, SUB), :]
-
-    def store(ref, f, field, part, block, group, value):
-        ref[f, field, part, block + REACH, pl.ds(SUB * (group + 1), SUB), :] = value
-
-    zero = jnp.zeros((SUB, LANES), jnp.float32)
-
-    @pl.loop(0, freq_local)
-    def _(f):
-        for ref in (a_ref, b_ref):
-            for field in range(2):
-                for part in range(2):
-                    for block in range(blocks + 2 * REACH):
-                        ref[f, field, part, block, 0:SUB, :] = zero
-                        ref[f, field, part, block, SUB * (groups + 1) : SUB * (groups + 2), :] = zero
+
+    def number(f):
+        return (base_ref[0] + f).astype(jnp.float32) + 1.0
 
     @pl.loop(0, freq_local)
     def _(f):
@@ -111,14 +108,17 @@
                     for b in range(blocks)
                 ]
                 for b, value in enumerate(interleave(loaded)):
-                    store(a_ref, f, 1, part, b, g, -value if part else value)
+                    tile(field_ref, f, 1, part, b, g)[...] = -value if part else value
+        for d in range(len(directions)):
+            for i in range(6):
+                taps_out_ref[f, d, i] = jnp.full((SUB, LANES), taps_ref[f, d, i], jnp.float32)
+        rate_ref[f] = jnp.full((SUB, LANES), number(f) * (lens_rate / freq_total), jnp.float32)
+
+    for t in range(mismatch_ref.shape[0]):
+        turn_ref[t] = jnp.full((SUB, LANES), mismatch_ref[t], jnp.int32)
 
     src_row = position_ref[0].astype(jnp.float32)
     src_col = position_ref[1].astype(jnp.float32)
-
-    def number(f):
-        return (base_ref[0] + f).astype(jnp.float32) + 1.0
-
     for g in range(groups):
         for b in range(blocks):
             d_row = (row + SUB * g).astype(jnp.float32) - src_row
@@ -130,8 +130,37 @@
                 base_re = amplitude * cos_value
                 base_im = -amplitude * sin_value
                 w_re, w_im = spectrum_ref[f, 0], spectrum_ref[f, 1]
-                store(a_ref, f, 0, 0, b, g, w_re * base_re - w_im * base_im)
-                store(a_ref, f, 0, 1, b, g, w_re * base_im + w_im * base_re)
+                tile(field_ref, f, 0, 0, b, g)[...] = w_re * base_re - w_im * base_im
+                tile(field_ref, f, 0, 1, b, g)[...] = w_re * base_im + w_im * base_re
+
+
+def migrate_kernel(
+    freq_total, field_ref, taps_ref, rate_ref, slab_ref, out_ref, a_ref, b_ref, v_ref, c_ref
+):
+    freq_local = field_ref.shape[0]
+    levels, height, breadth = slab_ref.shape
+    blocks = breadth // LANES
+    groups = height // SUB
+    lane = lax.broadcasted_iota(jnp.int32, (SUB, LANES), 1)
+    not_first = lane > 0
+    not_last = lane < LANES - 1
+
+    def load(ref, f, field, part, block, group, shift=0):
+        return tile(ref, f, field, part, block + REACH, group + 1, shift)[...]
+
+    def store(ref, f, field, part, block, group, value):
+        tile(ref, f, field, part, block + REACH, group + 1)[...] = value
+
+    zero = jnp.zeros((SUB, LANES), jnp.float32)
+
+    @pl.loop(0, freq_local)
+    def _(f):
+        for ref in (a_ref, b_ref):
+            for field in range(2):
+                for part in range(2):
+                    for block in range(blocks + 2 * REACH):
+                        tile(ref, f, field, part, block, 0)[...] = zero
+                        tile(ref, f, field, part, block, groups + 1)[...] = zero
 
     @pl.loop(0, levels)
     def _(t):
@@ -142,16 +171,15 @@
             for b, value in enumerate(interleave(loaded)):
                 v_ref[t, b, SUB * g : SUB * (g + 1), :] = value
 
-    def lens(t):
+    def lens(t, get):
         @pl.loop(0, freq_local)
         def _(f):
-            rate = number(f) * (lens_rate / freq_total)
+            rate = rate_ref[f]
             for g in range(groups):
                 for b in range(blocks):
                     cos_value, sin_value = cos_sin(rate * v_ref[t, b, SUB * g : SUB * (g + 1), :])
                     for field in range(2):
-                        re = load(a_ref, f, field, 0, b, g)
-                        im = load(a_ref, f, field, 1, b, g)
+                        re, im = get(f, field, 0, b, g), get(f, field, 1, b, g)
                         store(a_ref, f, field, 0, b, g, re * cos_value + im * sin_value)
                         store(a_ref, f, field, 1, b, g, im * cos_value - re * sin_value)
 
@@ -181,11 +209,13 @@
                         for part, value in enumerate(filtered(src, f, field, b, g, d, taps)):
                             store(dst, f, field, part, b, g, value)
                             if b < REACH:
-                                store(dst, f, field, part, b + blocks, g, jnp.where(not_last, pltpu.roll(value, LANES - 1, 1), 0.0))
+                                beside = jnp.where(not_last, pltpu.roll(value, LANES - 1, 1), 0.0)
+                                store(dst, f, field, part, b + blocks, g, beside)
                             if b >= blocks - REACH:
-                                store(dst, f, field, part, b - blocks, g, jnp.where(not_first, pltpu.roll(value, 1, 1), 0.0))
-
-    def last_sweep(src, dst, d, t):
+                                beside = jnp.where(not_first, pltpu.roll(value, 1, 1), 0.0)
+                                store(dst, f, field, part, b - blocks, g, beside)
+
+    def last_sweep(src, dst, d):
         @pl.loop(0, freq_local)
         def _(f):
             taps = [taps_ref[f, d, i] for i in range(6)]
@@ -201,13 +231,11 @@
                     at = (b, slice(SUB * g, SUB * (g + 1)))
                     c_ref[at] = jnp.where(f == 0, term, c_ref[at] + term)
 
-    @pl.loop(0, levels)
-    def _(t):
-        lens(t)
+    def depth_step(t):
         sweep(a_ref, b_ref, 0)
         sweep(b_ref, a_ref, 1)
         sweep(a_ref, b_ref, 2)
-        last_sweep(b_ref, a_ref, 3, t)
+        last_sweep(b_ref, a_ref, 3)
         for g in range(groups):
             summed = [c_ref[b, SUB * g : SUB * (g + 1)] for b in range(blocks)]
             for b, value in enumerate(deinterleave(summed)):
@@ -215,19 +243,49 @@
                     1.0 / math.sqrt(freq_total)
                 )
 
-
-def migrate(receiver, slabs, spectrum, taps, position, base, freq_total):
+    lens(0, lambda f, field, part, b, g: tile(field_ref, f, field, part, b, g)[...])
+
+    @pl.loop(0, levels)
+    def _(t):
+        @pl.when(t > 0)
+        def _():
+            lens(t, lambda f, field, part, b, g: load(a_ref, f, field, part, b, g))
+
+        depth_step(t)
+
+
+SMEM = pl.BlockSpec(memory_space=pltpu.SMEM)
+VMEM = pl.BlockSpec(memory_space=pltpu.VMEM)
+
+
+def prepare(receiver, spectrum, taps, position, mismatch, base, freq_total):
     freq_local, _, height, breadth = receiver.shape
+    blocks = breadth // LANES
+    cells = freq_local * height * breadth
+    return pl.pallas_call(
+        functools.partial(prepare_kernel, freq_total),
+        out_shape=(
+            jax.ShapeDtypeStruct((freq_local, 2, 2, blocks, height, LANES), jnp.float32),
+            jax.ShapeDtypeStruct((freq_local, len(directions), 6, SUB, LANES), jnp.float32),
+            jax.ShapeDtypeStruct((freq_local, SUB, LANES), jnp.float32),
+            jax.ShapeDtypeStruct((mismatch.shape[0], SUB, LANES), jnp.int32),
+        ),
+        in_specs=[SMEM, SMEM, SMEM, SMEM, SMEM, VMEM],
+        out_specs=(VMEM, VMEM, VMEM, VMEM),
+        cost_estimate=pl.CostEstimate(flops=100 * cells, bytes_accessed=24 * cells, transcendentals=0),
+        compiler_params=pltpu.CompilerParams(vmem_limit_bytes=32 * 1024 * 1024),
+    )(base, position, mismatch, spectrum, taps, receiver)
+
+
+def migrate(field, taps, rate, slabs, freq_total):
+    freq_local, _, _, blocks, height, _ = field.shape
     levels = slabs.shape[0]
-    blocks = breadth // LANES
     state = pltpu.VMEM((freq_local, 2, 2, blocks + 2 * REACH, height + 2 * SUB, LANES), jnp.float32)
-    smem = pl.BlockSpec(memory_space=pltpu.SMEM)
-    vmem = pl.BlockSpec(memory_space=pltpu.VMEM)
     return pl.pallas_call(
         functools.partial(migrate_kernel, freq_total),
-        out_shape=jax.ShapeDtypeStruct((levels, height, breadth), jnp.float32),
-        in_specs=[smem, smem, smem, smem, vmem, vmem],
-        out_specs=vmem,
+        out_shape=jax.ShapeDtypeStruct(slabs.shape, jnp.float32),
+        in_specs=[VMEM, VMEM, VMEM, VMEM],
+        out_specs=VMEM,
         scratch_shapes=[
             state,
             state,
@@ -235,49 +293,86 @@
             pltpu.VMEM((blocks, height, LANES), jnp.float32),
         ],
         compiler_params=pltpu.CompilerParams(vmem_limit_bytes=32 * 1024 * 1024),
-    )(base, position, spectrum, taps, receiver, slabs)
-
-
-def across(bit, size):
-    return [(i, i ^ bit) for i in range(size)]
-
-
-def exchange(value, bit, size):
-    return lax.ppermute(value, "freq", across(bit, size))
-
-
-def fetch_slabs(own, owners, rank, size):
-    half = own.shape[0] // 2
-    parity = rank & 1
-    halves = own.reshape(2, half, own.shape[1])
-    mine, other = halves[parity], halves[1 - parity]
-    got = exchange(other, 1, size)
-    mismatch = owners ^ rank
-    carried = jnp.where(((mismatch & 1) == 0)[:, None, None], mine[None], got[None])
-    bit = 2
+    )(field, taps, rate, slabs)
+
+
+def exchange(value, mask, size):
+    return lax.ppermute(value, "freq", [(i, i ^ mask) for i in range(size)])
+
+
+def plan(size, height):
+    split, cross = [], []
+    bit = 1
     while bit < size:
-        got = exchange(carried, bit, size)
-        carried = jnp.where(((mismatch & bit) == 0)[:, None, None], carried, got)
+        if len(split) < 2 and (height >> (len(split) + 1)) % SUB == 0:
+            split.append(bit)
+        else:
+            cross.append((bit, bit | sum(b for b, _ in cross)))
         bit *= 2
-    got = exchange(carried, 1, size)
+    return split, cross
+
+
+def halves_of(value, upper):
+    half = value.shape[-2] // 2
+    low, high = value[..., :half, :], value[..., half:, :]
+    return jnp.where(upper, high, low), jnp.where(upper, low, high)
+
+
+def joined(mine, other, upper):
     return jnp.where(
-        parity == 0, jnp.concatenate([carried, got], axis=1), jnp.concatenate([got, carried], axis=1)
+        upper, jnp.concatenate([other, mine], axis=-2), jnp.concatenate([mine, other], axis=-2)
     )
 
 
-def sum_over(partial, rank, size):
-    levels, height, breadth = partial.shape
-    parity = rank & 1
-    halves = partial.reshape(levels, 2, height // 2, breadth)
-    carried = halves[:, parity] + exchange(halves[:, 1 - parity], 1, size)
-    bit = 2
-    while bit < size:
-        carried = carried + exchange(carried, bit, size)
-        bit *= 2
-    got = exchange(carried, 1, size)
-    return jnp.where(
-        parity == 0, jnp.concatenate([carried, got], axis=1), jnp.concatenate([got, carried], axis=1)
-    )
+def fetch_slabs(own, mismatch, turn, rank, size):
+    split, cross = plan(size, own.shape[0])
+    held = own[None]
+    wanted = jnp.zeros_like(mismatch)
+    for i, bit in enumerate(split):
+        upper = (rank & bit) != 0
+        if i == 0:
+            got, _ = halves_of(exchange(held, bit, size), upper)
+            mine, _ = halves_of(held, upper)
+        else:
+            mine, other = halves_of(held, upper)
+            got = exchange(other, bit, size)
+        wanted = wanted + jnp.where((mismatch & bit) != 0, held.shape[0], 0)
+        held = jnp.concatenate([mine, got], axis=0)
+    carried = jnp.broadcast_to(held[:1], (mismatch.shape[0], *held.shape[1:]))
+    for c in range(1, held.shape[0]):
+        carried = jnp.where((wanted == c)[:, None, None], held[c][None], carried)
+    for bit, mask in cross:
+        got = exchange(carried, mask, size)
+        keep = (mismatch & bit)[:, None, None] if bit != cross[-1][0] else turn[:, :1, :1] & bit
+        carried = jnp.where(keep == 0, carried, got)
+    for bit in reversed(split):
+        carried = joined(carried, exchange(carried, bit, size), (rank & bit) != 0)
+    return carried
+
+
+def sums_to_owner(partial, owners, rank, size):
+    split, cross = plan(size, partial.shape[1])
+    carried = partial
+    for bit in split:
+        mine, other = halves_of(carried, (rank & bit) != 0)
+        carried = mine + exchange(other, bit, size)
+    for _, mask in cross:
+        carried = carried + exchange(carried, mask, size)
+
+    def slot(place):
+        return jnp.sum(jnp.where((owners == place)[:, None, None], carried, 0.0), axis=0)
+
+    near = [0]
+    for bit in split:
+        near = near + [n | bit for n in near]
+    slots = {n: slot(rank ^ n) for n in near}
+    for bit in reversed(split):
+        sent = [n for n in near if n & bit]
+        near = [n for n in near if not n & bit]
+        got = exchange(jnp.stack([slots[n] for n in sent]), bit, size)
+        upper = (rank & bit) != 0
+        slots = {n: joined(slots[n], got[sent.index(n | bit)], upper) for n in near}
+    return slots[0]
 
 
 def local(receiver_data, source_spectrum, filter_taps, slowness, depth_owner, source_position):
@@ -285,14 +380,14 @@
     size = lax.axis_size("freq")
     rank = lax.axis_index("freq")
     freq_total = size * freq_local
-    slabs = fetch_slabs(slowness[0], depth_owner, rank, size)
     base = (rank * freq_local).astype(jnp.int32).reshape(1)
-    partial = migrate(
-        receiver_data, slabs, source_spectrum, filter_taps, source_position, base, freq_total
+    mismatch = depth_owner ^ rank
+    field, taps, rate, turn = prepare(
+        receiver_data, source_spectrum, filter_taps, source_position, mismatch, base, freq_total
     )
-    summed = sum_over(partial, rank, size)
-    owned = (depth_owner == rank).astype(jnp.float32)
-    return jnp.sum(summed * owned[:, None, None], axis=0)[None]
+    slabs = fetch_slabs(slowness[0], mismatch, turn, rank, size)
+    partial = migrate(field, taps, rate, slabs, freq_total)
+    return sums_to_owner(partial, depth_owner, rank, size)[None]
 
 
 def solution(mesh):

time: 69.9 us -> 59.4 us (0.85)
  waiting for transfers between devices: 43.1 us -> 24 us
  starting transfers between devices: 11.6 us -> 19.5 us
  other arithmetic: 1.25 us -> 2.27 us
    ppermute x10 -> x12, waiting for transfers between devices: 43.1 us -> 24 us  [exchange(): return lax.ppermute(value, 'freq', [(i, i ^ mask) for i in range(size)])]
    ppermute x10 -> x12, starting transfers between devices: 11.6 us -> 19.5 us  [exchange(): return lax.ppermute(value, 'freq', [(i, i ^ mask) for i in range(size)])]
    pallas_call x0 -> x1, Pallas kernels: none -> 2.06 us  [prepare(): pl.pallas_call(functools.partial(prepare_kernel, freq_total), out_shape=(...]
    pallas_call x1, Pallas kernels: 11.9 us -> 9.83 us  [migrate(): pl.pallas_call(functools.partial(migrate_kernel, freq_total), out_shape=j...]
    select_n x5 -> x12, other arithmetic: 0.39 us -> 1.91 us  [the longest x5 0.95 us: halves_of(): return (jnp.where(upper, high, low), jnp.where(upper, low, high))]
    broadcast_in_dim x1 -> x2, local copies, waits for them, and re-layouts: 0.88 us -> 0.01 us  [fetch_slabs(): carried = jnp.where((wanted == c)[:, None, None], held[c][None], carried)]
  transfers between devices with their start and end apart: 10 -> 12, of which waited for: 10 -> 11; matrix products, arithmetic and copies ran while one was open for 0% -> 2% of each run, Pallas kernels for 0% -> 3%
where the time goes in v2:
time: 59.4 us; the launch traced here: 59.2 us
  waiting for transfers between devices  24 us (40%)
  starting transfers between devices  19.5 us (33%)
  Pallas kernels  11.9 us (20%)
  other arithmetic  2.27 us (4%)
  local copies, waits for them, and re-layouts  1.35 us (2%)
    ppermute x12, waiting for transfers between devices, exchange(): return lax.ppermute(value, 'freq', [(i, i ^ mask) for i in range(size)])  24 us
    ppermute x12, starting transfers between devices, exchange(): return lax.ppermute(value, 'freq', [(i, i ^ mask) for i in range(size)])  19.5 us
    pallas_call x1, Pallas kernels, migrate(): pl.pallas_call(functools.partial(migrate_kernel, freq_total), out_shape=j...  9.83 us
    pallas_call x1, Pallas kernels, prepare(): pl.pallas_call(functools.partial(prepare_kernel, freq_total), out_shape=(...  2.06 us
    unnamed x10, local copies, waits for them, and re-layouts  1.34 us
  transfers between devices with their start and end apart: 12, of which 11 were waited for; matrix products, arithmetic and copies ran while one was open for 2% of the time, Pallas kernels for 3%

profile of v2, /device:TPU:0, one launch (start us, length us, event | category | flops | bytes accessed | tf_op | source)
XLA Modules:
  0.0 59.2 jit_solution(17205027018541065369)
XLA Ops:
  0.0 0.5 collective-permute-start
  0.5 0.0 copy-start.4
  0.5 0.7 %copy-done.4 = s32[3]{0:T(128)S(1)} copy-done((s32[3]{0:T(128)S(1)}, s32[3]{0:T(128)}, u32[]{:S(2)}) %copy-start.4) | copy-done | bytes 36
  1.1 0.9 %slice_select_fusion.3 = f32[1,16,1024]{2,1,0:T(8,128)S(1)} fusion(f32[1,32,1024]{2,1,0:T(8,128)} %param.9, pred[]{:T(512)S(6)} %ne.8), kind=kLoop, calls=%fused_computation.21 | loop fusion | flops 16384 | bytes 196609 | tf_op jit(solution)/shard_map/jit(_where)/select_n | solution.py:318
  2.0 0.0 copy-start
  2.0 0.0 collective-permute-done
  2.1 2.6 %collective-permute-start.1 = (f32[2,8,1024]{2,1,0:T(8,128)S(1)}, f32[2,8,1024]{2,1,0:T(8,128)S(1)}, u32[]{:S(2)}, u32[]{:S(2)}) collective-permute-start(f32[2,8,1024]{2,1,0:T(8,128)S(1)} %get-tuple-element.21), channel_id=1, source_target_pairs={{0,2},{1,3},{2,0},{3,1},{4,6},{5,7},{6,4},{7,5},{8,10},{9,11},{10,... | collective-permute-start | bytes 196616 | tf_op jit(solution)/shard_map/ppermute | solution.py:300
  4.7 2.8 %collective-permute-done.1 = f32[2,8,1024]{2,1,0:T(8,128)S(1)} collective-permute-done((f32[2,8,1024]{2,1,0:T(8,128)S(1)}, f32[2,8,1024]{2,1,0:T(8,128)S(1)}, u32[]{:S(2)}, u32[]{:S(2)}) %collective-permute-start.1) | collective-permute-done | bytes 65568 | tf_op jit(solution)/shard_map/ppermute | solution.py:300
  7.4 0.0 copy-start.1
  7.4 0.1 select_select_fusion
  7.5 1.9 %collective-permute-start.2 = (f32[3,8,1024]{2,1,0:T(8,128)S(1)}, f32[3,8,1024]{2,1,0:T(8,128)S(1)}, u32[]{:S(2)}, u32[]{:S(2)}) collective-permute-start(f32[3,8,1024]{2,1,0:T(8,128)S(1)} %select_select_fusion), channel_id=1, source_target_pairs={{0,4},{1,5},{2,6},{3,7},{4,0},{5,1},{6,2},{7,3},{8,12},{9,13},{10,... | collective-permute-start | bytes 294920 | tf_op jit(solution)/shard_map/ppermute | solution.py:300
  9.4 0.0 copy-start.2
  9.4 0.0 copy-start.3
  9.4 0.0 copy-done
  9.4 0.0 copy-done.1
  9.4 0.7 %copy-done.2 = f32[2,2]{1,0:T(2,128)S(1)} copy-done((f32[2,2]{1,0:T(2,128)S(1)}, f32[2,2]{1,0:T(2,128)}, u32[]{:S(2)}) %copy-start.2) | copy-done | bytes 40
  10.1 0.0 copy-done.3
  10.1 2.1 %shard_map.64 = (f32[2,2,2,8,32,128]{5,4,3,2,1,0:T(8,128)S(1)}, f32[2,4,6,8,128]{4,3,2,1,0:T(8,128)S(1)}, f32[2,8,128]{2,1,0:T(8,128)S(1)}, s32[3,8,128]{2,1,0:T(8,128)S(1)}) custom-call(s32[1]{0:T(128)} %bitcast.base_ref, s32[2]{0:T(128)S(1)} %copy-done.3, s32[3]{0:T(128)S(1)} %get-tuple-element.32.mismatch_ref, f32[2,2]{1,0:T(2,128)S(1)} %copy-done.2, ...), custom_call_target="tpu_custom_call" | custom-call | flops 6553600 | bytes 1572864 | tf_op jit(solution)/shard_map/pallas_call | solution.py:265
  12.1 0.1 collective-permute-done.2
  12.2 0.1 broadcast_select_fusion
  12.3 3.9 %collective-permute-start.3 = (f32[3,8,1024]{2,1,0:T(8,128)S(1)}, f32[3,8,1024]{2,1,0:T(8,128)S(1)}, u32[]{:S(2)}, u32[]{:S(2)}) collective-permute-start(f32[3,8,1024]{2,1,0:T(8,128)S(1)} %broadcast_select_fusion), channel_id=1, source_target_pairs={{0,12},{1,13},{2,14},{3,15},{4,8},{5,9},{6,10},{7,11},{8,4},{9,5},... | collective-permute-start | bytes 294920 | tf_op jit(solution)/shard_map/ppermute | solution.py:300
  16.2 0.2 compare_reduce_fusion
  16.4 2.5 %collective-permute-done.3 = f32[3,8,1024]{2,1,0:T(8,128)S(1)} collective-permute-done((f32[3,8,1024]{2,1,0:T(8,128)S(1)}, f32[3,8,1024]{2,1,0:T(8,128)S(1)}, u32[]{:S(2)}, u32[]{:S(2)}) %collective-permute-start.3) | collective-permute-done | bytes 98336 | tf_op jit(solution)/shard_map/ppermute | solution.py:300
  18.9 0.1 broadcast_select_fusion.1
  18.9 1.8 %collective-permute-start.4 = (f32[3,8,1024]{2,1,0:T(8,128)S(1)}, f32[3,8,1024]{2,1,0:T(8,128)S(1)}, u32[]{:S(2)}, u32[]{:S(2)}) collective-permute-start(f32[3,8,1024]{2,1,0:T(8,128)S(1)} %broadcast_select_fusion.1), channel_id=1, source_target_pairs={{0,2},{1,3},{2,0},{3,1},{4,6},{5,7},{6,4},{7,5},{8,10},{9,11},{10,... | collective-permute-start | bytes 294920 | tf_op jit(solution)/shard_map/ppermute | solution.py:300
  20.7 2.8 %collective-permute-done.4 = f32[3,8,1024]{2,1,0:T(8,128)S(1)} collective-permute-done((f32[3,8,1024]{2,1,0:T(8,128)S(1)}, f32[3,8,1024]{2,1,0:T(8,128)S(1)}, u32[]{:S(2)}, u32[]{:S(2)}) %collective-permute-start.4) | collective-permute-done | bytes 98336 | tf_op jit(solution)/shard_map/ppermute | solution.py:300
  23.6 0.1 collective-permute-start.5
  23.7 1.4 %collective-permute-done.5 = f32[3,16,1024]{2,1,0:T(8,128)S(1)} collective-permute-done((f32[3,16,1024]{2,1,0:T(8,128)S(1)}, f32[3,16,1024]{2,1,0:T(8,128)S(1)}, u32[]{:S(2)}, u32[]{:S(2)}) %collective-permute-start.5) | collective-permute-done | bytes 196640 | tf_op jit(solution)/shard_map/ppermute | solution.py:300
  25.1 9.8 %shard_map.65 = f32[3,32,1024]{2,1,0:T(8,128)S(1)} custom-call(f32[2,2,2,8,32,128]{5,4,3,2,1,0:T(8,128)S(1)} %get-tuple-element.9.field_ref, f32[2,4,6,8,128]{4,3,2,1,0:T(8,128)S(1)} %get-tuple-element.10.taps_ref, f32[2,8,128]{2,1,0:T(8,128)S(1)} %get-tuple-element.11.rate_ref, f32[3,32,1024]{2,1,0:T(8,128)S(1)} %maximum_select_fusion.slab_ref), custom_call_target="tpu_custom_call" | custom-call | tf_op jit(solution)/shard_map/pallas_call | solution.py:284
  35.0 0.2 collective-permute-start.6
  35.2 1.3 %collective-permute-done.6 = f32[3,16,1024]{2,1,0:T(8,128)S(1)} collective-permute-done((f32[3,16,1024]{2,1,0:T(8,128)S(1)}, f32[3,16,1024]{2,1,0:T(8,128)S(1)}, u32[]{:S(2)}, u32[]{:S(2)}) %collective-permute-start.6) | collective-permute-done | bytes 196640 | tf_op jit(solution)/shard_map/ppermute | solution.py:300
  36.6 1.8 %collective-permute-start.7 = (f32[3,8,1024]{2,1,0:T(8,128)S(1)}, f32[3,8,1024]{2,1,0:T(8,128)S(1)}, u32[]{:S(2)}, u32[]{:S(2)}) collective-permute-start(f32[3,8,1024]{2,1,0:T(8,128)S(1)} %slice_select_fusion.1), channel_id=1, source_target_pairs={{0,2},{1,3},{2,0},{3,1},{4,6},{5,7},{6,4},{7,5},{8,10},{9,11},{10,... | collective-permute-start | bytes 294920 | tf_op jit(solution)/shard_map/ppermute | solution.py:300
  38.4 3.1 %collective-permute-done.7 = f32[3,8,1024]{2,1,0:T(8,128)S(1)} collective-permute-done((f32[3,8,1024]{2,1,0:T(8,128)S(1)}, f32[3,8,1024]{2,1,0:T(8,128)S(1)}, u32[]{:S(2)}, u32[]{:S(2)}) %collective-permute-start.7) | collective-permute-done | bytes 98336 | tf_op jit(solution)/shard_map/ppermute | solution.py:300
  41.6 1.1 %collective-permute-start.8 = (f32[3,8,1024]{2,1,0:T(8,128)S(1)}, f32[3,8,1024]{2,1,0:T(8,128)S(1)}, u32[]{:S(2)}, u32[]{:S(2)}) collective-permute-start(f32[3,8,1024]{2,1,0:T(8,128)S(1)} %select_add_fusion.1), channel_id=1, source_target_pairs={{0,4},{1,5},{2,6},{3,7},{4,0},{5,1},{6,2},{7,3},{8,12},{9,13},{10,... | collective-permute-start | bytes 294920 | tf_op jit(solution)/shard_map/ppermute | solution.py:300
  42.7 3.5 %collective-permute-done.8 = f32[3,8,1024]{2,1,0:T(8,128)S(1)} collective-permute-done((f32[3,8,1024]{2,1,0:T(8,128)S(1)}, f32[3,8,1024]{2,1,0:T(8,128)S(1)}, u32[]{:S(2)}, u32[]{:S(2)}) %collective-permute-start.8) | collective-permute-done | bytes 98336 | tf_op jit(solution)/shard_map/ppermute | solution.py:300
  46.2 3.8 %collective-permute-start.9 = (f32[3,8,1024]{2,1,0:T(8,128)S(1)}, f32[3,8,1024]{2,1,0:T(8,128)S(1)}, u32[]{:S(2)}, u32[]{:S(2)}) collective-permute-start(f32[3,8,1024]{2,1,0:T(8,128)S(1)} %add.18), channel_id=1, source_target_pairs={{0,12},{1,13},{2,14},{3,15},{4,8},{5,9},{6,10},{7,11},{8,4},{9,5},... | collective-permute-start | bytes 294920 | tf_op jit(solution)/shard_map/ppermute | solution.py:300
  50.0 2.7 %collective-permute-done.9 = f32[3,8,1024]{2,1,0:T(8,128)S(1)} collective-permute-done((f32[3,8,1024]{2,1,0:T(8,128)S(1)}, f32[3,8,1024]{2,1,0:T(8,128)S(1)}, u32[]{:S(2)}, u32[]{:S(2)}) %collective-permute-start.9) | collective-permute-done | bytes 98336 | tf_op jit(solution)/shard_map/ppermute | solution.py:300
  52.7 0.1 select_reduce_fusion.1
  52.8 1.8 %collective-permute-start.10 = (f32[2,8,1024]{2,1,0:T(8,128)S(1)}, f32[2,8,1024]{2,1,0:T(8,128)S(1)}, u32[]{:S(2)}, u32[]{:S(2)}) collective-permute-start(f32[2,8,1024]{2,1,0:T(8,128)S(1)} %pad_maximum_fusion.1), channel_id=1, source_target_pairs={{0,2},{1,3},{2,0},{3,1},{4,6},{5,7},{6,4},{7,5},{8,10},{9,11},{10,... | collective-permute-start | bytes 196616 | tf_op jit(solution)/shard_map/ppermute | solution.py:300
  54.6 2.5 %collective-permute-done.10 = f32[2,8,1024]{2,1,0:T(8,128)S(1)} collective-permute-done((f32[2,8,1024]{2,1,0:T(8,128)S(1)}, f32[2,8,1024]{2,1,0:T(8,128)S(1)}, u32[]{:S(2)}, u32[]{:S(2)}) %collective-permute-start.10) | collective-permute-done | bytes 65568 | tf_op jit(solution)/shard_map/ppermute | solution.py:300
  57.2 0.1 collective-permute-start.11
  57.3 1.2 %collective-permute-done.11 = f32[1,16,1024]{2,1,0:T(8,128)S(1)} collective-permute-done((f32[1,16,1024]{2,1,0:T(8,128)S(1)}, f32[1,16,1024]{2,1,0:T(8,128)S(1)}, u32[]{:S(2)}, u32[]{:S(2)}) %collective-permute-start.11) | collective-permute-done | bytes 65568 | tf_op jit(solution)/shard_map/ppermute | solution.py:300
  58.5 0.7 %maximum_select_fusion.2 = f32[1,32,1024]{2,1,0:T(8,128)} fusion(f32[1,16,1024]{2,1,0:T(8,128)S(1)} %fusion.1, f32[1,16,1024]{2,1,0:T(8,128)S(1)} %collective-permute-done.11, pred[]{:T(512)S(6)} %ne.8), kind=kLoop, calls=%fused_computation.6 | loop fusion | flops 98304 | bytes 262145 | tf_op jit(solution)/shard_map/jit(_where)/select_n | solution.py:322
  (18 shorter events, 0.2 us)
Async XLA Ops:
  0.0 2.0 %collective-permute-start = (f32[1,32,1024]{2,1,0:T(8,128)}, f32[1,32,1024]{2,1,0:T(8,128)S(1)}, u32[]{:S(2)}, u32[]{:S(2)}) collective-permute-start(f32[1,32,1024]{2,1,0:T(8,128)} %param.9), channel_id=1, source_target_pairs={{0,1},{1,0},{2,3},{3,2},{4,5},{5,4},{6,7},{7,6},{8,9},{9,8},{10,11... | collective-permute-start | bytes 393224 | tf_op jit(solution)/shard_map/ppermute | solution.py:300
  0.5 0.7 %copy-start.4 = (s32[3]{0:T(128)S(1)}, s32[3]{0:T(128)}, u32[]{:S(2)}) copy-start(s32[3]{0:T(128)} %param.10) | copy-start | bytes 40
  2.0 7.4 %copy-start = (f32[2,2,32,1024]{3,2,1,0:T(8,128)S(1)}, f32[2,2,32,1024]{3,2,1,0:T(8,128)}, u32[]{:S(2)}) copy-start(f32[2,2,32,1024]{3,2,1,0:T(8,128)} %receiver_ref.1) | copy-start | bytes 1572868
  2.1 5.3 %collective-permute-start.1 = (f32[2,8,1024]{2,1,0:T(8,128)S(1)}, f32[2,8,1024]{2,1,0:T(8,128)S(1)}, u32[]{:S(2)}, u32[]{:S(2)}) collective-permute-start(f32[2,8,1024]{2,1,0:T(8,128)S(1)} %get-tuple-element.21), channel_id=1, source_target_pairs={{0,2},{1,3},{2,0},{3,1},{4,6},{5,7},{6,4},{7,5},{8,10},{9,11},{10,... | collective-permute-start | bytes 196616 | tf_op jit(solution)/shard_map/ppermute | solution.py:300
  7.4 2.0 %copy-start.1 = (f32[2,4,6]{2,1,0:T(4,128)S(1)}, f32[2,4,6]{2,1,0:T(4,128)}, u32[]{:S(2)}) copy-start(f32[2,4,6]{2,1,0:T(4,128)} %taps_ref.1) | copy-start | bytes 580
  7.5 4.7 %collective-permute-start.2 = (f32[3,8,1024]{2,1,0:T(8,128)S(1)}, f32[3,8,1024]{2,1,0:T(8,128)S(1)}, u32[]{:S(2)}, u32[]{:S(2)}) collective-permute-start(f32[3,8,1024]{2,1,0:T(8,128)S(1)} %select_select_fusion), channel_id=1, source_target_pairs={{0,4},{1,5},{2,6},{3,7},{4,0},{5,1},{6,2},{7,3},{8,12},{9,13},{10,... | collective-permute-start | bytes 294920 | tf_op jit(solution)/shard_map/ppermute | solution.py:300
  9.4 0.7 %copy-start.2 = (f32[2,2]{1,0:T(2,128)S(1)}, f32[2,2]{1,0:T(2,128)}, u32[]{:S(2)}) copy-start(f32[2,2]{1,0:T(2,128)} %spectrum_ref.1) | copy-start | bytes 52
  9.4 0.7 %copy-start.3 = (s32[2]{0:T(128)S(1)}, s32[2]{0:T(128)}, u32[]{:S(2)}) copy-start(s32[2]{0:T(128)} %position_ref.1) | copy-start | bytes 28
  12.3 6.5 %collective-permute-start.3 = (f32[3,8,1024]{2,1,0:T(8,128)S(1)}, f32[3,8,1024]{2,1,0:T(8,128)S(1)}, u32[]{:S(2)}, u32[]{:S(2)}) collective-permute-start(f32[3,8,1024]{2,1,0:T(8,128)S(1)} %broadcast_select_fusion), channel_id=1, source_target_pairs={{0,12},{1,13},{2,14},{3,15},{4,8},{5,9},{6,10},{7,11},{8,4},{9,5},... | collective-permute-start | bytes 294920 | tf_op jit(solution)/shard_map/ppermute | solution.py:300
  18.9 4.6 %collective-permute-start.4 = (f32[3,8,1024]{2,1,0:T(8,128)S(1)}, f32[3,8,1024]{2,1,0:T(8,128)S(1)}, u32[]{:S(2)}, u32[]{:S(2)}) collective-permute-start(f32[3,8,1024]{2,1,0:T(8,128)S(1)} %broadcast_select_fusion.1), channel_id=1, source_target_pairs={{0,2},{1,3},{2,0},{3,1},{4,6},{5,7},{6,4},{7,5},{8,10},{9,11},{10,... | collective-permute-start | bytes 294920 | tf_op jit(solution)/shard_map/ppermute | solution.py:300
  23.6 1.5 %collective-permute-start.5 = (f32[3,16,1024]{2,1,0:T(8,128)S(1)}, f32[3,16,1024]{2,1,0:T(8,128)S(1)}, u32[]{:S(2)}, u32[]{:S(2)}) collective-permute-start(f32[3,16,1024]{2,1,0:T(8,128)S(1)} %maximum_select_fusion.1), channel_id=1, source_target_pairs={{0,1},{1,0},{2,3},{3,2},{4,5},{5,4},{6,7},{7,6},{8,9},{9,8},{10,11... | collective-permute-start | bytes 589832 | tf_op jit(solution)/shard_map/ppermute | solution.py:300
  35.0 1.5 %collective-permute-start.6 = (f32[3,16,1024]{2,1,0:T(8,128)S(1)}, f32[3,16,1024]{2,1,0:T(8,128)S(1)}, u32[]{:S(2)}, u32[]{:S(2)}) collective-permute-start(f32[3,16,1024]{2,1,0:T(8,128)S(1)} %slice_select_fusion), channel_id=1, source_target_pairs={{0,1},{1,0},{2,3},{3,2},{4,5},{5,4},{6,7},{7,6},{8,9},{9,8},{10,11... | collective-permute-start | bytes 589832 | tf_op jit(solution)/shard_map/ppermute | solution.py:300
  36.6 4.9 %collective-permute-start.7 = (f32[3,8,1024]{2,1,0:T(8,128)S(1)}, f32[3,8,1024]{2,1,0:T(8,128)S(1)}, u32[]{:S(2)}, u32[]{:S(2)}) collective-permute-start(f32[3,8,1024]{2,1,0:T(8,128)S(1)} %slice_select_fusion.1), channel_id=1, source_target_pairs={{0,2},{1,3},{2,0},{3,1},{4,6},{5,7},{6,4},{7,5},{8,10},{9,11},{10,... | collective-permute-start | bytes 294920 | tf_op jit(solution)/shard_map/ppermute | solution.py:300
  41.6 4.7 %collective-permute-start.8 = (f32[3,8,1024]{2,1,0:T(8,128)S(1)}, f32[3,8,1024]{2,1,0:T(8,128)S(1)}, u32[]{:S(2)}, u32[]{:S(2)}) collective-permute-start(f32[3,8,1024]{2,1,0:T(8,128)S(1)} %select_add_fusion.1), channel_id=1, source_target_pairs={{0,4},{1,5},{2,6},{3,7},{4,0},{5,1},{6,2},{7,3},{8,12},{9,13},{10,... | collective-permute-start | bytes 294920 | tf_op jit(solution)/shard_map/ppermute | solution.py:300
  46.2 6.5 %collective-permute-start.9 = (f32[3,8,1024]{2,1,0:T(8,128)S(1)}, f32[3,8,1024]{2,1,0:T(8,128)S(1)}, u32[]{:S(2)}, u32[]{:S(2)}) collective-permute-start(f32[3,8,1024]{2,1,0:T(8,128)S(1)} %add.18), channel_id=1, source_target_pairs={{0,12},{1,13},{2,14},{3,15},{4,8},{5,9},{6,10},{7,11},{8,4},{9,5},... | collective-permute-start | bytes 294920 | tf_op jit(solution)/shard_map/ppermute | solution.py:300
  52.8 4.3 %collective-permute-start.10 = (f32[2,8,1024]{2,1,0:T(8,128)S(1)}, f32[2,8,1024]{2,1,0:T(8,128)S(1)}, u32[]{:S(2)}, u32[]{:S(2)}) collective-permute-start(f32[2,8,1024]{2,1,0:T(8,128)S(1)} %pad_maximum_fusion.1), channel_id=1, source_target_pairs={{0,2},{1,3},{2,0},{3,1},{4,6},{5,7},{6,4},{7,5},{8,10},{9,11},{10,... | collective-permute-start | bytes 196616 | tf_op jit(solution)/shard_map/ppermute | solution.py:300
  57.2 1.3 %collective-permute-start.11 = (f32[1,16,1024]{2,1,0:T(8,128)S(1)}, f32[1,16,1024]{2,1,0:T(8,128)S(1)}, u32[]{:S(2)}, u32[]{:S(2)}) collective-permute-start(f32[1,16,1024]{2,1,0:T(8,128)S(1)} %maximum_select_fusion.3), channel_id=1, source_target_pairs={{0,1},{1,0},{2,3},{3,2},{4,5},{5,4},{6,7},{7,6},{8,9},{9,8},{10,11... | collective-permute-start | bytes 196616 | tf_op jit(solution)/shard_map/ppermute | solution.py:300

commit v3 on v2

v3 whole, which is shorter than its diff:
```python
import functools
import math

import jax
import jax.numpy as jnp
from jax import lax
from jax.experimental import pallas as pl
from jax.experimental.pallas import tpu as pltpu
from jax.sharding import PartitionSpec as P

lens_rate = 3.0
wave_rate = 0.5
directions = ((1, 0), (0, 1), (1, 1), (1, -1))
LANES = 128
SUB = 8
REACH = 2
TWO_OVER_PI = 2.0 / math.pi
PI_2 = (1.5703125, 4.837512969970703125e-4, 7.54978995489188216e-8)


def cos_sin(x):
    turns = jnp.floor(x * TWO_OVER_PI + 0.5)
    r = x - turns * PI_2[0]
    r = r - turns * PI_2[1]
    r = r - turns * PI_2[2]
    r2 = r * r
    s = r + r * r2 * (-1.6666654611e-1 + r2 * (8.3321608736e-3 + r2 * -1.9515295891e-4))
    c = (1.0 - 0.5 * r2) + r2 * r2 * (
        4.166664568298827e-2 + r2 * (-1.388731625493765e-3 + r2 * 2.443315711809948e-5)
    )
    quadrant = turns.astype(jnp.int32)
    odd = (quadrant & 1) == 1
    cos_value = jnp.where(odd, s, c)
    sin_value = jnp.where(odd, c, s)
    cos_value = jnp.where(((quadrant + 1) & 2) == 2, -cos_value, cos_value)
    sin_value = jnp.where((quadrant & 2) == 2, -sin_value, sin_value)
    return cos_value, sin_value


def quotient(x, divisor):
    return jnp.floor((x.astype(jnp.float32) + 0.5) * (1.0 / divisor)).astype(jnp.int32)


def columns():
    return lax.broadcasted_iota(jnp.int32, (SUB, LANES), 1)


def interleave(blocks):
    count = len(blocks)
    out = []
    for c in range(count):
        column = columns() * count + c
        pick, source = column & (LANES - 1), column >> (LANES.bit_length() - 1)
        value = jnp.take_along_axis(blocks[0], pick, axis=1)
        for b in range(1, count):
            value = jnp.where(source == b, jnp.take_along_axis(blocks[b], pick, axis=1), value)
        out.append(value)
    return out


def deinterleave(blocks):
    count = len(blocks)
    out = []
    for b in range(count):
        column = columns() + LANES * b
        pick = quotient(column, count)
        source = column - pick * count
        value = jnp.take_along_axis(blocks[0], pick, axis=1)
        for c in range(1, count):
            value = jnp.where(source == c, jnp.take_along_axis(blocks[c], pick, axis=1), value)
        out.append(value)
    return out


def tile(ref, f, field, part, block, group, shift=0):
    return ref.at[f, field, part, block, pl.ds(SUB * group + shift, SUB), :]


def prepare_kernel(
    freq_total,
    base_ref,
    place_ref,
    mismatch_ref,
    own_ref,
    own_scalars_ref,
    near_ref,
    near_scalars_ref,
    field_ref,
    taps_out_ref,
    rate_ref,
    turn_ref,
):
    freq_local, _, height, breadth = own_ref.shape
    blocks = breadth // LANES
    groups = height // SUB
    lane = columns()
    row = lax.broadcasted_iota(jnp.int32, (SUB, LANES), 0)
    taps_count = len(directions) * 6

    def scalar(ref, i):
        at = LANES * (i % blocks)
        return jnp.broadcast_to(ref[i // blocks : i // blocks + 1, at : at + LANES], (SUB, LANES))

    def number(side, f):
        return (base_ref[side] + f).astype(jnp.float32) + 1.0

    both = ((own_ref, own_scalars_ref), (near_ref, near_scalars_ref))
    for side, (receiver_ref, scalars_ref) in enumerate(both):
        for f in range(freq_local):
            for d in range(len(directions)):
                for i in range(6):
                    taps_out_ref[side * freq_local + f, d, i] = scalar(scalars_ref, f * taps_count + d * 6 + i)
            rate_ref[side * freq_local + f] = jnp.full(
                (SUB, LANES), number(side, f) * (lens_rate / freq_total), jnp.float32
            )

        @pl.loop(0, freq_local)
        def _(f):
            for part in range(2):
                for g in range(groups):
                    loaded = [
                        receiver_ref[f, part, SUB * g : SUB * (g + 1), LANES * b : LANES * (b + 1)]
                        for b in range(blocks)
                    ]
                    for b, value in enumerate(interleave(loaded)):
                        at = tile(field_ref, side * freq_local + f, 1, part, b, g)
                        at[...] = -value if part else value

    for t in range(mismatch_ref.shape[0]):
        turn_ref[t] = jnp.full((SUB, LANES), mismatch_ref[t], jnp.int32)

    src_row = place_ref[0].astype(jnp.float32)
    src_col = place_ref[1].astype(jnp.float32)
    first_col = place_ref[2]
    for g in range(groups):
        for b in range(blocks):
            d_row = (row + SUB * g).astype(jnp.float32) - src_row
            d_col = (lane * blocks + (first_col + b)).astype(jnp.float32) - src_col
            distance = jnp.sqrt(d_row * d_row + d_col * d_col + 1.0)
            amplitude = 1.0 / (1.0 + distance / (height / 4.0))
            for side, (_, scalars_ref) in enumerate(both):
                for f in range(freq_local):
                    cos_value, sin_value = cos_sin(number(side, f) * (wave_rate / freq_total) * distance)
                    base_re = amplitude * cos_value
                    base_im = -amplitude * sin_value
                    w_re = scalar(scalars_ref, freq_local * taps_count + 2 * f)
                    w_im = scalar(scalars_ref, freq_local * taps_count + 2 * f + 1)
                    at = side * freq_local + f
                    tile(field_ref, at, 0, 0, b, g)[...] = w_re * base_re - w_im * base_im
                    tile(field_ref, at, 0, 1, b, g)[...] = w_re * base_im + w_im * base_re


def migrate_kernel(
    freq_total, field_ref, taps_ref, rate_ref, slab_ref, out_ref, a_ref, b_ref, v_ref, c_ref
):
    freq_local = field_ref.shape[0]
    levels, height, breadth = slab_ref.shape
    blocks = breadth // LANES
    groups = height // SUB
    lane = lax.broadcasted_iota(jnp.int32, (SUB, LANES), 1)
    not_first = lane > 0
    not_last = lane < LANES - 1

    def load(ref, f, field, part, block, group, shift=0):
        return tile(ref, f, field, part, block + REACH, group + 1, shift)[...]

    def store(ref, f, field, part, block, group, value):
        tile(ref, f, field, part, block + REACH, group + 1)[...] = value

    zero = jnp.zeros((SUB, LANES), jnp.float32)

    @pl.loop(0, freq_local)
    def _(f):
        for ref in (a_ref, b_ref):
            for field in range(2):
                for part in range(2):
                    for block in range(blocks + 2 * REACH):
                        tile(ref, f, field, part, block, 0)[...] = zero
                        tile(ref, f, field, part, block, groups + 1)[...] = zero

    def rows_of(g):
        return pl.ds(pl.multiple_of(SUB * g, SUB), SUB)

    def take_slab(t, g):
        rows = rows_of(g)
        loaded = [slab_ref[t, rows, LANES * b : LANES * (b + 1)] for b in range(blocks)]
        for b, value in enumerate(interleave(loaded)):
            v_ref[t, b, rows, :] = value

    def give_sum(t, g):
        rows = rows_of(g)
        for b, value in enumerate(deinterleave([c_ref[t, b, rows] for b in range(blocks)])):
            out_ref[t, rows, LANES * b : LANES * (b + 1)] = value * (1.0 / math.sqrt(freq_total))

    def beside(work, t, f):
        share = -(-groups // freq_local)
        for k in range(share):
            work(t, jnp.minimum(f * share + k, groups - 1))

    for g in range(groups):
        take_slab(0, g)

    def lens(t, get):
        @pl.loop(0, freq_local)
        def _(f):
            rate = rate_ref[f]
            for g in range(groups):
                for b in range(blocks):
                    cos_value, sin_value = cos_sin(rate * v_ref[t, b, SUB * g : SUB * (g + 1), :])
                    for field in range(2):
                        re, im = get(f, field, 0, b, g), get(f, field, 1, b, g)
                        store(a_ref, f, field, 0, b, g, re * cos_value + im * sin_value)
                        store(a_ref, f, field, 1, b, g, im * cos_value - re * sin_value)

    def filtered(src, f, field, b, g, d, taps):
        step_x, step_y = directions[d]

        def at(part, k):
            return load(src, f, field, part, b + k * step_y, g, k * step_x)

        c0r, c0i, c1r, c1i, c2r, c2i = taps
        re, im = at(0, 0), at(1, 0)
        p1r, p1i = at(0, 1) + at(0, -1), at(1, 1) + at(1, -1)
        p2r, p2i = at(0, 2) + at(0, -2), at(1, 2) + at(1, -2)
        out_re = (re * c0r - im * c0i) + (p1r * c1r - p1i * c1i) + (p2r * c2r - p2i * c2i)
        out_im = (re * c0i + im * c0r) + (p1r * c1i + p1i * c1r) + (p2r * c2i + p2i * c2r)
        return out_re, out_im

    def sweep(src, dst, d, work=None, level=None):
        @pl.loop(0, freq_local)
        def _(f):
            taps = [taps_ref[f, d, i] for i in range(6)]
            if work is not None:
                beside(work, level, f)
            for field in range(2):
                for g in range(groups):
                    for b in range(blocks):
                        for part, value in enumerate(filtered(src, f, field, b, g, d, taps)):
                            store(dst, f, field, part, b, g, value)
                            if b < REACH:
                                edge = jnp.where(not_last, pltpu.roll(value, LANES - 1, 1), 0.0)
                                store(dst, f, field, part, b + blocks, g, edge)
                            if b >= blocks - REACH:
                                edge = jnp.where(not_first, pltpu.roll(value, 1, 1), 0.0)
                                store(dst, f, field, part, b - blocks, g, edge)

    def last_sweep(src, dst, d, t):
        @pl.loop(0, freq_local)
        def _(f):
            taps = [taps_ref[f, d, i] for i in range(6)]
            for g in range(groups):
                for b in range(blocks):
                    s_re, s_im = filtered(src, f, 0, b, g, d, taps)
                    r_re, r_im = filtered(src, f, 1, b, g, d, taps)
                    store(dst, f, 0, 0, b, g, s_re)
                    store(dst, f, 0, 1, b, g, s_im)
                    store(dst, f, 1, 0, b, g, r_re)
                    store(dst, f, 1, 1, b, g, r_im)
                    term = s_re * r_re - s_im * r_im
                    at = (t, b, slice(SUB * g, SUB * (g + 1)))
                    c_ref[at] = jnp.where(f == 0, term, c_ref[at] + term)

    def depth_step(t):
        sweep(a_ref, b_ref, 0, take_slab, jnp.minimum(t + 1, levels - 1))
        sweep(b_ref, a_ref, 1, give_sum, jnp.maximum(t - 1, 0))
        sweep(a_ref, b_ref, 2)
        last_sweep(b_ref, a_ref, 3, t)

    lens(0, lambda f, field, part, b, g: tile(field_ref, f, field, part, b, g)[...])

    @pl.loop(0, levels)
    def _(t):
        @pl.when(t > 0)
        def _():
            lens(t, lambda f, field, part, b, g: load(a_ref, f, field, part, b, g))

        depth_step(t)

    for g in range(groups):
        give_sum(levels - 1, g)


SMEM = pl.BlockSpec(memory_space=pltpu.SMEM)
VMEM = pl.BlockSpec(memory_space=pltpu.VMEM)


def prepare(own, own_scalars, near, near_scalars, place, mismatch, base, freq_total):
    freq_local, _, height, breadth = own.shape
    blocks = breadth // LANES
    cells = 2 * freq_local * height * breadth
    return pl.pallas_call(
        functools.partial(prepare_kernel, freq_total),
        out_shape=(
            jax.ShapeDtypeStruct((2 * freq_local, 2, 2, blocks, height, LANES), jnp.float32),
            jax.ShapeDtypeStruct((2 * freq_local, len(directions), 6, SUB, LANES), jnp.float32),
            jax.ShapeDtypeStruct((2 * freq_local, SUB, LANES), jnp.float32),
            jax.ShapeDtypeStruct((mismatch.shape[0], SUB, LANES), jnp.int32),
        ),
        in_specs=[SMEM, SMEM, SMEM, VMEM, VMEM, VMEM, VMEM],
        out_specs=(VMEM, VMEM, VMEM, VMEM),
        cost_estimate=pl.CostEstimate(flops=100 * cells, bytes_accessed=24 * cells, transcendentals=0),
        compiler_params=pltpu.CompilerParams(vmem_limit_bytes=32 * 1024 * 1024),
    )(base, place, mismatch, own, own_scalars, near, near_scalars)


def migrate(field, taps, rate, slabs, freq_total):
    freq_local, _, _, blocks, height, _ = field.shape
    levels = slabs.shape[0]
    state = pltpu.VMEM((freq_local, 2, 2, blocks + 2 * REACH, height + 2 * SUB, LANES), jnp.float32)
    return pl.pallas_call(
        functools.partial(migrate_kernel, freq_total),
        out_shape=jax.ShapeDtypeStruct(slabs.shape, jnp.float32),
        in_specs=[VMEM, VMEM, VMEM, VMEM],
        out_specs=VMEM,
        scratch_shapes=[
            state,
            state,
            pltpu.VMEM((levels, blocks, height, LANES), jnp.float32),
            pltpu.VMEM((levels, blocks, height, LANES), jnp.float32),
        ],
        compiler_params=pltpu.CompilerParams(vmem_limit_bytes=32 * 1024 * 1024),
    )(field, taps, rate, slabs)


def exchange(value, mask, size):
    return lax.ppermute(value, "freq", [(i, i ^ mask) for i in range(size)])


NEAR_ROWS = 1
NEAR_COLUMNS = 2


def far_bits(size):
    found = []
    bit = 2 * NEAR_COLUMNS
    while bit < size:
        found.append((bit, bit | sum(b for b, _ in found)))
        bit *= 2
    return found


def rows_split(value, upper):
    half = value.shape[-2] // 2
    low, high = value[..., :half, :], value[..., half:, :]
    return jnp.where(upper, high, low), jnp.where(upper, low, high)


def columns_split(value, upper, width):
    low, high = value[..., :width], value[..., value.shape[-1] - width :]
    return jnp.where(upper, high, low), jnp.where(upper, low, high)


def joined(mine, other, upper, axis):
    return jnp.where(
        upper, jnp.concatenate([other, mine], axis=axis), jnp.concatenate([mine, other], axis=axis)
    )


def fetch_slabs(own, mismatch, turn, rank, size, width):
    upper_rows = (rank & NEAR_ROWS) != 0
    upper_columns = (rank & NEAR_COLUMNS) != 0
    got, _ = rows_split(exchange(own, NEAR_ROWS, size), upper_rows)
    mine, _ = rows_split(own, upper_rows)
    held = jnp.stack([mine, got])
    mine, other = columns_split(held, upper_columns, width)
    held = jnp.concatenate([mine, exchange(other, NEAR_COLUMNS, size)], axis=0)
    wanted = mismatch & (NEAR_ROWS | NEAR_COLUMNS)
    carried = jnp.broadcast_to(held[:1], (mismatch.shape[0], *held.shape[1:]))
    for c in range(1, held.shape[0]):
        carried = jnp.where((wanted == c)[:, None, None], held[c][None], carried)
    far = far_bits(size)
    for bit, mask in far:
        got = exchange(carried, mask, size)
        keep = (mismatch & bit)[:, None, None] if bit != far[-1][0] else turn[:, :1, :1] & bit
        carried = jnp.where(keep == 0, carried, got)
    return joined(carried, exchange(carried, NEAR_ROWS, size), upper_rows, -2)


def sums_to_owner(partial, owners, rank, size, half):
    upper_rows = (rank & NEAR_ROWS) != 0
    upper_columns = (rank & NEAR_COLUMNS) != 0
    partial, _ = columns_split(partial, upper_columns, half)
    mine, other = rows_split(partial, upper_rows)
    carried = mine + exchange(other, NEAR_ROWS, size)
    for _, mask in far_bits(size):
        carried = carried + exchange(carried, mask, size)

    def slot(place):
        return jnp.sum(jnp.where((owners == place)[:, None, None], carried, 0.0), axis=0)

    mine = jnp.stack([slot(rank), slot(rank ^ NEAR_ROWS)])
    other = jnp.stack([slot(rank ^ NEAR_COLUMNS), slot(rank ^ NEAR_ROWS ^ NEAR_COLUMNS)])
    both = joined(mine, exchange(other, NEAR_COLUMNS, size), upper_columns, -1)
    return joined(both[0], exchange(both[1], NEAR_ROWS, size), upper_rows, -2)


def local(receiver_data, source_spectrum, filter_taps, slowness, depth_owner, source_position):
    freq_local, _, height, breadth = receiver_data.shape
    levels = depth_owner.shape[0]
    size = lax.axis_size("freq")
    rank = lax.axis_index("freq")
    freq_total = size * freq_local
    half = breadth // 2
    border = REACH * sum(1 for _, step_y in directions if step_y) * levels
    width = -(-(half + border) // LANES) * LANES
    upper_columns = (rank & NEAR_COLUMNS) != 0

    scalars = jnp.concatenate([filter_taps.reshape(-1), source_spectrum.reshape(-1)])
    scalar_rows = -(-scalars.shape[0] * LANES // (width * SUB)) * SUB
    scalars = jnp.pad(scalars, (0, scalar_rows * width // LANES - scalars.shape[0]))
    scalars = jnp.repeat(scalars, LANES).reshape(scalar_rows, width)
    own, sent = columns_split(receiver_data, upper_columns, width)
    sent = jnp.concatenate([sent.reshape(-1, width), scalars], axis=0)
    near = exchange(sent, NEAR_COLUMNS, size)
    near, near_scalars = near[:-scalar_rows].reshape(own.shape), near[-scalar_rows:]

    mismatch = depth_owner ^ rank
    first_column = jnp.where(upper_columns, breadth - width, 0).astype(jnp.int32).reshape(1)
    place = jnp.concatenate([source_position, first_column])
    base = (jnp.stack([rank, rank ^ NEAR_COLUMNS]) * freq_local).astype(jnp.int32)
    field, taps, rate, turn = prepare(
        own, scalars, near, near_scalars, place, mismatch, base, freq_total
    )
    slabs = fetch_slabs(slowness[0], mismatch, turn, rank, size, width)
    partial = migrate(field, taps, rate, slabs, freq_total)
    return sums_to_owner(partial, depth_owner, rank, size, half)[None]


def solution(mesh):
    return jax.shard_map(
        local,
        mesh=mesh,
        in_specs=(
            P(("shot", "freq"), None, None, None),
            P("freq", None),
            P("freq", None, None),
            P("freq", None, None),
            P("shot"),
            P("shot"),
        ),
        out_specs=P(("shot", "freq"), None, None),
        check_vma=False,
    )
```

time: 59.4 us -> 57.9 us (0.975)
  starting transfers between devices: 19.5 us -> 15.2 us
  Pallas kernels: 11.9 us -> 14.4 us
  waiting for transfers between devices: 24 us -> 22.5 us
  other arithmetic: 2.27 us -> 3.6 us
    ppermute x12 -> x11, starting transfers between devices: 19.5 us -> 15.2 us  [exchange(): return lax.ppermute(value, 'freq', [(i, i ^ mask) for i in range(size)])]
    pallas_call x1, Pallas kernels: 9.83 us -> 11.6 us  [migrate(): pl.pallas_call(functools.partial(migrate_kernel, freq_total), out_shape=j...]
    reshape x0 -> x2, local copies, waits for them, and re-layouts: none -> 1.53 us  [the longest x1 0.77 us: local(): filter_taps.reshape(-1)]
    ppermute x12 -> x11, waiting for transfers between devices: 24 us -> 22.5 us  [exchange(): return lax.ppermute(value, 'freq', [(i, i ^ mask) for i in range(size)])]
    unnamed x10 -> x5, local copies, waits for them, and re-layouts: 1.34 us -> 0.03 us
    select_n x9 -> x8, other arithmetic: 1.67 us -> 2.76 us  [the longest x3 1.16 us: columns_split(): return (jnp.where(upper, high, low), jnp.where(upper, low, high))]
    pallas_call x1, Pallas kernels: 2.06 us -> 2.83 us  [prepare(): pl.pallas_call(functools.partial(prepare_kernel, freq_total), out_shape=(...]
  transfers between devices with their start and end apart: 12 -> 11, of which waited for: 11 -> 9; matrix products, arithmetic and copies ran while one was open for 2% -> 7% of each run, Pallas kernels for 3% -> 5%
where the time goes in v3:
time: 57.9 us; the launch traced here: 57.7 us
  waiting for transfers between devices  22.5 us (39%)
  starting transfers between devices  15.2 us (26%)
  Pallas kernels  14.4 us (25%)
  other arithmetic  3.6 us (6%)
  local copies, waits for them, and re-layouts  1.77 us (3%)
    ppermute x11, waiting for transfers between devices, exchange(): return lax.ppermute(value, 'freq', [(i, i ^ mask) for i in range(size)])  22.5 us
    ppermute x11, starting transfers between devices, exchange(): return lax.ppermute(value, 'freq', [(i, i ^ mask) for i in range(size)])  15.2 us
    pallas_call x1, Pallas kernels, migrate(): pl.pallas_call(functools.partial(migrate_kernel, freq_total), out_shape=j...  11.6 us
    pallas_call x1, Pallas kernels, prepare(): pl.pallas_call(functools.partial(prepare_kernel, freq_total), out_shape=(...  2.83 us
  transfers between devices with their start and end apart: 11, of which 9 were waited for; matrix products, arithmetic and copies ran while one was open for 7% of the time, Pallas kernels for 5%

profile of v3, /device:TPU:0, one launch (start us, length us, event | category | flops | bytes accessed | tf_op | source)
XLA Modules:
  0.0 57.7 jit_solution(5886926367286458783)
XLA Ops:
  0.0 0.0 copy-start
  0.0 0.5 collective-permute-start.1
  0.5 0.8 %reshape.81 = f32[4]{0:T(128)S(1)} reshape(f32[2,2]{1,0:T(2,128)} %param.7) | data formatting | bytes 32 | tf_op jit(solution)/shard_map/reshape | solution.py:408
  1.2 0.8 %reshape.80 = f32[48]{0:T(128)S(1)} reshape(f32[2,4,6]{2,1,0:T(4,128)} %param.8) | data formatting | bytes 384 | tf_op jit(solution)/shard_map/reshape | solution.py:408
  2.0 0.1 fusion.4
  2.1 0.1 broadcast_in_dim.111
  2.1 0.1 broadcast_in_dim.112
  2.3 0.9 %slice_select_fusion.5 = f32[1,16,1024]{2,1,0:T(8,128)S(1)} fusion(f32[1,32,1024]{2,1,0:T(8,128)} %param.9, pred[]{:T(512)S(6)} %ne.4), kind=kLoop, calls=%fused_computation.22 | loop fusion | flops 16384 | bytes 196609 | tf_op jit(solution)/shard_map/jit(_where)/select_n | solution.py:345
  3.1 1.1 %slice_select_fusion = (f32[2,2,32,640]{3,2,1,0:T(8,128)S(1)}, f32[2,2,32,640]{3,2,1,0:T(8,128)S(1)}) fusion(f32[2,2,32,1024]{3,2,1,0:T(8,128)} %param.6, pred[]{:T(512)S(6)} %ne.10), kind=kLoop, calls=%fused_computation.1 | loop fusion | flops 163840 | bytes 1310721 | tf_op jit(solution)/shard_map/jit(_where)/select_n | solution.py:350
  4.3 0.0 copy-done
  4.3 0.0 copy-start.1
  4.3 0.0 collective-permute-done.1
  4.4 2.6 %collective-permute-start.2 = (f32[2,16,640]{2,1,0:T(8,128)S(1)}, f32[2,16,640]{2,1,0:T(8,128)S(1)}, u32[]{:S(2)}, u32[]{:S(2)}) collective-permute-start(f32[2,16,640]{2,1,0:T(8,128)S(1)} %get-tuple-element.23), channel_id=1, source_target_pairs={{0,2},{1,3},{2,0},{3,1},{4,6},{5,7},{6,4},{7,5},{8,10},{9,11},{10,... | collective-permute-start | bytes 245768 | tf_op jit(solution)/shard_map/ppermute | solution.py:326
  7.0 3.1 %collective-permute-done.2 = f32[2,16,640]{2,1,0:T(8,128)S(1)} collective-permute-done((f32[2,16,640]{2,1,0:T(8,128)S(1)}, f32[2,16,640]{2,1,0:T(8,128)S(1)}, u32[]{:S(2)}, u32[]{:S(2)}) %collective-permute-start.2) | collective-permute-done | bytes 81952 | tf_op jit(solution)/shard_map/ppermute | solution.py:326
  10.1 0.1 select_select_fusion
  10.2 1.9 %collective-permute-start.3 = (f32[3,16,640]{2,1,0:T(8,128)S(1)}, f32[3,16,640]{2,1,0:T(8,128)S(1)}, u32[]{:S(2)}, u32[]{:S(2)}) collective-permute-start(f32[3,16,640]{2,1,0:T(8,128)S(1)} %select_select_fusion), channel_id=1, source_target_pairs={{0,4},{1,5},{2,6},{3,7},{4,0},{5,1},{6,2},{7,3},{8,12},{9,13},{10,... | collective-permute-start | bytes 368648 | tf_op jit(solution)/shard_map/ppermute | solution.py:326
  12.1 1.6 %collective-permute-start = (f32[144,640]{1,0:T(8,128)S(1)}, f32[144,640]{1,0:T(8,128)S(1)}, u32[]{:S(2)}, u32[]{:S(2)}) collective-permute-start(f32[144,640]{1,0:T(8,128)S(1)} %pad_maximum_fusion), channel_id=1, source_target_pairs={{0,2},{1,3},{2,0},{3,1},{4,6},{5,7},{6,4},{7,5},{8,10},{9,11},{10,... | collective-permute-start | bytes 1105928 | tf_op jit(solution)/shard_map/ppermute | solution.py:326
  13.7 0.1 add_multiply_fusion.base_ref
  13.7 1.7 %collective-permute-done.3 = f32[3,16,640]{2,1,0:T(8,128)S(1)} collective-permute-done((f32[3,16,640]{2,1,0:T(8,128)S(1)}, f32[3,16,640]{2,1,0:T(8,128)S(1)}, u32[]{:S(2)}, u32[]{:S(2)}) %collective-permute-start.3) | collective-permute-done | bytes 122912 | tf_op jit(solution)/shard_map/ppermute | solution.py:326
  15.4 0.1 broadcast_select_fusion
  15.5 3.7 %collective-permute-start.4 = (f32[3,16,640]{2,1,0:T(8,128)S(1)}, f32[3,16,640]{2,1,0:T(8,128)S(1)}, u32[]{:S(2)}, u32[]{:S(2)}) collective-permute-start(f32[3,16,640]{2,1,0:T(8,128)S(1)} %broadcast_select_fusion), channel_id=1, source_target_pairs={{0,12},{1,13},{2,14},{3,15},{4,8},{5,9},{6,10},{7,11},{8,4},{9,5},... | collective-permute-start | bytes 368648 | tf_op jit(solution)/shard_map/ppermute | solution.py:326
  19.2 0.0 copy-done.1
  19.2 0.1 pad_add_fusion.place_ref
  19.3 2.8 %collective-permute-done = f32[144,640]{1,0:T(8,128)S(1)} collective-permute-done((f32[144,640]{1,0:T(8,128)S(1)}, f32[144,640]{1,0:T(8,128)S(1)}, u32[]{:S(2)}, u32[]{:S(2)}) %collective-permute-start) | collective-permute-done | bytes 368672 | tf_op jit(solution)/shard_map/ppermute | solution.py:326
  22.1 2.8 %shard_map.64 = (f32[4,2,2,5,32,128]{5,4,3,2,1,0:T(8,128)S(1)}, f32[4,4,6,8,128]{4,3,2,1,0:T(8,128)S(1)}, f32[4,8,128]{2,1,0:T(8,128)S(1)}, s32[3,8,128]{2,1,0:T(8,128)S(1)}) custom-call(s32[2]{0:T(128)S(1)} %add_multiply_fusion.base_ref, s32[3]{0:T(128)S(1)} %pad_add_fusion.place_ref, s32[3]{0:T(128)S(1)} %get-tuple-element.18.mismatch_ref, ...), custom_call_target="tpu_custom_call" | custom-call | flops 8192000 | bytes 1966080 | tf_op jit(solution)/shard_map/pallas_call | solution.py:291
  24.9 0.2 compare_reduce_fusion
  25.1 0.0 collective-permute-done.4
  25.1 0.1 broadcast_select_fusion.1
  25.2 0.1 collective-permute-start.5
  25.3 1.3 %collective-permute-done.5 = f32[3,16,640]{2,1,0:T(8,128)S(1)} collective-permute-done((f32[3,16,640]{2,1,0:T(8,128)S(1)}, f32[3,16,640]{2,1,0:T(8,128)S(1)}, u32[]{:S(2)}, u32[]{:S(2)}) %collective-permute-start.5) | collective-permute-done | bytes 122912 | tf_op jit(solution)/shard_map/ppermute | solution.py:326
  26.6 11.6 %shard_map.65 = f32[3,32,640]{2,1,0:T(8,128)S(1)} custom-call(f32[4,2,2,5,32,128]{5,4,3,2,1,0:T(8,128)S(1)} %get-tuple-element.9.field_ref, f32[4,4,6,8,128]{4,3,2,1,0:T(8,128)S(1)} %get-tuple-element.10.taps_ref, f32[4,8,128]{2,1,0:T(8,128)S(1)} %get-tuple-element.11.rate_ref, f32[3,32,640]{2,1,0:T(8,128)S(1)} %maximum_select_fusion.slab_ref), custom_call_target="tpu_custom_call" | custom-call | tf_op jit(solution)/shard_map/pallas_call | solution.py:310
  38.3 0.2 collective-permute-start.6
  38.5 1.2 %collective-permute-done.6 = f32[3,16,512]{2,1,0:T(8,128)S(1)} collective-permute-done((f32[3,16,512]{2,1,0:T(8,128)S(1)}, f32[3,16,512]{2,1,0:T(8,128)S(1)}, u32[]{:S(2)}, u32[]{:S(2)}) %collective-permute-start.6) | collective-permute-done | bytes 98336 | tf_op jit(solution)/shard_map/ppermute | solution.py:326
  39.7 0.5 collective-permute-start.7
  40.2 4.4 %collective-permute-done.7 = f32[3,16,512]{2,1,0:T(8,128)S(1)} collective-permute-done((f32[3,16,512]{2,1,0:T(8,128)S(1)}, f32[3,16,512]{2,1,0:T(8,128)S(1)}, u32[]{:S(2)}, u32[]{:S(2)}) %collective-permute-start.7) | collective-permute-done | bytes 98336 | tf_op jit(solution)/shard_map/ppermute | solution.py:326
  44.6 2.5 %collective-permute-start.8 = (f32[3,16,512]{2,1,0:T(8,128)S(1)}, f32[3,16,512]{2,1,0:T(8,128)S(1)}, u32[]{:S(2)}, u32[]{:S(2)}) collective-permute-start(f32[3,16,512]{2,1,0:T(8,128)S(1)} %add.12), channel_id=1, source_target_pairs={{0,12},{1,13},{2,14},{3,15},{4,8},{5,9},{6,10},{7,11},{8,4},{9,5},... | collective-permute-start | bytes 294920 | tf_op jit(solution)/shard_map/ppermute | solution.py:326
  47.1 4.0 %collective-permute-done.8 = f32[3,16,512]{2,1,0:T(8,128)S(1)} collective-permute-done((f32[3,16,512]{2,1,0:T(8,128)S(1)}, f32[3,16,512]{2,1,0:T(8,128)S(1)}, u32[]{:S(2)}, u32[]{:S(2)}) %collective-permute-start.8) | collective-permute-done | bytes 98336 | tf_op jit(solution)/shard_map/ppermute | solution.py:326
  51.2 0.1 select_reduce_fusion.3
  51.3 1.6 %collective-permute-start.9 = (f32[2,16,512]{2,1,0:T(8,128)S(1)}, f32[2,16,512]{2,1,0:T(8,128)S(1)}, u32[]{:S(2)}, u32[]{:S(2)}) collective-permute-start(f32[2,16,512]{2,1,0:T(8,128)S(1)} %pad_maximum_fusion.2), channel_id=1, source_target_pairs={{0,2},{1,3},{2,0},{3,1},{4,6},{5,7},{6,4},{7,5},{8,10},{9,11},{10,... | collective-permute-start | bytes 196616 | tf_op jit(solution)/shard_map/ppermute | solution.py:326
  52.9 2.7 %collective-permute-done.9 = f32[2,16,512]{2,1,0:T(8,128)S(1)} collective-permute-done((f32[2,16,512]{2,1,0:T(8,128)S(1)}, f32[2,16,512]{2,1,0:T(8,128)S(1)}, u32[]{:S(2)}, u32[]{:S(2)}) %collective-permute-start.9) | collective-permute-done | bytes 65568 | tf_op jit(solution)/shard_map/ppermute | solution.py:326
  55.7 0.1 collective-permute-start.10
  55.7 1.2 %collective-permute-done.10 = f32[16,1024]{1,0:T(8,128)S(1)} collective-permute-done((f32[16,1024]{1,0:T(8,128)S(1)}, f32[16,1024]{1,0:T(8,128)S(1)}, u32[]{:S(2)}, u32[]{:S(2)}) %collective-permute-start.10) | collective-permute-done | bytes 65568 | tf_op jit(solution)/shard_map/ppermute | solution.py:326
  57.0 0.7 %maximum_select_fusion.2 = f32[1,32,1024]{2,1,0:T(8,128)} fusion(f32[1,16,1024]{2,1,0:T(8,128)S(1)} %get-tuple-element.22, f32[1,16,1024]{2,1,0:T(8,128)S(1)} %bitcast.37, pred[]{:T(512)S(6)} %ne.4), kind=kLoop, calls=%fused_computation.8 | loop fusion | flops 98304 | bytes 262145 | tf_op jit(solution)/shard_map/jit(_where)/select_n | solution.py:354
  (18 shorter events, 0.3 us)
Async XLA Ops:
  0.0 4.3 %copy-start = (s32[3]{0:T(128)S(1)}, s32[3]{0:T(128)}, u32[]{:S(2)}) copy-start(s32[3]{0:T(128)} %param.10) | copy-start | bytes 40
  0.0 4.3 %collective-permute-start.1 = (f32[32,1024]{1,0:T(8,128)}, f32[32,1024]{1,0:T(8,128)S(1)}, u32[]{:S(2)}, u32[]{:S(2)}) collective-permute-start(f32[32,1024]{1,0:T(8,128)} %bitcast.32), channel_id=1, source_target_pairs={{0,1},{1,0},{2,3},{3,2},{4,5},{5,4},{6,7},{7,6},{8,9},{9,8},{10,11... | collective-permute-start | bytes 393224 | tf_op jit(solution)/shard_map/ppermute | solution.py:326
  4.3 14.9 %copy-start.1 = (s32[2]{0:T(128)S(1)}, s32[2]{0:T(128)}, u32[]{:S(2)}) copy-start(s32[2]{0:T(128)} %param.11) | copy-start | bytes 28
  4.4 5.7 %collective-permute-start.2 = (f32[2,16,640]{2,1,0:T(8,128)S(1)}, f32[2,16,640]{2,1,0:T(8,128)S(1)}, u32[]{:S(2)}, u32[]{:S(2)}) collective-permute-start(f32[2,16,640]{2,1,0:T(8,128)S(1)} %get-tuple-element.23), channel_id=1, source_target_pairs={{0,2},{1,3},{2,0},{3,1},{4,6},{5,7},{6,4},{7,5},{8,10},{9,11},{10,... | collective-permute-start | bytes 245768 | tf_op jit(solution)/shard_map/ppermute | solution.py:326
  10.2 5.2 %collective-permute-start.3 = (f32[3,16,640]{2,1,0:T(8,128)S(1)}, f32[3,16,640]{2,1,0:T(8,128)S(1)}, u32[]{:S(2)}, u32[]{:S(2)}) collective-permute-start(f32[3,16,640]{2,1,0:T(8,128)S(1)} %select_select_fusion), channel_id=1, source_target_pairs={{0,4},{1,5},{2,6},{3,7},{4,0},{5,1},{6,2},{7,3},{8,12},{9,13},{10,... | collective-permute-start | bytes 368648 | tf_op jit(solution)/shard_map/ppermute | solution.py:326
  12.1 10.0 %collective-permute-start = (f32[144,640]{1,0:T(8,128)S(1)}, f32[144,640]{1,0:T(8,128)S(1)}, u32[]{:S(2)}, u32[]{:S(2)}) collective-permute-start(f32[144,640]{1,0:T(8,128)S(1)} %pad_maximum_fusion), channel_id=1, source_target_pairs={{0,2},{1,3},{2,0},{3,1},{4,6},{5,7},{6,4},{7,5},{8,10},{9,11},{10,... | collective-permute-start | bytes 1105928 | tf_op jit(solution)/shard_map/ppermute | solution.py:326
  15.5 9.6 %collective-permute-start.4 = (f32[3,16,640]{2,1,0:T(8,128)S(1)}, f32[3,16,640]{2,1,0:T(8,128)S(1)}, u32[]{:S(2)}, u32[]{:S(2)}) collective-permute-start(f32[3,16,640]{2,1,0:T(8,128)S(1)} %broadcast_select_fusion), channel_id=1, source_target_pairs={{0,12},{1,13},{2,14},{3,15},{4,8},{5,9},{6,10},{7,11},{8,4},{9,5},... | collective-permute-start | bytes 368648 | tf_op jit(solution)/shard_map/ppermute | solution.py:326
  25.2 1.4 %collective-permute-start.5 = (f32[3,16,640]{2,1,0:T(8,128)S(1)}, f32[3,16,640]{2,1,0:T(8,128)S(1)}, u32[]{:S(2)}, u32[]{:S(2)}) collective-permute-start(f32[3,16,640]{2,1,0:T(8,128)S(1)} %broadcast_select_fusion.1), channel_id=1, source_target_pairs={{0,1},{1,0},{2,3},{3,2},{4,5},{5,4},{6,7},{7,6},{8,9},{9,8},{10,11... | collective-permute-start | bytes 368648 | tf_op jit(solution)/shard_map/ppermute | solution.py:326
  38.3 1.4 %collective-permute-start.6 = (f32[3,16,512]{2,1,0:T(8,128)S(1)}, f32[3,16,512]{2,1,0:T(8,128)S(1)}, u32[]{:S(2)}, u32[]{:S(2)}) collective-permute-start(f32[3,16,512]{2,1,0:T(8,128)S(1)} %slice_select_fusion.3), channel_id=1, source_target_pairs={{0,1},{1,0},{2,3},{3,2},{4,5},{5,4},{6,7},{7,6},{8,9},{9,8},{10,11... | collective-permute-start | bytes 294920 | tf_op jit(solution)/shard_map/ppermute | solution.py:326
  39.7 4.9 %collective-permute-start.7 = (f32[3,16,512]{2,1,0:T(8,128)S(1)}, f32[3,16,512]{2,1,0:T(8,128)S(1)}, u32[]{:S(2)}, u32[]{:S(2)}) collective-permute-start(f32[3,16,512]{2,1,0:T(8,128)S(1)} %select_add_fusion), channel_id=1, source_target_pairs={{0,4},{1,5},{2,6},{3,7},{4,0},{5,1},{6,2},{7,3},{8,12},{9,13},{10,... | collective-permute-start | bytes 294920 | tf_op jit(solution)/shard_map/ppermute | solution.py:326
  44.6 6.6 %collective-permute-start.8 = (f32[3,16,512]{2,1,0:T(8,128)S(1)}, f32[3,16,512]{2,1,0:T(8,128)S(1)}, u32[]{:S(2)}, u32[]{:S(2)}) collective-permute-start(f32[3,16,512]{2,1,0:T(8,128)S(1)} %add.12), channel_id=1, source_target_pairs={{0,12},{1,13},{2,14},{3,15},{4,8},{5,9},{6,10},{7,11},{8,4},{9,5},... | collective-permute-start | bytes 294920 | tf_op jit(solution)/shard_map/ppermute | solution.py:326
  51.3 4.3 %collective-permute-start.9 = (f32[2,16,512]{2,1,0:T(8,128)S(1)}, f32[2,16,512]{2,1,0:T(8,128)S(1)}, u32[]{:S(2)}, u32[]{:S(2)}) collective-permute-start(f32[2,16,512]{2,1,0:T(8,128)S(1)} %pad_maximum_fusion.2), channel_id=1, source_target_pairs={{0,2},{1,3},{2,0},{3,1},{4,6},{5,7},{6,4},{7,5},{8,10},{9,11},{10,... | collective-permute-start | bytes 196616 | tf_op jit(solution)/shard_map/ppermute | solution.py:326
  55.7 1.3 %collective-permute-start.10 = (f32[16,1024]{1,0:T(8,128)S(1)}, f32[16,1024]{1,0:T(8,128)S(1)}, u32[]{:S(2)}, u32[]{:S(2)}) collective-permute-start(f32[16,1024]{1,0:T(8,128)S(1)} %get-tuple-element.21), channel_id=1, source_target_pairs={{0,1},{1,0},{2,3},{3,2},{4,5},{5,4},{6,7},{7,6},{8,9},{9,8},{10,11... | collective-permute-start | bytes 196616 | tf_op jit(solution)/shard_map/ppermute | solution.py:326

commit v4 on v3

--- a/solution.py
+++ b/solution.py
@@ -14,6 +14,8 @@
 LANES = 128
 SUB = 8
 REACH = 2
+NEAR_ROWS = 1
+NEAR_COLUMNS = 2
 TWO_OVER_PI = 2.0 / math.pi
 PI_2 = (1.5703125, 4.837512969970703125e-4, 7.54978995489188216e-8)
 
@@ -76,84 +78,146 @@
     return ref.at[f, field, part, block, pl.ds(SUB * group + shift, SUB), :]
 
 
-def prepare_kernel(
-    freq_total,
-    base_ref,
-    place_ref,
-    mismatch_ref,
-    own_ref,
-    own_scalars_ref,
-    near_ref,
-    near_scalars_ref,
-    field_ref,
-    taps_out_ref,
-    rate_ref,
-    turn_ref,
-):
-    freq_local, _, height, breadth = own_ref.shape
-    blocks = breadth // LANES
+def spread_turn(owner_ref, turn_ref):
+    for t in range(owner_ref.shape[0]):
+        turn_ref[t] = jnp.full((SUB, LANES), owner_ref[t] ^ lax.axis_index("freq"), jnp.int32)
+
+
+def pack_kernel(owner_ref, taps_ref, spectrum_ref, receiver_ref, slab_ref, out_ref, turn_ref):
+    spread_turn(owner_ref, turn_ref)
+    freq_local, _, height, breadth = receiver_ref.shape
+    width = out_ref.shape[1]
+    start = jnp.where((lax.axis_index("freq") & NEAR_COLUMNS) != 0, 0, breadth - width)
+    row = 0
+    for f in range(freq_local):
+        for part in range(2):
+            for b in range(width // LANES):
+                column = pl.ds(pl.multiple_of(start + LANES * b, LANES), LANES)
+                out_ref[row : row + height, LANES * b : LANES * (b + 1)] = receiver_ref[f, part, :, column]
+            row += height
+    scalars = [
+        taps_ref[f, d, i] for f in range(freq_local) for d in range(len(directions)) for i in range(6)
+    ] + [spectrum_ref[f, i] for f in range(freq_local) for i in range(2)]
+    lane = columns()
+    for b in range(width // LANES):
+        value = jnp.zeros((SUB, LANES), jnp.float32)
+        for i, scalar in enumerate(scalars[LANES * b : LANES * (b + 1)]):
+            value = jnp.where(lane == i, scalar, value)
+        out_ref[row : row + SUB, LANES * b : LANES * (b + 1)] = value
+
+
+def prepare(freq_total, rank, first_column, owner_ref, position_ref, block_of, taps_of, wave_of, results):
+    field_ref, taps_out_ref, rate_ref, turn_ref = results
+    freq_local, _, _, blocks, height, _ = field_ref.shape
     groups = height // SUB
     lane = columns()
     row = lax.broadcasted_iota(jnp.int32, (SUB, LANES), 0)
-    taps_count = len(directions) * 6
-
-    def scalar(ref, i):
-        at = LANES * (i % blocks)
-        return jnp.broadcast_to(ref[i // blocks : i // blocks + 1, at : at + LANES], (SUB, LANES))
-
-    def number(side, f):
-        return (base_ref[side] + f).astype(jnp.float32) + 1.0
-
-    both = ((own_ref, own_scalars_ref), (near_ref, near_scalars_ref))
-    for side, (receiver_ref, scalars_ref) in enumerate(both):
-        for f in range(freq_local):
-            for d in range(len(directions)):
-                for i in range(6):
-                    taps_out_ref[side * freq_local + f, d, i] = scalar(scalars_ref, f * taps_count + d * 6 + i)
-            rate_ref[side * freq_local + f] = jnp.full(
-                (SUB, LANES), number(side, f) * (lens_rate / freq_total), jnp.float32
-            )
-
-        @pl.loop(0, freq_local)
-        def _(f):
-            for part in range(2):
-                for g in range(groups):
-                    loaded = [
-                        receiver_ref[f, part, SUB * g : SUB * (g + 1), LANES * b : LANES * (b + 1)]
-                        for b in range(blocks)
-                    ]
-                    for b, value in enumerate(interleave(loaded)):
-                        at = tile(field_ref, side * freq_local + f, 1, part, b, g)
-                        at[...] = -value if part else value
-
-    for t in range(mismatch_ref.shape[0]):
-        turn_ref[t] = jnp.full((SUB, LANES), mismatch_ref[t], jnp.int32)
-
-    src_row = place_ref[0].astype(jnp.float32)
-    src_col = place_ref[1].astype(jnp.float32)
-    first_col = place_ref[2]
+
+    def number(f):
+        return (rank * freq_local + f).astype(jnp.float32) + 1.0
+
+    for f in range(freq_local):
+        for d in range(len(directions)):
+            for i in range(6):
+                taps_out_ref[f, d, i] = jnp.broadcast_to(taps_of(f, d, i), (SUB, LANES))
+        rate_ref[f] = jnp.full((SUB, LANES), number(f) * (lens_rate / freq_total), jnp.float32)
+    spread_turn(owner_ref, turn_ref)
+
+    @pl.loop(0, freq_local)
+    def _(f):
+        for part in range(2):
+            for g in range(groups):
+                loaded = [block_of(f, part, g, b) for b in range(blocks)]
+                for b, value in enumerate(interleave(loaded)):
+                    tile(field_ref, f, 1, part, b, g)[...] = -value if part else value
+
+    src_row = position_ref[0].astype(jnp.float32)
+    src_col = position_ref[1].astype(jnp.float32)
+    waves = [(wave_of(f, 0), wave_of(f, 1)) for f in range(freq_local)]
     for g in range(groups):
         for b in range(blocks):
             d_row = (row + SUB * g).astype(jnp.float32) - src_row
-            d_col = (lane * blocks + (first_col + b)).astype(jnp.float32) - src_col
+            d_col = (lane * blocks + (first_column + b)).astype(jnp.float32) - src_col
             distance = jnp.sqrt(d_row * d_row + d_col * d_col + 1.0)
             amplitude = 1.0 / (1.0 + distance / (height / 4.0))
-            for side, (_, scalars_ref) in enumerate(both):
-                for f in range(freq_local):
-                    cos_value, sin_value = cos_sin(number(side, f) * (wave_rate / freq_total) * distance)
-                    base_re = amplitude * cos_value
-                    base_im = -amplitude * sin_value
-                    w_re = scalar(scalars_ref, freq_local * taps_count + 2 * f)
-                    w_im = scalar(scalars_ref, freq_local * taps_count + 2 * f + 1)
-                    at = side * freq_local + f
-                    tile(field_ref, at, 0, 0, b, g)[...] = w_re * base_re - w_im * base_im
-                    tile(field_ref, at, 0, 1, b, g)[...] = w_re * base_im + w_im * base_re
+            for f, (w_re, w_im) in enumerate(waves):
+                cos_value, sin_value = cos_sin(number(f) * (wave_rate / freq_total) * distance)
+                base_re = amplitude * cos_value
+                base_im = -amplitude * sin_value
+                tile(field_ref, f, 0, 0, b, g)[...] = w_re * base_re - w_im * base_im
+                tile(field_ref, f, 0, 1, b, g)[...] = w_re * base_im + w_im * base_re
+
+
+def prepare_own_kernel(
+    freq_total, owner_ref, position_ref, taps_ref, spectrum_ref, receiver_ref, *results
+):
+    blocks = results[0].shape[3]
+    here = lax.axis_index("freq")
+    first_column = jnp.where((here & NEAR_COLUMNS) != 0, receiver_ref.shape[3] - blocks * LANES, 0)
+
+    def block_of(f, part, g, b):
+        column = pl.ds(pl.multiple_of(first_column + LANES * b, LANES), LANES)
+        return receiver_ref[f, part, SUB * g : SUB * (g + 1), column]
+
+    prepare(
+        freq_total,
+        here,
+        first_column,
+        owner_ref,
+        position_ref,
+        block_of,
+        lambda f, d, i: taps_ref[f, d, i],
+        lambda f, i: spectrum_ref[f, i],
+        results,
+    )
+
+
+def prepare_near_kernel(freq_total, breadth, owner_ref, position_ref, packed_ref, *results):
+    freq_local, _, _, blocks, height, _ = results[0].shape
+    here = lax.axis_index("freq")
+    first_column = jnp.where((here & NEAR_COLUMNS) != 0, breadth - blocks * LANES, 0)
+    rows = freq_local * 2 * height
+    taps_count = len(directions) * 6
+
+    def block_of(f, part, g, b):
+        row = pl.multiple_of((2 * f + part) * height + SUB * g, SUB)
+        return packed_ref[pl.ds(row, SUB), LANES * b : LANES * (b + 1)]
+
+    def scalar(i):
+        return jnp.broadcast_to(packed_ref[rows : rows + SUB, i : i + 1], (SUB, LANES))
+
+    prepare(
+        freq_total,
+        here ^ NEAR_COLUMNS,
+        first_column,
+        owner_ref,
+        position_ref,
+        block_of,
+        lambda f, d, i: scalar(f * taps_count + 6 * d + i),
+        lambda f, i: scalar(freq_local * taps_count + 2 * f + i),
+        results,
+    )
 
 
 def migrate_kernel(
-    freq_total, field_ref, taps_ref, rate_ref, slab_ref, out_ref, a_ref, b_ref, v_ref, c_ref
+    freq_total,
+    own_ref,
+    own_taps_ref,
+    own_rate_ref,
+    near_ref,
+    near_taps_ref,
+    near_rate_ref,
+    slab_ref,
+    out_ref,
+    a_ref,
+    b_ref,
+    v_ref,
+    c_ref,
+    taps_ref,
+    rate_ref,
 ):
-    freq_local = field_ref.shape[0]
+    freq_own = own_ref.shape[0]
+    freq_local = 2 * freq_own
     levels, height, breadth = slab_ref.shape
     blocks = breadth // LANES
     groups = height // SUB
@@ -166,6 +230,15 @@
 
     def store(ref, f, field, part, block, group, value):
         tile(ref, f, field, part, block + REACH, group + 1)[...] = value
+
+    for side, (one_taps_ref, one_rate_ref) in enumerate(
+        ((own_taps_ref, own_rate_ref), (near_taps_ref, near_rate_ref))
+    ):
+        for f in range(freq_own):
+            rate_ref[side * freq_own + f] = one_rate_ref[f]
+            for d in range(len(directions)):
+                for i in range(6):
+                    taps_ref[side * freq_own + f, d, i] = one_taps_ref[f, d, i]
 
     zero = jnp.zeros((SUB, LANES), jnp.float32)
 
@@ -200,8 +273,8 @@
     for g in range(groups):
         take_slab(0, g)
 
-    def lens(t, get):
-        @pl.loop(0, freq_local)
+    def lens(t, get, first, count):
+        @pl.loop(first, first + count)
         def _(f):
             rate = rate_ref[f]
             for g in range(groups):
@@ -266,13 +339,19 @@
         sweep(a_ref, b_ref, 2)
         last_sweep(b_ref, a_ref, 3, t)
 
-    lens(0, lambda f, field, part, b, g: tile(field_ref, f, field, part, b, g)[...])
+    for side, ref in enumerate((own_ref, near_ref)):
+        first = side * freq_own
+
+        def surface(f, field, part, b, g, ref=ref, first=first):
+            return tile(ref, f - first, field, part, b, g)[...]
+
+        lens(0, surface, first, freq_own)
 
     @pl.loop(0, levels)
     def _(t):
         @pl.when(t > 0)
         def _():
-            lens(t, lambda f, field, part, b, g: load(a_ref, f, field, part, b, g))
+            lens(t, lambda f, field, part, b, g: load(a_ref, f, field, part, b, g), 0, freq_local)
 
         depth_step(t)
 
@@ -284,50 +363,64 @@
 VMEM = pl.BlockSpec(memory_space=pltpu.VMEM)
 
 
-def prepare(own, own_scalars, near, near_scalars, place, mismatch, base, freq_total):
-    freq_local, _, height, breadth = own.shape
-    blocks = breadth // LANES
-    cells = 2 * freq_local * height * breadth
+def pack(owners, taps, spectrum, receiver, slab, width):
+    freq_local, _, height, _ = receiver.shape
+    rows = freq_local * 2 * height + SUB
     return pl.pallas_call(
-        functools.partial(prepare_kernel, freq_total),
+        pack_kernel,
         out_shape=(
-            jax.ShapeDtypeStruct((2 * freq_local, 2, 2, blocks, height, LANES), jnp.float32),
-            jax.ShapeDtypeStruct((2 * freq_local, len(directions), 6, SUB, LANES), jnp.float32),
-            jax.ShapeDtypeStruct((2 * freq_local, SUB, LANES), jnp.float32),
-            jax.ShapeDtypeStruct((mismatch.shape[0], SUB, LANES), jnp.int32),
+            jax.ShapeDtypeStruct((rows, width), jnp.float32),
+            jax.ShapeDtypeStruct((owners.shape[0], SUB, LANES), jnp.int32),
         ),
-        in_specs=[SMEM, SMEM, SMEM, VMEM, VMEM, VMEM, VMEM],
+        in_specs=[SMEM, SMEM, SMEM, VMEM, pl.BlockSpec(memory_space=pl.ANY)],
+        out_specs=(VMEM, VMEM),
+        cost_estimate=pl.CostEstimate(flops=0, bytes_accessed=8 * rows * width, transcendentals=0),
+        compiler_params=pltpu.CompilerParams(vmem_limit_bytes=32 * 1024 * 1024),
+    )(owners, taps, spectrum, receiver, slab)
+
+
+def prepared(kernel, shape, levels, width, specs, operands):
+    freq_local, _, height, _ = shape
+    cells = freq_local * height * width
+    return pl.pallas_call(
+        kernel,
+        out_shape=(
+            jax.ShapeDtypeStruct((freq_local, 2, 2, width // LANES, height, LANES), jnp.float32),
+            jax.ShapeDtypeStruct((freq_local, len(directions), 6, SUB, LANES), jnp.float32),
+            jax.ShapeDtypeStruct((freq_local, SUB, LANES), jnp.float32),
+            jax.ShapeDtypeStruct((levels, SUB, LANES), jnp.int32),
+        ),
+        in_specs=specs,
         out_specs=(VMEM, VMEM, VMEM, VMEM),
         cost_estimate=pl.CostEstimate(flops=100 * cells, bytes_accessed=24 * cells, transcendentals=0),
         compiler_params=pltpu.CompilerParams(vmem_limit_bytes=32 * 1024 * 1024),
-    )(base, place, mismatch, own, own_scalars, near, near_scalars)
-
-
-def migrate(field, taps, rate, slabs, freq_total):
-    freq_local, _, _, blocks, height, _ = field.shape
+    )(*operands)
+
+
+def migrate(own, near, slabs, freq_total):
+    freq_own, _, _, blocks, height, _ = own[0].shape
+    freq_local = 2 * freq_own
     levels = slabs.shape[0]
     state = pltpu.VMEM((freq_local, 2, 2, blocks + 2 * REACH, height + 2 * SUB, LANES), jnp.float32)
     return pl.pallas_call(
         functools.partial(migrate_kernel, freq_total),
         out_shape=jax.ShapeDtypeStruct(slabs.shape, jnp.float32),
-        in_specs=[VMEM, VMEM, VMEM, VMEM],
+        in_specs=[VMEM] * 7,
         out_specs=VMEM,
         scratch_shapes=[
             state,
             state,
             pltpu.VMEM((levels, blocks, height, LANES), jnp.float32),
             pltpu.VMEM((levels, blocks, height, LANES), jnp.float32),
+            pltpu.VMEM((freq_local, len(directions), 6, SUB, LANES), jnp.float32),
+            pltpu.VMEM((freq_local, SUB, LANES), jnp.float32),
         ],
         compiler_params=pltpu.CompilerParams(vmem_limit_bytes=32 * 1024 * 1024),
-    )(field, taps, rate, slabs)
+    )(*own, *near, slabs)
 
 
 def exchange(value, mask, size):
     return lax.ppermute(value, "freq", [(i, i ^ mask) for i in range(size)])
-
-
-NEAR_ROWS = 1
-NEAR_COLUMNS = 2
 
 
 def far_bits(size):
@@ -356,23 +449,23 @@
     )
 
 
-def fetch_slabs(own, mismatch, turn, rank, size, width):
+def fetch_slabs(own, got, turns, rank, size, width):
     upper_rows = (rank & NEAR_ROWS) != 0
     upper_columns = (rank & NEAR_COLUMNS) != 0
-    got, _ = rows_split(exchange(own, NEAR_ROWS, size), upper_rows)
     mine, _ = rows_split(own, upper_rows)
+    got, _ = rows_split(got, upper_rows)
     held = jnp.stack([mine, got])
     mine, other = columns_split(held, upper_columns, width)
     held = jnp.concatenate([mine, exchange(other, NEAR_COLUMNS, size)], axis=0)
-    wanted = mismatch & (NEAR_ROWS | NEAR_COLUMNS)
-    carried = jnp.broadcast_to(held[:1], (mismatch.shape[0], *held.shape[1:]))
+    wanted = turns[0][:, :1, :1] & (NEAR_ROWS | NEAR_COLUMNS)
+    carried = jnp.broadcast_to(held[:1], (wanted.shape[0], *held.shape[1:]))
     for c in range(1, held.shape[0]):
-        carried = jnp.where((wanted == c)[:, None, None], held[c][None], carried)
+        carried = jnp.where(wanted == c, held[c][None], carried)
     far = far_bits(size)
-    for bit, mask in far:
+    for i, (bit, mask) in enumerate(far):
         got = exchange(carried, mask, size)
-        keep = (mismatch & bit)[:, None, None] if bit != far[-1][0] else turn[:, :1, :1] & bit
-        carried = jnp.where(keep == 0, carried, got)
+        turn = turns[2 if i == len(far) - 1 else 1][:, :1, :1]
+        carried = jnp.where((turn & bit) == 0, carried, got)
     return joined(carried, exchange(carried, NEAR_ROWS, size), upper_rows, -2)
 
 
@@ -403,26 +496,32 @@
     half = breadth // 2
     border = REACH * sum(1 for _, step_y in directions if step_y) * levels
     width = -(-(half + border) // LANES) * LANES
-    upper_columns = (rank & NEAR_COLUMNS) != 0
-
-    scalars = jnp.concatenate([filter_taps.reshape(-1), source_spectrum.reshape(-1)])
-    scalar_rows = -(-scalars.shape[0] * LANES // (width * SUB)) * SUB
-    scalars = jnp.pad(scalars, (0, scalar_rows * width // LANES - scalars.shape[0]))
-    scalars = jnp.repeat(scalars, LANES).reshape(scalar_rows, width)
-    own, sent = columns_split(receiver_data, upper_columns, width)
-    sent = jnp.concatenate([sent.reshape(-1, width), scalars], axis=0)
-    near = exchange(sent, NEAR_COLUMNS, size)
-    near, near_scalars = near[:-scalar_rows].reshape(own.shape), near[-scalar_rows:]
-
-    mismatch = depth_owner ^ rank
-    first_column = jnp.where(upper_columns, breadth - width, 0).astype(jnp.int32).reshape(1)
-    place = jnp.concatenate([source_position, first_column])
-    base = (jnp.stack([rank, rank ^ NEAR_COLUMNS]) * freq_local).astype(jnp.int32)
-    field, taps, rate, turn = prepare(
-        own, scalars, near, near_scalars, place, mismatch, base, freq_total
-    )
-    slabs = fetch_slabs(slowness[0], mismatch, turn, rank, size, width)
-    partial = migrate(field, taps, rate, slabs, freq_total)
+    shape = receiver_data.shape
+
+    near_slab = exchange(slowness[0], NEAR_ROWS, size)
+    packed, pack_turn = pack(
+        depth_owner, filter_taps, source_spectrum, receiver_data, near_slab, width
+    )
+    packed = exchange(packed, NEAR_COLUMNS, size)
+    *own, own_turn = prepared(
+        functools.partial(prepare_own_kernel, freq_total),
+        shape,
+        levels,
+        width,
+        [SMEM, SMEM, SMEM, SMEM, VMEM],
+        (depth_owner, source_position, filter_taps, source_spectrum, receiver_data),
+    )
+    *near, near_turn = prepared(
+        functools.partial(prepare_near_kernel, freq_total, breadth),
+        shape,
+        levels,
+        width,
+        [SMEM, SMEM, VMEM],
+        (depth_owner, source_position, packed),
+    )
+    turns = (pack_turn, own_turn, near_turn)
+    slabs = fetch_slabs(slowness[0], near_slab, turns, rank, size, width)
+    partial = migrate(own, near, slabs, freq_total)
     return sums_to_owner(partial, depth_owner, rank, size, half)[None]
 
 

time: 57.9 us -> 55 us (0.950)
  waiting for transfers between devices: 22.5 us -> 20.3 us
  local copies, waits for them, and re-layouts: 1.77 us -> 0.05 us
  Pallas kernels: 14.4 us -> 15.8 us
  other arithmetic: 3.6 us -> 2.62 us
  starting transfers between devices: 15.2 us -> 15.9 us
    ppermute x11, waiting for transfers between devices: 22.5 us -> 20.3 us  [exchange(): return lax.ppermute(value, 'freq', [(i, i ^ mask) for i in range(size)])]
    reshape x2 -> x0, local copies, waits for them, and re-layouts: 1.53 us -> none  [the longest x1 0.77 us: local(): filter_taps.reshape(-1)]
    pallas_call x1 -> x3, Pallas kernels: 2.83 us -> 4.32 us  [the longest x2 3.63 us: prepared(): pl.pallas_call(kernel, out_shape=(jax.ShapeDtypeStruct((freq_local, 2, 2,...]
    select_n x3 -> x2, other arithmetic: 1.16 us -> 0.03 us  [columns_split(): return (jnp.where(upper, high, low), jnp.where(upper, low, high))]
    ppermute x11, starting transfers between devices: 15.2 us -> 15.9 us  [exchange(): return lax.ppermute(value, 'freq', [(i, i ^ mask) for i in range(size)])]
  transfers between devices with their start and end apart: 11 -> 11, of which waited for: 9 -> 9; matrix products, arithmetic and copies ran while one was open for 7% -> 3% of each run, Pallas kernels for 5% -> 8%
where the time goes in v4:
time: 55 us; the launch traced here: 54.8 us
  waiting for transfers between devices  20.3 us (37%)
  starting transfers between devices  15.9 us (29%)
  Pallas kernels  15.8 us (29%)
  other arithmetic  2.62 us (5%)
    ppermute x11, waiting for transfers between devices, exchange(): return lax.ppermute(value, 'freq', [(i, i ^ mask) for i in range(size)])  20.3 us
    ppermute x11, starting transfers between devices, exchange(): return lax.ppermute(value, 'freq', [(i, i ^ mask) for i in range(size)])  15.9 us
    pallas_call x1, Pallas kernels, migrate(): pl.pallas_call(functools.partial(migrate_kernel, freq_total), out_shape=j...  11.5 us
    pallas_call x2, Pallas kernels, prepared(): pl.pallas_call(kernel, out_shape=(jax.ShapeDtypeStruct((freq_local, 2, 2,...  3.63 us
  transfers between devices with their start and end apart: 11, of which 9 were waited for; matrix products, arithmetic and copies ran while one was open for 3% of the time, Pallas kernels for 8%

profile of v4, /device:TPU:0, one launch (start us, length us, event | category | flops | bytes accessed | tf_op | source)
XLA Modules:
  0.0 54.8 jit_solution(8985494418897375101)
XLA Ops:
  0.0 0.0 copy-start
  0.0 0.5 collective-permute-start
  0.5 0.9 %slice_select_fusion.3 = f32[1,16,1024]{2,1,0:T(8,128)S(1)} fusion(f32[1,32,1024]{2,1,0:T(8,128)} %param.9, pred[]{:T(512)S(6)} %ne.8), kind=kLoop, calls=%fused_computation.19 | loop fusion | flops 16384 | bytes 196609 | tf_op jit(solution)/shard_map/jit(_where)/select_n | solution.py:438
  1.3 0.3 collective-permute-done.slab_ref
  1.7 0.0 copy-start.1
  1.7 0.0 copy-start.2
  1.7 0.0 copy-start.3
  1.7 2.9 %collective-permute-start.2 = (f32[2,16,640]{2,1,0:T(8,128)S(1)}, f32[2,16,640]{2,1,0:T(8,128)S(1)}, u32[]{:S(2)}, u32[]{:S(2)}) collective-permute-start(f32[2,16,640]{2,1,0:T(8,128)S(1)} %get-tuple-element.34), channel_id=1, source_target_pairs={{0,2},{1,3},{2,0},{3,1},{4,6},{5,7},{6,4},{7,5},{8,10},{9,11},{10,... | collective-permute-start | bytes 245768 | tf_op jit(solution)/shard_map/ppermute | solution.py:423
  4.7 0.0 copy-done
  4.7 0.0 copy-done.1
  4.7 0.0 copy-done.2
  4.7 0.0 copy-done.3
  4.7 0.7 %shard_map.65 = (f32[136,640]{1,0:T(8,128)S(1)}, s32[3,8,128]{2,1,0:T(8,128)S(1)}) custom-call(s32[3]{0:T(128)S(1)} %copy-done.2, f32[2,4,6]{2,1,0:T(4,128)S(1)} %copy-done.1, f32[2,2]{1,0:T(2,128)S(1)} %copy-done.3, f32[2,2,32,1024]{3,2,1,0:T(8,128)S(1)} %copy-done, f32[32,1024]{1,0:T(8,128)S(1)} %collective-permute-done.slab_ref), custom_call_target="tpu_custom_call" | custom-call | bytes 696320 | tf_op jit(solution)/shard_map/pallas_call | solution.py:369
  5.4 0.3 compare_reduce_fusion.2
  5.7 1.8 %collective-permute-done.2 = f32[2,16,640]{2,1,0:T(8,128)S(1)} collective-permute-done((f32[2,16,640]{2,1,0:T(8,128)S(1)}, f32[2,16,640]{2,1,0:T(8,128)S(1)}, u32[]{:S(2)}, u32[]{:S(2)}) %collective-permute-start.2) | collective-permute-done | bytes 81952 | tf_op jit(solution)/shard_map/ppermute | solution.py:423
  7.4 0.0 copy-start.4
  7.5 0.1 select_select_fusion
  7.5 1.9 %collective-permute-start.3 = (f32[3,16,640]{2,1,0:T(8,128)S(1)}, f32[3,16,640]{2,1,0:T(8,128)S(1)}, u32[]{:S(2)}, u32[]{:S(2)}) collective-permute-start(f32[3,16,640]{2,1,0:T(8,128)S(1)} %select_select_fusion), channel_id=1, source_target_pairs={{0,4},{1,5},{2,6},{3,7},{4,0},{5,1},{6,2},{7,3},{8,12},{9,13},{10,... | collective-permute-start | bytes 368648 | tf_op jit(solution)/shard_map/ppermute | solution.py:423
  9.4 0.0 copy-done.4
  9.4 1.8 %shard_map.64 = (f32[2,2,2,5,32,128]{5,4,3,2,1,0:T(8,128)S(1)}, f32[2,4,6,8,128]{4,3,2,1,0:T(8,128)S(1)}, f32[2,8,128]{2,1,0:T(8,128)S(1)}, s32[3,8,128]{2,1,0:T(8,128)S(1)}) custom-call(s32[3]{0:T(128)S(1)} %copy-done.2, s32[2]{0:T(128)S(1)} %copy-done.4, f32[2,4,6]{2,1,0:T(4,128)S(1)} %copy-done.1, f32[2,2]{1,0:T(2,128)S(1)} %copy-done.3, ...), custom_call_target="tpu_custom_call" | custom-call | flops 4096000 | bytes 983040 | tf_op jit(solution)/shard_map/pallas_call | solution.py:385
  11.2 1.6 %collective-permute-start.1 = (f32[136,640]{1,0:T(8,128)S(1)}, f32[136,640]{1,0:T(8,128)S(1)}, u32[]{:S(2)}, u32[]{:S(2)}) collective-permute-start(f32[136,640]{1,0:T(8,128)S(1)} %get-tuple-element.18), channel_id=1, source_target_pairs={{0,2},{1,3},{2,0},{3,1},{4,6},{5,7},{6,4},{7,5},{8,10},{9,11},{10,... | collective-permute-start | bytes 1044488 | tf_op jit(solution)/shard_map/ppermute | solution.py:423
  12.8 0.2 compare_reduce_fusion.3
  13.0 0.0 collective-permute-done.3
  13.0 0.1 broadcast_select_fusion
  13.1 3.4 %collective-permute-start.4 = (f32[3,16,640]{2,1,0:T(8,128)S(1)}, f32[3,16,640]{2,1,0:T(8,128)S(1)}, u32[]{:S(2)}, u32[]{:S(2)}) collective-permute-start(f32[3,16,640]{2,1,0:T(8,128)S(1)} %broadcast_select_fusion), channel_id=1, source_target_pairs={{0,12},{1,13},{2,14},{3,15},{4,8},{5,9},{6,10},{7,11},{8,4},{9,5},... | collective-permute-start | bytes 368648 | tf_op jit(solution)/shard_map/ppermute | solution.py:423
  16.5 3.9 %collective-permute-done.1.packed_ref = f32[136,640]{1,0:T(8,128)S(1)} collective-permute-done((f32[136,640]{1,0:T(8,128)S(1)}, f32[136,640]{1,0:T(8,128)S(1)}, u32[]{:S(2)}, u32[]{:S(2)}) %collective-permute-start.1) | collective-permute-done | bytes 348192 | tf_op jit(solution)/shard_map/ppermute | solution.py:423
  20.4 1.8 %shard_map.66 = (f32[2,2,2,5,32,128]{5,4,3,2,1,0:T(8,128)S(1)}, f32[2,4,6,8,128]{4,3,2,1,0:T(8,128)S(1)}, f32[2,8,128]{2,1,0:T(8,128)S(1)}, s32[3,8,128]{2,1,0:T(8,128)S(1)}) custom-call(s32[3]{0:T(128)S(1)} %copy-done.2, s32[2]{0:T(128)S(1)} %copy-done.4, f32[136,640]{1,0:T(8,128)S(1)} %collective-permute-done.1.packed_ref), custom_call_target="tpu_custom_call" | custom-call | flops 4096000 | bytes 983040 | tf_op jit(solution)/shard_map/pallas_call | solution.py:385
  22.2 0.2 compare_reduce_fusion.4
  22.4 0.0 collective-permute-done.4
  22.4 0.1 broadcast_select_fusion.1
  22.5 0.1 collective-permute-start.5
  22.5 1.3 %collective-permute-done.5 = f32[3,16,640]{2,1,0:T(8,128)S(1)} collective-permute-done((f32[3,16,640]{2,1,0:T(8,128)S(1)}, f32[3,16,640]{2,1,0:T(8,128)S(1)}, u32[]{:S(2)}, u32[]{:S(2)}) %collective-permute-start.5) | collective-permute-done | bytes 122912 | tf_op jit(solution)/shard_map/ppermute | solution.py:423
  23.9 11.5 %shard_map.67 = f32[3,32,640]{2,1,0:T(8,128)S(1)} custom-call(f32[2,2,2,5,32,128]{5,4,3,2,1,0:T(8,128)S(1)} %get-tuple-element.15.own_ref, f32[2,4,6,8,128]{4,3,2,1,0:T(8,128)S(1)} %get-tuple-element.16.own_taps_ref, f32[2,8,128]{2,1,0:T(8,128)S(1)} %get-tuple-element.17.own_rate_ref, f32[2,2,2,5,32,128]{5,4,3,2,1,0:T(8,128)S(1)} %get-tuple-element.19.near_ref, ...), custom_call_target="tpu_custom_call" | custom-call | tf_op jit(solution)/shard_map/pallas_call | solution.py:405
  35.4 0.2 collective-permute-start.6
  35.7 1.2 %collective-permute-done.6 = f32[3,16,512]{2,1,0:T(8,128)S(1)} collective-permute-done((f32[3,16,512]{2,1,0:T(8,128)S(1)}, f32[3,16,512]{2,1,0:T(8,128)S(1)}, u32[]{:S(2)}, u32[]{:S(2)}) %collective-permute-start.6) | collective-permute-done | bytes 98336 | tf_op jit(solution)/shard_map/ppermute | solution.py:423
  36.8 0.8 %collective-permute-start.7 = (f32[3,16,512]{2,1,0:T(8,128)S(1)}, f32[3,16,512]{2,1,0:T(8,128)S(1)}, u32[]{:S(2)}, u32[]{:S(2)}) collective-permute-start(f32[3,16,512]{2,1,0:T(8,128)S(1)} %select_add_fusion), channel_id=1, source_target_pairs={{0,4},{1,5},{2,6},{3,7},{4,0},{5,1},{6,2},{7,3},{8,12},{9,13},{10,... | collective-permute-start | bytes 294920 | tf_op jit(solution)/shard_map/ppermute | solution.py:423
  37.7 4.1 %collective-permute-done.7 = f32[3,16,512]{2,1,0:T(8,128)S(1)} collective-permute-done((f32[3,16,512]{2,1,0:T(8,128)S(1)}, f32[3,16,512]{2,1,0:T(8,128)S(1)}, u32[]{:S(2)}, u32[]{:S(2)}) %collective-permute-start.7) | collective-permute-done | bytes 98336 | tf_op jit(solution)/shard_map/ppermute | solution.py:423
  41.8 2.9 %collective-permute-start.8 = (f32[3,16,512]{2,1,0:T(8,128)S(1)}, f32[3,16,512]{2,1,0:T(8,128)S(1)}, u32[]{:S(2)}, u32[]{:S(2)}) collective-permute-start(f32[3,16,512]{2,1,0:T(8,128)S(1)} %add.10), channel_id=1, source_target_pairs={{0,12},{1,13},{2,14},{3,15},{4,8},{5,9},{6,10},{7,11},{8,4},{9,5},... | collective-permute-start | bytes 294920 | tf_op jit(solution)/shard_map/ppermute | solution.py:423
  44.6 3.7 %collective-permute-done.8 = f32[3,16,512]{2,1,0:T(8,128)S(1)} collective-permute-done((f32[3,16,512]{2,1,0:T(8,128)S(1)}, f32[3,16,512]{2,1,0:T(8,128)S(1)}, u32[]{:S(2)}, u32[]{:S(2)}) %collective-permute-start.8) | collective-permute-done | bytes 98336 | tf_op jit(solution)/shard_map/ppermute | solution.py:423
  48.4 0.1 select_reduce_fusion.3
  48.5 1.6 %collective-permute-start.9 = (f32[2,16,512]{2,1,0:T(8,128)S(1)}, f32[2,16,512]{2,1,0:T(8,128)S(1)}, u32[]{:S(2)}, u32[]{:S(2)}) collective-permute-start(f32[2,16,512]{2,1,0:T(8,128)S(1)} %pad_maximum_fusion.1), channel_id=1, source_target_pairs={{0,2},{1,3},{2,0},{3,1},{4,6},{5,7},{6,4},{7,5},{8,10},{9,11},{10,... | collective-permute-start | bytes 196616 | tf_op jit(solution)/shard_map/ppermute | solution.py:423
  50.1 2.7 %collective-permute-done.9 = f32[2,16,512]{2,1,0:T(8,128)S(1)} collective-permute-done((f32[2,16,512]{2,1,0:T(8,128)S(1)}, f32[2,16,512]{2,1,0:T(8,128)S(1)}, u32[]{:S(2)}, u32[]{:S(2)}) %collective-permute-start.9) | collective-permute-done | bytes 65568 | tf_op jit(solution)/shard_map/ppermute | solution.py:423
  52.8 0.1 collective-permute-start.10
  52.9 1.2 %collective-permute-done.10 = f32[16,1024]{1,0:T(8,128)S(1)} collective-permute-done((f32[16,1024]{1,0:T(8,128)S(1)}, f32[16,1024]{1,0:T(8,128)S(1)}, u32[]{:S(2)}, u32[]{:S(2)}) %collective-permute-start.10) | collective-permute-done | bytes 65568 | tf_op jit(solution)/shard_map/ppermute | solution.py:423
  54.2 0.7 %maximum_select_fusion.2 = f32[1,32,1024]{2,1,0:T(8,128)} fusion(f32[1,16,1024]{2,1,0:T(8,128)S(1)} %get-tuple-element.33, f32[1,16,1024]{2,1,0:T(8,128)S(1)} %bitcast.23, pred[]{:T(512)S(6)} %ne.8), kind=kLoop, calls=%fused_computation.5 | loop fusion | flops 98304 | bytes 262145 | tf_op jit(solution)/shard_map/jit(_where)/select_n | solution.py:447
  (13 shorter events, 0.2 us)
Async XLA Ops:
  0.0 4.7 %copy-start = (f32[2,2,32,1024]{3,2,1,0:T(8,128)S(1)}, f32[2,2,32,1024]{3,2,1,0:T(8,128)}, u32[]{:S(2)}) copy-start(f32[2,2,32,1024]{3,2,1,0:T(8,128)} %receiver_ref.3) | copy-start | bytes 1572868
  0.0 1.6 %collective-permute-start = (f32[32,1024]{1,0:T(8,128)}, f32[32,1024]{1,0:T(8,128)S(1)}, u32[]{:S(2)}, u32[]{:S(2)}) collective-permute-start(f32[32,1024]{1,0:T(8,128)} %bitcast.18), channel_id=1, source_target_pairs={{0,1},{1,0},{2,3},{3,2},{4,5},{5,4},{6,7},{7,6},{8,9},{9,8},{10,11... | collective-permute-start | bytes 393224 | tf_op jit(solution)/shard_map/ppermute | solution.py:423
  1.7 3.0 %copy-start.1 = (f32[2,4,6]{2,1,0:T(4,128)S(1)}, f32[2,4,6]{2,1,0:T(4,128)}, u32[]{:S(2)}) copy-start(f32[2,4,6]{2,1,0:T(4,128)} %taps_ref.3) | copy-start | bytes 580
  1.7 3.0 %copy-start.2 = (s32[3]{0:T(128)S(1)}, s32[3]{0:T(128)}, u32[]{:S(2)}) copy-start(s32[3]{0:T(128)} %owner_ref.5) | copy-start | bytes 40
  1.7 3.0 %copy-start.3 = (f32[2,2]{1,0:T(2,128)S(1)}, f32[2,2]{1,0:T(2,128)}, u32[]{:S(2)}) copy-start(f32[2,2]{1,0:T(2,128)} %spectrum_ref.3) | copy-start | bytes 52
  1.7 5.7 %collective-permute-start.2 = (f32[2,16,640]{2,1,0:T(8,128)S(1)}, f32[2,16,640]{2,1,0:T(8,128)S(1)}, u32[]{:S(2)}, u32[]{:S(2)}) collective-permute-start(f32[2,16,640]{2,1,0:T(8,128)S(1)} %get-tuple-element.34), channel_id=1, source_target_pairs={{0,2},{1,3},{2,0},{3,1},{4,6},{5,7},{6,4},{7,5},{8,10},{9,11},{10,... | collective-permute-start | bytes 245768 | tf_op jit(solution)/shard_map/ppermute | solution.py:423
  7.4 2.0 %copy-start.4 = (s32[2]{0:T(128)S(1)}, s32[2]{0:T(128)}, u32[]{:S(2)}) copy-start(s32[2]{0:T(128)} %position_ref.3) | copy-start | bytes 28
  7.5 5.4 %collective-permute-start.3 = (f32[3,16,640]{2,1,0:T(8,128)S(1)}, f32[3,16,640]{2,1,0:T(8,128)S(1)}, u32[]{:S(2)}, u32[]{:S(2)}) collective-permute-start(f32[3,16,640]{2,1,0:T(8,128)S(1)} %select_select_fusion), channel_id=1, source_target_pairs={{0,4},{1,5},{2,6},{3,7},{4,0},{5,1},{6,2},{7,3},{8,12},{9,13},{10,... | collective-permute-start | bytes 368648 | tf_op jit(solution)/shard_map/ppermute | solution.py:423
  11.2 9.2 %collective-permute-start.1 = (f32[136,640]{1,0:T(8,128)S(1)}, f32[136,640]{1,0:T(8,128)S(1)}, u32[]{:S(2)}, u32[]{:S(2)}) collective-permute-start(f32[136,640]{1,0:T(8,128)S(1)} %get-tuple-element.18), channel_id=1, source_target_pairs={{0,2},{1,3},{2,0},{3,1},{4,6},{5,7},{6,4},{7,5},{8,10},{9,11},{10,... | collective-permute-start | bytes 1044488 | tf_op jit(solution)/shard_map/ppermute | solution.py:423
  13.1 9.3 %collective-permute-start.4 = (f32[3,16,640]{2,1,0:T(8,128)S(1)}, f32[3,16,640]{2,1,0:T(8,128)S(1)}, u32[]{:S(2)}, u32[]{:S(2)}) collective-permute-start(f32[3,16,640]{2,1,0:T(8,128)S(1)} %broadcast_select_fusion), channel_id=1, source_target_pairs={{0,12},{1,13},{2,14},{3,15},{4,8},{5,9},{6,10},{7,11},{8,4},{9,5},... | collective-permute-start | bytes 368648 | tf_op jit(solution)/shard_map/ppermute | solution.py:423
  22.5 1.4 %collective-permute-start.5 = (f32[3,16,640]{2,1,0:T(8,128)S(1)}, f32[3,16,640]{2,1,0:T(8,128)S(1)}, u32[]{:S(2)}, u32[]{:S(2)}) collective-permute-start(f32[3,16,640]{2,1,0:T(8,128)S(1)} %broadcast_select_fusion.1), channel_id=1, source_target_pairs={{0,1},{1,0},{2,3},{3,2},{4,5},{5,4},{6,7},{7,6},{8,9},{9,8},{10,11... | collective-permute-start | bytes 368648 | tf_op jit(solution)/shard_map/ppermute | solution.py:423
  35.4 1.4 %collective-permute-start.6 = (f32[3,16,512]{2,1,0:T(8,128)S(1)}, f32[3,16,512]{2,1,0:T(8,128)S(1)}, u32[]{:S(2)}, u32[]{:S(2)}) collective-permute-start(f32[3,16,512]{2,1,0:T(8,128)S(1)} %slice_select_fusion.1), channel_id=1, source_target_pairs={{0,1},{1,0},{2,3},{3,2},{4,5},{5,4},{6,7},{7,6},{8,9},{9,8},{10,11... | collective-permute-start | bytes 294920 | tf_op jit(solution)/shard_map/ppermute | solution.py:423
  36.8 4.9 %collective-permute-start.7 = (f32[3,16,512]{2,1,0:T(8,128)S(1)}, f32[3,16,512]{2,1,0:T(8,128)S(1)}, u32[]{:S(2)}, u32[]{:S(2)}) collective-permute-start(f32[3,16,512]{2,1,0:T(8,128)S(1)} %select_add_fusion), channel_id=1, source_target_pairs={{0,4},{1,5},{2,6},{3,7},{4,0},{5,1},{6,2},{7,3},{8,12},{9,13},{10,... | collective-permute-start | bytes 294920 | tf_op jit(solution)/shard_map/ppermute | solution.py:423
  41.8 6.6 %collective-permute-start.8 = (f32[3,16,512]{2,1,0:T(8,128)S(1)}, f32[3,16,512]{2,1,0:T(8,128)S(1)}, u32[]{:S(2)}, u32[]{:S(2)}) collective-permute-start(f32[3,16,512]{2,1,0:T(8,128)S(1)} %add.10), channel_id=1, source_target_pairs={{0,12},{1,13},{2,14},{3,15},{4,8},{5,9},{6,10},{7,11},{8,4},{9,5},... | collective-permute-start | bytes 294920 | tf_op jit(solution)/shard_map/ppermute | solution.py:423
  48.5 4.3 %collective-permute-start.9 = (f32[2,16,512]{2,1,0:T(8,128)S(1)}, f32[2,16,512]{2,1,0:T(8,128)S(1)}, u32[]{:S(2)}, u32[]{:S(2)}) collective-permute-start(f32[2,16,512]{2,1,0:T(8,128)S(1)} %pad_maximum_fusion.1), channel_id=1, source_target_pairs={{0,2},{1,3},{2,0},{3,1},{4,6},{5,7},{6,4},{7,5},{8,10},{9,11},{10,... | collective-permute-start | bytes 196616 | tf_op jit(solution)/shard_map/ppermute | solution.py:423
  52.8 1.3 %collective-permute-start.10 = (f32[16,1024]{1,0:T(8,128)S(1)}, f32[16,1024]{1,0:T(8,128)S(1)}, u32[]{:S(2)}, u32[]{:S(2)}) collective-permute-start(f32[16,1024]{1,0:T(8,128)S(1)} %get-tuple-element.32), channel_id=1, source_target_pairs={{0,1},{1,0},{2,3},{3,2},{4,5},{5,4},{6,7},{7,6},{8,9},{9,8},{10,11... | collective-permute-start | bytes 196616 | tf_op jit(solution)/shard_map/ppermute | solution.py:423

commit v5 on v4

--- a/solution.py
+++ b/solution.py
@@ -83,27 +83,53 @@
         turn_ref[t] = jnp.full((SUB, LANES), owner_ref[t] ^ lax.axis_index("freq"), jnp.int32)
 
 
-def pack_kernel(owner_ref, taps_ref, spectrum_ref, receiver_ref, slab_ref, out_ref, turn_ref):
-    spread_turn(owner_ref, turn_ref)
+def tail_of(ref, rows, i):
+    across = ref.shape[1] // LANES
+    down = rows + SUB * (i // across)
+    return ref.at[down : down + SUB, LANES * (i % across) : LANES * (i % across + 1)]
+
+
+def tail_rows(freq_local, height, half, border):
+    strips = -(-freq_local * 2 * (height // SUB) // (LANES // border))
+    scalars = -(-freq_local * (len(directions) * 6 + 2) // LANES)
+    return SUB * -(-(strips + scalars) // (half // LANES)), strips
+
+
+def pack_kernel(border, taps_ref, spectrum_ref, receiver_ref, slab_ref, out_ref):
     freq_local, _, height, breadth = receiver_ref.shape
-    width = out_ref.shape[1]
-    start = jnp.where((lax.axis_index("freq") & NEAR_COLUMNS) != 0, 0, breadth - width)
-    row = 0
+    half = out_ref.shape[1]
+    groups = height // SUB
+    _, strips = tail_rows(freq_local, height, half, border)
+    lane = columns()
+    to_lower = (lax.axis_index("freq") & NEAR_COLUMNS) != 0
+    start = jnp.where(to_lower, 0, breadth - half)
+    beside = pl.ds(pl.multiple_of(jnp.where(to_lower, half, half - LANES), LANES), LANES)
+    rows = freq_local * 2 * height
+    per = LANES // border
+    strip = [jnp.zeros((SUB, LANES), jnp.float32) for _ in range(strips)]
     for f in range(freq_local):
         for part in range(2):
-            for b in range(width // LANES):
+            row = (2 * f + part) * height
+            for b in range(half // LANES):
                 column = pl.ds(pl.multiple_of(start + LANES * b, LANES), LANES)
                 out_ref[row : row + height, LANES * b : LANES * (b + 1)] = receiver_ref[f, part, :, column]
-            row += height
+            for g in range(groups):
+                value = receiver_ref[f, part, SUB * g : SUB * (g + 1), beside]
+                value = jnp.where(to_lower, value, pltpu.roll(value, border, 1))
+                i, at = divmod((2 * f + part) * groups + g, per)
+                if at:
+                    value = pltpu.roll(value, border * at, 1)
+                strip[i] = jnp.where((lane >= border * at) & (lane < border * (at + 1)), value, strip[i])
+    for i, value in enumerate(strip):
+        tail_of(out_ref, rows, i)[...] = value
     scalars = [
         taps_ref[f, d, i] for f in range(freq_local) for d in range(len(directions)) for i in range(6)
     ] + [spectrum_ref[f, i] for f in range(freq_local) for i in range(2)]
-    lane = columns()
-    for b in range(width // LANES):
+    for b in range(-(-len(scalars) // LANES)):
         value = jnp.zeros((SUB, LANES), jnp.float32)
         for i, scalar in enumerate(scalars[LANES * b : LANES * (b + 1)]):
             value = jnp.where(lane == i, scalar, value)
-        out_ref[row : row + SUB, LANES * b : LANES * (b + 1)] = value
+        tail_of(out_ref, rows, strips + b)[...] = value
 
 
 def prepare(freq_total, rank, first_column, owner_ref, position_ref, block_of, taps_of, wave_of, results):
@@ -123,8 +149,7 @@
         rate_ref[f] = jnp.full((SUB, LANES), number(f) * (lens_rate / freq_total), jnp.float32)
     spread_turn(owner_ref, turn_ref)
 
-    @pl.loop(0, freq_local)
-    def _(f):
+    for f in range(freq_local):
         for part in range(2):
             for g in range(groups):
                 loaded = [block_of(f, part, g, b) for b in range(blocks)]
@@ -149,7 +174,7 @@
 
 
 def prepare_own_kernel(
-    freq_total, owner_ref, position_ref, taps_ref, spectrum_ref, receiver_ref, *results
+    freq_total, owner_ref, position_ref, taps_ref, spectrum_ref, receiver_ref, packed_ref, *results
 ):
     blocks = results[0].shape[3]
     here = lax.axis_index("freq")
@@ -172,19 +197,41 @@
     )
 
 
-def prepare_near_kernel(freq_total, breadth, owner_ref, position_ref, packed_ref, *results):
+def prepare_near_kernel(freq_total, breadth, border, owner_ref, position_ref, packed_ref, *results):
     freq_local, _, _, blocks, height, _ = results[0].shape
+    half = packed_ref.shape[1]
+    groups = height // SUB
     here = lax.axis_index("freq")
-    first_column = jnp.where((here & NEAR_COLUMNS) != 0, breadth - blocks * LANES, 0)
+    upper = (here & NEAR_COLUMNS) != 0
+    first_column = jnp.where(upper, breadth - blocks * LANES, 0)
     rows = freq_local * 2 * height
+    _, strips = tail_rows(freq_local, height, half, border)
+    per = LANES // border
     taps_count = len(directions) * 6
+    lane = columns()
+
+    def main(f, part, g, b):
+        row = (2 * f + part) * height + SUB * g
+        return packed_ref[row : row + SUB, LANES * b : LANES * (b + 1)]
+
+    def beside(f, part, g):
+        i, at = divmod((2 * f + part) * groups + g, per)
+        value = tail_of(packed_ref, rows, i)[...]
+        if at:
+            value = pltpu.roll(value, LANES - border * at, 1)
+        value = jnp.where(lane < border, value, 0.0)
+        return jnp.where(upper, pltpu.roll(value, LANES - border, 1), value)
 
     def block_of(f, part, g, b):
-        row = pl.multiple_of((2 * f + part) * height + SUB * g, SUB)
-        return packed_ref[pl.ds(row, SUB), LANES * b : LANES * (b + 1)]
+        if b == 0:
+            return jnp.where(upper, beside(f, part, g), main(f, part, g, 0))
+        if b == blocks - 1:
+            return jnp.where(upper, main(f, part, g, b - 1), beside(f, part, g))
+        return jnp.where(upper, main(f, part, g, b - 1), main(f, part, g, b))
 
     def scalar(i):
-        return jnp.broadcast_to(packed_ref[rows : rows + SUB, i : i + 1], (SUB, LANES))
+        value = tail_of(packed_ref, rows, strips + i // LANES)[...]
+        return jnp.broadcast_to(value[:, i % LANES : i % LANES + 1], (SUB, LANES))
 
     prepare(
         freq_total,
@@ -363,20 +410,17 @@
 VMEM = pl.BlockSpec(memory_space=pltpu.VMEM)
 
 
-def pack(owners, taps, spectrum, receiver, slab, width):
+def pack(taps, spectrum, receiver, slab, half, border):
     freq_local, _, height, _ = receiver.shape
-    rows = freq_local * 2 * height + SUB
+    rows = freq_local * 2 * height + tail_rows(freq_local, height, half, border)[0]
     return pl.pallas_call(
-        pack_kernel,
-        out_shape=(
-            jax.ShapeDtypeStruct((rows, width), jnp.float32),
-            jax.ShapeDtypeStruct((owners.shape[0], SUB, LANES), jnp.int32),
-        ),
-        in_specs=[SMEM, SMEM, SMEM, VMEM, pl.BlockSpec(memory_space=pl.ANY)],
-        out_specs=(VMEM, VMEM),
-        cost_estimate=pl.CostEstimate(flops=0, bytes_accessed=8 * rows * width, transcendentals=0),
+        functools.partial(pack_kernel, border),
+        out_shape=jax.ShapeDtypeStruct((rows, half), jnp.float32),
+        in_specs=[SMEM, SMEM, VMEM, pl.BlockSpec(memory_space=pl.ANY)],
+        out_specs=VMEM,
+        cost_estimate=pl.CostEstimate(flops=0, bytes_accessed=8 * rows * half, transcendentals=0),
         compiler_params=pltpu.CompilerParams(vmem_limit_bytes=32 * 1024 * 1024),
-    )(owners, taps, spectrum, receiver, slab)
+    )(taps, spectrum, receiver, slab)
 
 
 def prepared(kernel, shape, levels, width, specs, operands):
@@ -464,7 +508,7 @@
     far = far_bits(size)
     for i, (bit, mask) in enumerate(far):
         got = exchange(carried, mask, size)
-        turn = turns[2 if i == len(far) - 1 else 1][:, :1, :1]
+        turn = turns[1 if i == len(far) - 1 else 0][:, :1, :1]
         carried = jnp.where((turn & bit) == 0, carried, got)
     return joined(carried, exchange(carried, NEAR_ROWS, size), upper_rows, -2)
 
@@ -495,31 +539,31 @@
     freq_total = size * freq_local
     half = breadth // 2
     border = REACH * sum(1 for _, step_y in directions if step_y) * levels
-    width = -(-(half + border) // LANES) * LANES
+    width = half + LANES
     shape = receiver_data.shape
 
     near_slab = exchange(slowness[0], NEAR_ROWS, size)
-    packed, pack_turn = pack(
-        depth_owner, filter_taps, source_spectrum, receiver_data, near_slab, width
-    )
-    packed = exchange(packed, NEAR_COLUMNS, size)
+    packed = pack(
+        filter_taps, source_spectrum, receiver_data, near_slab, half, border
+    )
+    arrived = exchange(packed, NEAR_COLUMNS, size)
     *own, own_turn = prepared(
         functools.partial(prepare_own_kernel, freq_total),
         shape,
         levels,
         width,
-        [SMEM, SMEM, SMEM, SMEM, VMEM],
-        (depth_owner, source_position, filter_taps, source_spectrum, receiver_data),
+        [SMEM, SMEM, SMEM, SMEM, VMEM, pl.BlockSpec(memory_space=pl.ANY)],
+        (depth_owner, source_position, filter_taps, source_spectrum, receiver_data, packed),
     )
     *near, near_turn = prepared(
-        functools.partial(prepare_near_kernel, freq_total, breadth),
+        functools.partial(prepare_near_kernel, freq_total, breadth, border),
         shape,
         levels,
         width,
         [SMEM, SMEM, VMEM],
-        (depth_owner, source_position, packed),
-    )
-    turns = (pack_turn, own_turn, near_turn)
+        (depth_owner, source_position, arrived),
+    )
+    turns = (own_turn, near_turn)
     slabs = fetch_slabs(slowness[0], near_slab, turns, rank, size, width)
     partial = migrate(own, near, slabs, freq_total)
     return sums_to_owner(partial, depth_owner, rank, size, half)[None]

time: 55 us -> 53.3 us (0.969)
  waiting for transfers between devices: 20.3 us -> 18 us
  Pallas kernels: 15.8 us -> 17.1 us
  starting transfers between devices: 15.9 us -> 15.3 us
    ppermute x11, waiting for transfers between devices: 20.3 us -> 18 us  [exchange(): return lax.ppermute(value, 'freq', [(i, i ^ mask) for i in range(size)])]
    pallas_call x2, Pallas kernels: 3.63 us -> 4.77 us  [prepared(): pl.pallas_call(kernel, out_shape=(jax.ShapeDtypeStruct((freq_local, 2, 2,...]
    ppermute x11, starting transfers between devices: 15.9 us -> 15.3 us  [exchange(): return lax.ppermute(value, 'freq', [(i, i ^ mask) for i in range(size)])]
  transfers between devices with their start and end apart: 11 -> 11, of which waited for: 9 -> 10; matrix products, arithmetic and copies ran while one was open for 3% -> 3% of each run, Pallas kernels for 8% -> 10%
where the time goes in v5:
time: 53.3 us; the launch traced here: 53.1 us
  waiting for transfers between devices  18 us (34%)
  Pallas kernels  17.1 us (32%)
  starting transfers between devices  15.3 us (29%)
  other arithmetic  2.51 us (5%)
    ppermute x11, waiting for transfers between devices, exchange(): return lax.ppermute(value, 'freq', [(i, i ^ mask) for i in range(size)])  18 us
    ppermute x11, starting transfers between devices, exchange(): return lax.ppermute(value, 'freq', [(i, i ^ mask) for i in range(size)])  15.3 us
    pallas_call x1, Pallas kernels, migrate(): pl.pallas_call(functools.partial(migrate_kernel, freq_total), out_shape=j...  11.5 us
    pallas_call x2, Pallas kernels, prepared(): pl.pallas_call(kernel, out_shape=(jax.ShapeDtypeStruct((freq_local, 2, 2,...  4.77 us
  transfers between devices with their start and end apart: 11, of which 10 were waited for; matrix products, arithmetic and copies ran while one was open for 3% of the time, Pallas kernels for 10%

profile of v5, /device:TPU:0, one launch (start us, length us, event | category | flops | bytes accessed | tf_op | source)
XLA Modules:
  0.0 53.1 jit_solution(6101247580089515100)
XLA Ops:
  0.0 0.0 copy-start
  0.0 0.5 collective-permute-start
  0.5 0.9 %slice_select_fusion.3 = f32[1,16,1024]{2,1,0:T(8,128)S(1)} fusion(f32[1,32,1024]{2,1,0:T(8,128)} %param.9, pred[]{:T(512)S(6)} %ne.8), kind=kLoop, calls=%fused_computation.19 | loop fusion | flops 16384 | bytes 196609 | tf_op jit(solution)/shard_map/jit(_where)/select_n | solution.py:482
  1.3 0.3 collective-permute-done.slab_ref
  1.7 0.0 copy-start.1
  1.7 0.0 copy-start.3
  1.7 0.0 copy-start.2
  1.7 0.0 copy-start.4
  1.8 2.9 %collective-permute-start.2 = (f32[2,16,640]{2,1,0:T(8,128)S(1)}, f32[2,16,640]{2,1,0:T(8,128)S(1)}, u32[]{:S(2)}, u32[]{:S(2)}) collective-permute-start(f32[2,16,640]{2,1,0:T(8,128)S(1)} %get-tuple-element.31), channel_id=1, source_target_pairs={{0,2},{1,3},{2,0},{3,1},{4,6},{5,7},{6,4},{7,5},{8,10},{9,11},{10,... | collective-permute-start | bytes 245768 | tf_op jit(solution)/shard_map/ppermute | solution.py:467
  4.7 0.0 copy-done
  4.7 0.0 copy-done.1
  4.7 0.0 copy-done.3
  4.7 0.8 %shard_map.64.packed_ref = f32[136,512]{1,0:T(8,128)S(1)} custom-call(f32[2,4,6]{2,1,0:T(4,128)S(1)} %copy-done.1, f32[2,2]{1,0:T(2,128)S(1)} %copy-done.3, f32[2,2,32,1024]{3,2,1,0:T(8,128)S(1)} %copy-done, f32[32,1024]{1,0:T(8,128)S(1)} %collective-permute-done.slab_ref), custom_call_target="tpu_custom_call" | custom-call | bytes 557056 | tf_op jit(solution)/shard_map/pallas_call | solution.py:416
  5.5 0.0 copy-done.2
  5.5 0.0 copy-done.4
  5.5 1.5 %shard_map.65 = (f32[2,2,2,5,32,128]{5,4,3,2,1,0:T(8,128)S(1)}, f32[2,4,6,8,128]{4,3,2,1,0:T(8,128)S(1)}, f32[2,8,128]{2,1,0:T(8,128)S(1)}, s32[3,8,128]{2,1,0:T(8,128)S(1)}) custom-call(s32[3]{0:T(128)S(1)} %copy-done.2, s32[2]{0:T(128)S(1)} %copy-done.4, f32[2,4,6]{2,1,0:T(4,128)S(1)} %copy-done.1, f32[2,2]{1,0:T(2,128)S(1)} %copy-done.3, ...), custom_call_target="tpu_custom_call" | custom-call | flops 4096000 | bytes 983040 | tf_op jit(solution)/shard_map/pallas_call | solution.py:429
  7.1 0.3 compare_reduce_fusion.3
  7.4 0.1 collective-permute-done.2
  7.5 0.1 select_select_fusion
  7.6 1.9 %collective-permute-start.3 = (f32[3,16,640]{2,1,0:T(8,128)S(1)}, f32[3,16,640]{2,1,0:T(8,128)S(1)}, u32[]{:S(2)}, u32[]{:S(2)}) collective-permute-start(f32[3,16,640]{2,1,0:T(8,128)S(1)} %select_select_fusion), channel_id=1, source_target_pairs={{0,4},{1,5},{2,6},{3,7},{4,0},{5,1},{6,2},{7,3},{8,12},{9,13},{10,... | collective-permute-start | bytes 368648 | tf_op jit(solution)/shard_map/ppermute | solution.py:467
  9.4 1.5 %collective-permute-start.1 = (f32[136,512]{1,0:T(8,128)S(1)}, f32[136,512]{1,0:T(8,128)S(1)}, u32[]{:S(2)}, u32[]{:S(2)}) collective-permute-start(f32[136,512]{1,0:T(8,128)S(1)} %shard_map.64.packed_ref), channel_id=1, source_target_pairs={{0,2},{1,3},{2,0},{3,1},{4,6},{5,7},{6,4},{7,5},{8,10},{9,11},{10,... | collective-permute-start | bytes 835592 | tf_op jit(solution)/shard_map/ppermute | solution.py:467
  10.9 1.7 %collective-permute-done.3 = f32[3,16,640]{2,1,0:T(8,128)S(1)} collective-permute-done((f32[3,16,640]{2,1,0:T(8,128)S(1)}, f32[3,16,640]{2,1,0:T(8,128)S(1)}, u32[]{:S(2)}, u32[]{:S(2)}) %collective-permute-start.3) | collective-permute-done | bytes 122912 | tf_op jit(solution)/shard_map/ppermute | solution.py:467
  12.7 0.1 broadcast_select_fusion
  12.8 3.7 %collective-permute-start.4 = (f32[3,16,640]{2,1,0:T(8,128)S(1)}, f32[3,16,640]{2,1,0:T(8,128)S(1)}, u32[]{:S(2)}, u32[]{:S(2)}) collective-permute-start(f32[3,16,640]{2,1,0:T(8,128)S(1)} %broadcast_select_fusion), channel_id=1, source_target_pairs={{0,12},{1,13},{2,14},{3,15},{4,8},{5,9},{6,10},{7,11},{8,4},{9,5},... | collective-permute-start | bytes 368648 | tf_op jit(solution)/shard_map/ppermute | solution.py:467
  16.5 0.8 %collective-permute-done.1.packed_ref = f32[136,512]{1,0:T(8,128)S(1)} collective-permute-done((f32[136,512]{1,0:T(8,128)S(1)}, f32[136,512]{1,0:T(8,128)S(1)}, u32[]{:S(2)}, u32[]{:S(2)}) %collective-permute-start.1) | collective-permute-done | bytes 278560 | tf_op jit(solution)/shard_map/ppermute | solution.py:467
  17.3 3.2 %shard_map.66 = (f32[2,2,2,5,32,128]{5,4,3,2,1,0:T(8,128)S(1)}, f32[2,4,6,8,128]{4,3,2,1,0:T(8,128)S(1)}, f32[2,8,128]{2,1,0:T(8,128)S(1)}, s32[3,8,128]{2,1,0:T(8,128)S(1)}) custom-call(s32[3]{0:T(128)S(1)} %copy-done.2, s32[2]{0:T(128)S(1)} %copy-done.4, f32[136,512]{1,0:T(8,128)S(1)} %collective-permute-done.1.packed_ref), custom_call_target="tpu_custom_call" | custom-call | flops 4096000 | bytes 983040 | tf_op jit(solution)/shard_map/pallas_call | solution.py:429
  20.5 0.2 compare_reduce_fusion.4
  20.7 0.0 collective-permute-done.4
  20.7 0.1 broadcast_select_fusion.1
  20.8 0.1 collective-permute-start.5
  20.9 1.3 %collective-permute-done.5 = f32[3,16,640]{2,1,0:T(8,128)S(1)} collective-permute-done((f32[3,16,640]{2,1,0:T(8,128)S(1)}, f32[3,16,640]{2,1,0:T(8,128)S(1)}, u32[]{:S(2)}, u32[]{:S(2)}) %collective-permute-start.5) | collective-permute-done | bytes 122912 | tf_op jit(solution)/shard_map/ppermute | solution.py:467
  22.2 11.5 %shard_map.67 = f32[3,32,640]{2,1,0:T(8,128)S(1)} custom-call(f32[2,2,2,5,32,128]{5,4,3,2,1,0:T(8,128)S(1)} %get-tuple-element.13.own_ref, f32[2,4,6,8,128]{4,3,2,1,0:T(8,128)S(1)} %get-tuple-element.14.own_taps_ref, f32[2,8,128]{2,1,0:T(8,128)S(1)} %get-tuple-element.15.own_rate_ref, f32[2,2,2,5,32,128]{5,4,3,2,1,0:T(8,128)S(1)} %get-tuple-element.16.near_ref, ...), custom_call_target="tpu_custom_call" | custom-call | tf_op jit(solution)/shard_map/pallas_call | solution.py:449
  33.8 0.2 collective-permute-start.6
  34.0 1.2 %collective-permute-done.6 = f32[3,16,512]{2,1,0:T(8,128)S(1)} collective-permute-done((f32[3,16,512]{2,1,0:T(8,128)S(1)}, f32[3,16,512]{2,1,0:T(8,128)S(1)}, u32[]{:S(2)}, u32[]{:S(2)}) %collective-permute-start.6) | collective-permute-done | bytes 98336 | tf_op jit(solution)/shard_map/ppermute | solution.py:467
  35.2 0.5 collective-permute-start.7
  35.7 4.4 %collective-permute-done.7 = f32[3,16,512]{2,1,0:T(8,128)S(1)} collective-permute-done((f32[3,16,512]{2,1,0:T(8,128)S(1)}, f32[3,16,512]{2,1,0:T(8,128)S(1)}, u32[]{:S(2)}, u32[]{:S(2)}) %collective-permute-start.7) | collective-permute-done | bytes 98336 | tf_op jit(solution)/shard_map/ppermute | solution.py:467
  40.1 2.6 %collective-permute-start.8 = (f32[3,16,512]{2,1,0:T(8,128)S(1)}, f32[3,16,512]{2,1,0:T(8,128)S(1)}, u32[]{:S(2)}, u32[]{:S(2)}) collective-permute-start(f32[3,16,512]{2,1,0:T(8,128)S(1)} %add.10), channel_id=1, source_target_pairs={{0,12},{1,13},{2,14},{3,15},{4,8},{5,9},{6,10},{7,11},{8,4},{9,5},... | collective-permute-start | bytes 294920 | tf_op jit(solution)/shard_map/ppermute | solution.py:467
  42.7 3.9 %collective-permute-done.8 = f32[3,16,512]{2,1,0:T(8,128)S(1)} collective-permute-done((f32[3,16,512]{2,1,0:T(8,128)S(1)}, f32[3,16,512]{2,1,0:T(8,128)S(1)}, u32[]{:S(2)}, u32[]{:S(2)}) %collective-permute-start.8) | collective-permute-done | bytes 98336 | tf_op jit(solution)/shard_map/ppermute | solution.py:467
  46.7 0.1 select_reduce_fusion.3
  46.8 1.3 %collective-permute-start.9 = (f32[2,16,512]{2,1,0:T(8,128)S(1)}, f32[2,16,512]{2,1,0:T(8,128)S(1)}, u32[]{:S(2)}, u32[]{:S(2)}) collective-permute-start(f32[2,16,512]{2,1,0:T(8,128)S(1)} %pad_maximum_fusion.1), channel_id=1, source_target_pairs={{0,2},{1,3},{2,0},{3,1},{4,6},{5,7},{6,4},{7,5},{8,10},{9,11},{10,... | collective-permute-start | bytes 196616 | tf_op jit(solution)/shard_map/ppermute | solution.py:467
  48.1 3.0 %collective-permute-done.9 = f32[2,16,512]{2,1,0:T(8,128)S(1)} collective-permute-done((f32[2,16,512]{2,1,0:T(8,128)S(1)}, f32[2,16,512]{2,1,0:T(8,128)S(1)}, u32[]{:S(2)}, u32[]{:S(2)}) %collective-permute-start.9) | collective-permute-done | bytes 65568 | tf_op jit(solution)/shard_map/ppermute | solution.py:467
  51.2 0.1 collective-permute-start.10
  51.2 1.2 %collective-permute-done.10 = f32[16,1024]{1,0:T(8,128)S(1)} collective-permute-done((f32[16,1024]{1,0:T(8,128)S(1)}, f32[16,1024]{1,0:T(8,128)S(1)}, u32[]{:S(2)}, u32[]{:S(2)}) %collective-permute-start.10) | collective-permute-done | bytes 65568 | tf_op jit(solution)/shard_map/ppermute | solution.py:467
  52.5 0.7 %maximum_select_fusion.2 = f32[1,32,1024]{2,1,0:T(8,128)} fusion(f32[1,16,1024]{2,1,0:T(8,128)S(1)} %get-tuple-element.30, f32[1,16,1024]{2,1,0:T(8,128)S(1)} %bitcast.23, pred[]{:T(512)S(6)} %ne.8), kind=kLoop, calls=%fused_computation.5 | loop fusion | flops 98304 | bytes 262145 | tf_op jit(solution)/shard_map/jit(_where)/select_n | solution.py:491
  (13 shorter events, 0.2 us)
Async XLA Ops:
  0.0 4.7 %copy-start = (f32[2,2,32,1024]{3,2,1,0:T(8,128)S(1)}, f32[2,2,32,1024]{3,2,1,0:T(8,128)}, u32[]{:S(2)}) copy-start(f32[2,2,32,1024]{3,2,1,0:T(8,128)} %receiver_ref.3) | copy-start | bytes 1572868
  0.0 1.6 %collective-permute-start = (f32[32,1024]{1,0:T(8,128)}, f32[32,1024]{1,0:T(8,128)S(1)}, u32[]{:S(2)}, u32[]{:S(2)}) collective-permute-start(f32[32,1024]{1,0:T(8,128)} %bitcast.18), channel_id=1, source_target_pairs={{0,1},{1,0},{2,3},{3,2},{4,5},{5,4},{6,7},{7,6},{8,9},{9,8},{10,11... | collective-permute-start | bytes 393224 | tf_op jit(solution)/shard_map/ppermute | solution.py:467
  1.7 3.0 %copy-start.1 = (f32[2,4,6]{2,1,0:T(4,128)S(1)}, f32[2,4,6]{2,1,0:T(4,128)}, u32[]{:S(2)}) copy-start(f32[2,4,6]{2,1,0:T(4,128)} %taps_ref.3) | copy-start | bytes 580
  1.7 3.0 %copy-start.3 = (f32[2,2]{1,0:T(2,128)S(1)}, f32[2,2]{1,0:T(2,128)}, u32[]{:S(2)}) copy-start(f32[2,2]{1,0:T(2,128)} %spectrum_ref.3) | copy-start | bytes 52
  1.7 3.8 %copy-start.2 = (s32[3]{0:T(128)S(1)}, s32[3]{0:T(128)}, u32[]{:S(2)}) copy-start(s32[3]{0:T(128)} %owner_ref.3) | copy-start | bytes 40
  1.7 3.8 %copy-start.4 = (s32[2]{0:T(128)S(1)}, s32[2]{0:T(128)}, u32[]{:S(2)}) copy-start(s32[2]{0:T(128)} %position_ref.3) | copy-start | bytes 28
  1.8 5.7 %collective-permute-start.2 = (f32[2,16,640]{2,1,0:T(8,128)S(1)}, f32[2,16,640]{2,1,0:T(8,128)S(1)}, u32[]{:S(2)}, u32[]{:S(2)}) collective-permute-start(f32[2,16,640]{2,1,0:T(8,128)S(1)} %get-tuple-element.31), channel_id=1, source_target_pairs={{0,2},{1,3},{2,0},{3,1},{4,6},{5,7},{6,4},{7,5},{8,10},{9,11},{10,... | collective-permute-start | bytes 245768 | tf_op jit(solution)/shard_map/ppermute | solution.py:467
  7.6 5.1 %collective-permute-start.3 = (f32[3,16,640]{2,1,0:T(8,128)S(1)}, f32[3,16,640]{2,1,0:T(8,128)S(1)}, u32[]{:S(2)}, u32[]{:S(2)}) collective-permute-start(f32[3,16,640]{2,1,0:T(8,128)S(1)} %select_select_fusion), channel_id=1, source_target_pairs={{0,4},{1,5},{2,6},{3,7},{4,0},{5,1},{6,2},{7,3},{8,12},{9,13},{10,... | collective-permute-start | bytes 368648 | tf_op jit(solution)/shard_map/ppermute | solution.py:467
  9.4 7.9 %collective-permute-start.1 = (f32[136,512]{1,0:T(8,128)S(1)}, f32[136,512]{1,0:T(8,128)S(1)}, u32[]{:S(2)}, u32[]{:S(2)}) collective-permute-start(f32[136,512]{1,0:T(8,128)S(1)} %shard_map.64.packed_ref), channel_id=1, source_target_pairs={{0,2},{1,3},{2,0},{3,1},{4,6},{5,7},{6,4},{7,5},{8,10},{9,11},{10,... | collective-permute-start | bytes 835592 | tf_op jit(solution)/shard_map/ppermute | solution.py:467
  12.8 7.9 %collective-permute-start.4 = (f32[3,16,640]{2,1,0:T(8,128)S(1)}, f32[3,16,640]{2,1,0:T(8,128)S(1)}, u32[]{:S(2)}, u32[]{:S(2)}) collective-permute-start(f32[3,16,640]{2,1,0:T(8,128)S(1)} %broadcast_select_fusion), channel_id=1, source_target_pairs={{0,12},{1,13},{2,14},{3,15},{4,8},{5,9},{6,10},{7,11},{8,4},{9,5},... | collective-permute-start | bytes 368648 | tf_op jit(solution)/shard_map/ppermute | solution.py:467
  20.8 1.4 %collective-permute-start.5 = (f32[3,16,640]{2,1,0:T(8,128)S(1)}, f32[3,16,640]{2,1,0:T(8,128)S(1)}, u32[]{:S(2)}, u32[]{:S(2)}) collective-permute-start(f32[3,16,640]{2,1,0:T(8,128)S(1)} %broadcast_select_fusion.1), channel_id=1, source_target_pairs={{0,1},{1,0},{2,3},{3,2},{4,5},{5,4},{6,7},{7,6},{8,9},{9,8},{10,11... | collective-permute-start | bytes 368648 | tf_op jit(solution)/shard_map/ppermute | solution.py:467
  33.8 1.4 %collective-permute-start.6 = (f32[3,16,512]{2,1,0:T(8,128)S(1)}, f32[3,16,512]{2,1,0:T(8,128)S(1)}, u32[]{:S(2)}, u32[]{:S(2)}) collective-permute-start(f32[3,16,512]{2,1,0:T(8,128)S(1)} %slice_select_fusion.1), channel_id=1, source_target_pairs={{0,1},{1,0},{2,3},{3,2},{4,5},{5,4},{6,7},{7,6},{8,9},{9,8},{10,11... | collective-permute-start | bytes 294920 | tf_op jit(solution)/shard_map/ppermute | solution.py:467
  35.2 4.9 %collective-permute-start.7 = (f32[3,16,512]{2,1,0:T(8,128)S(1)}, f32[3,16,512]{2,1,0:T(8,128)S(1)}, u32[]{:S(2)}, u32[]{:S(2)}) collective-permute-start(f32[3,16,512]{2,1,0:T(8,128)S(1)} %select_add_fusion), channel_id=1, source_target_pairs={{0,4},{1,5},{2,6},{3,7},{4,0},{5,1},{6,2},{7,3},{8,12},{9,13},{10,... | collective-permute-start | bytes 294920 | tf_op jit(solution)/shard_map/ppermute | solution.py:467
  40.1 6.6 %collective-permute-start.8 = (f32[3,16,512]{2,1,0:T(8,128)S(1)}, f32[3,16,512]{2,1,0:T(8,128)S(1)}, u32[]{:S(2)}, u32[]{:S(2)}) collective-permute-start(f32[3,16,512]{2,1,0:T(8,128)S(1)} %add.10), channel_id=1, source_target_pairs={{0,12},{1,13},{2,14},{3,15},{4,8},{5,9},{6,10},{7,11},{8,4},{9,5},... | collective-permute-start | bytes 294920 | tf_op jit(solution)/shard_map/ppermute | solution.py:467
  46.8 4.3 %collective-permute-start.9 = (f32[2,16,512]{2,1,0:T(8,128)S(1)}, f32[2,16,512]{2,1,0:T(8,128)S(1)}, u32[]{:S(2)}, u32[]{:S(2)}) collective-permute-start(f32[2,16,512]{2,1,0:T(8,128)S(1)} %pad_maximum_fusion.1), channel_id=1, source_target_pairs={{0,2},{1,3},{2,0},{3,1},{4,6},{5,7},{6,4},{7,5},{8,10},{9,11},{10,... | collective-permute-start | bytes 196616 | tf_op jit(solution)/shard_map/ppermute | solution.py:467
  51.2 1.3 %collective-permute-start.10 = (f32[16,1024]{1,0:T(8,128)S(1)}, f32[16,1024]{1,0:T(8,128)S(1)}, u32[]{:S(2)}, u32[]{:S(2)}) collective-permute-start(f32[16,1024]{1,0:T(8,128)S(1)} %get-tuple-element.29), channel_id=1, source_target_pairs={{0,1},{1,0},{2,3},{3,2},{4,5},{5,4},{6,7},{7,6},{8,9},{9,8},{10,11... | collective-permute-start | bytes 196616 | tf_op jit(solution)/shard_map/ppermute | solution.py:467

commit v6 on v5

--- a/solution.py
+++ b/solution.py
@@ -10,6 +10,7 @@
 
 lens_rate = 3.0
 wave_rate = 0.5
+greatest_slowness = 2.0
 directions = ((1, 0), (0, 1), (1, 1), (1, -1))
 LANES = 128
 SUB = 8
@@ -20,16 +21,21 @@
 PI_2 = (1.5703125, 4.837512969970703125e-4, 7.54978995489188216e-8)
 
 
+def small_cos_sin(r):
+    r2 = r * r
+    s = r + r * r2 * (-1.6666654611e-1 + r2 * (8.3321608736e-3 + r2 * -1.9515295891e-4))
+    c = (1.0 - 0.5 * r2) + r2 * r2 * (
+        4.166664568298827e-2 + r2 * (-1.388731625493765e-3 + r2 * 2.443315711809948e-5)
+    )
+    return c, s
+
+
 def cos_sin(x):
     turns = jnp.floor(x * TWO_OVER_PI + 0.5)
     r = x - turns * PI_2[0]
     r = r - turns * PI_2[1]
     r = r - turns * PI_2[2]
-    r2 = r * r
-    s = r + r * r2 * (-1.6666654611e-1 + r2 * (8.3321608736e-3 + r2 * -1.9515295891e-4))
-    c = (1.0 - 0.5 * r2) + r2 * r2 * (
-        4.166664568298827e-2 + r2 * (-1.388731625493765e-3 + r2 * 2.443315711809948e-5)
-    )
+    c, s = small_cos_sin(r)
     quadrant = turns.astype(jnp.int32)
     odd = (quadrant & 1) == 1
     cos_value = jnp.where(odd, s, c)
@@ -47,15 +53,17 @@
     return lax.broadcasted_iota(jnp.int32, (SUB, LANES), 1)
 
 
-def interleave(blocks):
+def interleave(blocks, shifts=None):
     count = len(blocks)
     out = []
     for c in range(count):
         column = columns() * count + c
         pick, source = column & (LANES - 1), column >> (LANES.bit_length() - 1)
-        value = jnp.take_along_axis(blocks[0], pick, axis=1)
-        for b in range(1, count):
-            value = jnp.where(source == b, jnp.take_along_axis(blocks[b], pick, axis=1), value)
+        value = None
+        for b in range(count):
+            at = pick if shifts is None or shifts[b] is None else (pick + shifts[b]) & (LANES - 1)
+            found = jnp.take_along_axis(blocks[b], at, axis=1)
+            value = found if value is None else jnp.where(source == b, found, value)
         out.append(value)
     return out
 
@@ -132,7 +140,7 @@
         tail_of(out_ref, rows, strips + b)[...] = value
 
 
-def prepare(freq_total, rank, first_column, owner_ref, position_ref, block_of, taps_of, wave_of, results):
+def prepare(freq_total, rank, first_column, owner_ref, position_ref, window_of, taps_of, wave_of, results):
     field_ref, taps_out_ref, rate_ref, turn_ref = results
     freq_local, _, _, blocks, height, _ = field_ref.shape
     groups = height // SUB
@@ -152,8 +160,7 @@
     for f in range(freq_local):
         for part in range(2):
             for g in range(groups):
-                loaded = [block_of(f, part, g, b) for b in range(blocks)]
-                for b, value in enumerate(interleave(loaded)):
+                for b, value in enumerate(window_of(f, part, g)):
                     tile(field_ref, f, 1, part, b, g)[...] = -value if part else value
 
     src_row = position_ref[0].astype(jnp.float32)
@@ -180,9 +187,11 @@
     here = lax.axis_index("freq")
     first_column = jnp.where((here & NEAR_COLUMNS) != 0, receiver_ref.shape[3] - blocks * LANES, 0)
 
-    def block_of(f, part, g, b):
-        column = pl.ds(pl.multiple_of(first_column + LANES * b, LANES), LANES)
-        return receiver_ref[f, part, SUB * g : SUB * (g + 1), column]
+    def window_of(f, part, g):
+        starts = [pl.multiple_of(first_column + LANES * b, LANES) for b in range(blocks)]
+        return interleave(
+            [receiver_ref[f, part, SUB * g : SUB * (g + 1), pl.ds(start, LANES)] for start in starts]
+        )
 
     prepare(
         freq_total,
@@ -190,7 +199,7 @@
         first_column,
         owner_ref,
         position_ref,
-        block_of,
+        window_of,
         lambda f, d, i: taps_ref[f, d, i],
         lambda f, i: spectrum_ref[f, i],
         results,
@@ -214,20 +223,16 @@
         row = (2 * f + part) * height + SUB * g
         return packed_ref[row : row + SUB, LANES * b : LANES * (b + 1)]
 
-    def beside(f, part, g):
+    def window_of(f, part, g):
         i, at = divmod((2 * f + part) * groups + g, per)
-        value = tail_of(packed_ref, rows, i)[...]
-        if at:
-            value = pltpu.roll(value, LANES - border * at, 1)
-        value = jnp.where(lane < border, value, 0.0)
-        return jnp.where(upper, pltpu.roll(value, LANES - border, 1), value)
-
-    def block_of(f, part, g, b):
-        if b == 0:
-            return jnp.where(upper, beside(f, part, g), main(f, part, g, 0))
-        if b == blocks - 1:
-            return jnp.where(upper, main(f, part, g, b - 1), beside(f, part, g))
-        return jnp.where(upper, main(f, part, g, b - 1), main(f, part, g, b))
+        strip = tail_of(packed_ref, rows, i)[...]
+        mains = [main(f, part, g, b) for b in range(blocks - 1)]
+        found = [strip if b == 0 else mains[b - 1] for b in range(blocks)]
+        lower = mains + [strip]
+        shifts = [None] * blocks
+        shifts[0] = jnp.where(upper, border * (at + 1), 0)
+        shifts[-1] = jnp.where(upper, 0, border * at)
+        return interleave([jnp.where(upper, u, v) for u, v in zip(found, lower)], shifts)
 
     def scalar(i):
         value = tail_of(packed_ref, rows, strips + i // LANES)[...]
@@ -239,7 +244,7 @@
         first_column,
         owner_ref,
         position_ref,
-        block_of,
+        window_of,
         lambda f, d, i: scalar(f * taps_count + 6 * d + i),
         lambda f, i: scalar(freq_local * taps_count + 2 * f + i),
         results,
@@ -320,17 +325,25 @@
     for g in range(groups):
         take_slab(0, g)
 
-    def lens(t, get, first, count):
-        @pl.loop(first, first + count)
-        def _(f):
-            rate = rate_ref[f]
-            for g in range(groups):
-                for b in range(blocks):
-                    cos_value, sin_value = cos_sin(rate * v_ref[t, b, SUB * g : SUB * (g + 1), :])
+    def lens(t, get, first):
+        step_rate = lens_rate / freq_total
+        step = small_cos_sin if step_rate * greatest_slowness < math.pi / 4.0 else cos_sin
+        for g in range(groups):
+            for b in range(blocks):
+                slow = v_ref[t, b, SUB * g : SUB * (g + 1), :]
+                cos_value, sin_value = cos_sin(rate_ref[first] * slow)
+                if freq_own > 1:
+                    cos_step, sin_step = step(step_rate * slow)
+                for f in range(freq_own):
+                    if f:
+                        cos_value, sin_value = (
+                            cos_value * cos_step - sin_value * sin_step,
+                            sin_value * cos_step + cos_value * sin_step,
+                        )
                     for field in range(2):
-                        re, im = get(f, field, 0, b, g), get(f, field, 1, b, g)
-                        store(a_ref, f, field, 0, b, g, re * cos_value + im * sin_value)
-                        store(a_ref, f, field, 1, b, g, im * cos_value - re * sin_value)
+                        re, im = get(first + f, field, 0, b, g), get(first + f, field, 1, b, g)
+                        store(a_ref, first + f, field, 0, b, g, re * cos_value + im * sin_value)
+                        store(a_ref, first + f, field, 1, b, g, im * cos_value - re * sin_value)
 
     def filtered(src, f, field, b, g, d, taps):
         step_x, step_y = directions[d]
@@ -392,13 +405,15 @@
         def surface(f, field, part, b, g, ref=ref, first=first):
             return tile(ref, f - first, field, part, b, g)[...]
 
-        lens(0, surface, first, freq_own)
+        lens(0, surface, first)
 
     @pl.loop(0, levels)
     def _(t):
         @pl.when(t > 0)
         def _():
-            lens(t, lambda f, field, part, b, g: load(a_ref, f, field, part, b, g), 0, freq_local)
+            @pl.loop(0, 2)
+            def _(side):
+                lens(t, lambda f, field, part, b, g: load(a_ref, f, field, part, b, g), side * freq_own)
 
         depth_step(t)
 

time: 53.3 us -> 51.6 us (0.968)
  starting transfers between devices: 15.3 us -> 17.5 us
  Pallas kernels: 17.1 us -> 15.2 us
  waiting for transfers between devices: 18 us -> 16.1 us
    ppermute x11, starting transfers between devices: 15.3 us -> 17.5 us  [exchange(): return lax.ppermute(value, 'freq', [(i, i ^ mask) for i in range(size)])]
    ppermute x11, waiting for transfers between devices: 18 us -> 16.1 us  [exchange(): return lax.ppermute(value, 'freq', [(i, i ^ mask) for i in range(size)])]
    pallas_call x2, Pallas kernels: 4.77 us -> 3.41 us  [prepared(): pl.pallas_call(kernel, out_shape=(jax.ShapeDtypeStruct((freq_local, 2, 2,...]
    pallas_call x1, Pallas kernels: 11.5 us -> 10.9 us  [migrate(): pl.pallas_call(functools.partial(migrate_kernel, freq_total), out_shape=j...]
  transfers between devices with their start and end apart: 11 -> 11, of which waited for: 10 -> 11; matrix products, arithmetic and copies ran while one was open for 3% -> 3% of each run, Pallas kernels for 10% -> 8%
where the time goes in v6:
time: 51.6 us; the launch traced here: 51.4 us
  starting transfers between devices  17.5 us (34%)
  waiting for transfers between devices  16.1 us (31%)
  Pallas kernels  15.2 us (29%)
  other arithmetic  2.51 us (5%)
    ppermute x11, starting transfers between devices, exchange(): return lax.ppermute(value, 'freq', [(i, i ^ mask) for i in range(size)])  17.5 us
    ppermute x11, waiting for transfers between devices, exchange(): return lax.ppermute(value, 'freq', [(i, i ^ mask) for i in range(size)])  16.1 us
    pallas_call x1, Pallas kernels, migrate(): pl.pallas_call(functools.partial(migrate_kernel, freq_total), out_shape=j...  10.9 us
    pallas_call x2, Pallas kernels, prepared(): pl.pallas_call(kernel, out_shape=(jax.ShapeDtypeStruct((freq_local, 2, 2,...  3.41 us
  transfers between devices with their start and end apart: 11, of which 11 were waited for; matrix products, arithmetic and copies ran while one was open for 3% of the time, Pallas kernels for 8%

profile of v6, /device:TPU:0, one launch (start us, length us, event | category | flops | bytes accessed | tf_op | source)
XLA Modules:
  0.0 51.4 jit_solution(5616656306735448424)
XLA Ops:
  0.0 0.0 copy-start
  0.0 0.5 collective-permute-start
  0.5 0.9 %slice_select_fusion.3 = f32[1,16,1024]{2,1,0:T(8,128)S(1)} fusion(f32[1,32,1024]{2,1,0:T(8,128)} %param.9, pred[]{:T(512)S(6)} %ne.8), kind=kLoop, calls=%fused_computation.19 | loop fusion | flops 16384 | bytes 196609 | tf_op jit(solution)/shard_map/jit(_where)/select_n | solution.py:497
  1.3 0.3 collective-permute-done.slab_ref
  1.7 0.0 copy-start.1
  1.7 0.0 copy-start.3
  1.7 0.0 copy-start.2
  1.7 0.0 copy-start.4
  1.8 2.9 %collective-permute-start.2 = (f32[2,16,640]{2,1,0:T(8,128)S(1)}, f32[2,16,640]{2,1,0:T(8,128)S(1)}, u32[]{:S(2)}, u32[]{:S(2)}) collective-permute-start(f32[2,16,640]{2,1,0:T(8,128)S(1)} %get-tuple-element.31), channel_id=1, source_target_pairs={{0,2},{1,3},{2,0},{3,1},{4,6},{5,7},{6,4},{7,5},{8,10},{9,11},{10,... | collective-permute-start | bytes 245768 | tf_op jit(solution)/shard_map/ppermute | solution.py:482
  4.7 0.0 copy-done
  4.7 0.0 copy-done.1
  4.7 0.0 copy-done.3
  4.7 0.8 %shard_map.64.packed_ref = f32[136,512]{1,0:T(8,128)S(1)} custom-call(f32[2,4,6]{2,1,0:T(4,128)S(1)} %copy-done.1, f32[2,2]{1,0:T(2,128)S(1)} %copy-done.3, f32[2,2,32,1024]{3,2,1,0:T(8,128)S(1)} %copy-done, f32[32,1024]{1,0:T(8,128)S(1)} %collective-permute-done.slab_ref), custom_call_target="tpu_custom_call" | custom-call | bytes 557056 | tf_op jit(solution)/shard_map/pallas_call | solution.py:431
  5.5 0.0 copy-done.2
  5.5 0.0 copy-done.4
  5.5 1.5 %shard_map.65 = (f32[2,2,2,5,32,128]{5,4,3,2,1,0:T(8,128)S(1)}, f32[2,4,6,8,128]{4,3,2,1,0:T(8,128)S(1)}, f32[2,8,128]{2,1,0:T(8,128)S(1)}, s32[3,8,128]{2,1,0:T(8,128)S(1)}) custom-call(s32[3]{0:T(128)S(1)} %copy-done.2, s32[2]{0:T(128)S(1)} %copy-done.4, f32[2,4,6]{2,1,0:T(4,128)S(1)} %copy-done.1, f32[2,2]{1,0:T(2,128)S(1)} %copy-done.3, ...), custom_call_target="tpu_custom_call" | custom-call | flops 4096000 | bytes 983040 | tf_op jit(solution)/shard_map/pallas_call | solution.py:444
  7.1 0.3 compare_reduce_fusion.3
  7.4 0.1 collective-permute-done.2
  7.5 0.1 select_select_fusion
  7.6 1.9 %collective-permute-start.3 = (f32[3,16,640]{2,1,0:T(8,128)S(1)}, f32[3,16,640]{2,1,0:T(8,128)S(1)}, u32[]{:S(2)}, u32[]{:S(2)}) collective-permute-start(f32[3,16,640]{2,1,0:T(8,128)S(1)} %select_select_fusion), channel_id=1, source_target_pairs={{0,4},{1,5},{2,6},{3,7},{4,0},{5,1},{6,2},{7,3},{8,12},{9,13},{10,... | collective-permute-start | bytes 368648 | tf_op jit(solution)/shard_map/ppermute | solution.py:482
  9.4 1.5 %collective-permute-start.1 = (f32[136,512]{1,0:T(8,128)S(1)}, f32[136,512]{1,0:T(8,128)S(1)}, u32[]{:S(2)}, u32[]{:S(2)}) collective-permute-start(f32[136,512]{1,0:T(8,128)S(1)} %shard_map.64.packed_ref), channel_id=1, source_target_pairs={{0,2},{1,3},{2,0},{3,1},{4,6},{5,7},{6,4},{7,5},{8,10},{9,11},{10,... | collective-permute-start | bytes 835592 | tf_op jit(solution)/shard_map/ppermute | solution.py:482
  10.9 1.7 %collective-permute-done.3 = f32[3,16,640]{2,1,0:T(8,128)S(1)} collective-permute-done((f32[3,16,640]{2,1,0:T(8,128)S(1)}, f32[3,16,640]{2,1,0:T(8,128)S(1)}, u32[]{:S(2)}, u32[]{:S(2)}) %collective-permute-start.3) | collective-permute-done | bytes 122912 | tf_op jit(solution)/shard_map/ppermute | solution.py:482
  12.7 0.1 broadcast_select_fusion
  12.8 3.7 %collective-permute-start.4 = (f32[3,16,640]{2,1,0:T(8,128)S(1)}, f32[3,16,640]{2,1,0:T(8,128)S(1)}, u32[]{:S(2)}, u32[]{:S(2)}) collective-permute-start(f32[3,16,640]{2,1,0:T(8,128)S(1)} %broadcast_select_fusion), channel_id=1, source_target_pairs={{0,12},{1,13},{2,14},{3,15},{4,8},{5,9},{6,10},{7,11},{8,4},{9,5},... | collective-permute-start | bytes 368648 | tf_op jit(solution)/shard_map/ppermute | solution.py:482
  16.5 0.8 %collective-permute-done.1.packed_ref = f32[136,512]{1,0:T(8,128)S(1)} collective-permute-done((f32[136,512]{1,0:T(8,128)S(1)}, f32[136,512]{1,0:T(8,128)S(1)}, u32[]{:S(2)}, u32[]{:S(2)}) %collective-permute-start.1) | collective-permute-done | bytes 278560 | tf_op jit(solution)/shard_map/ppermute | solution.py:482
  17.3 1.9 %shard_map.66 = (f32[2,2,2,5,32,128]{5,4,3,2,1,0:T(8,128)S(1)}, f32[2,4,6,8,128]{4,3,2,1,0:T(8,128)S(1)}, f32[2,8,128]{2,1,0:T(8,128)S(1)}, s32[3,8,128]{2,1,0:T(8,128)S(1)}) custom-call(s32[3]{0:T(128)S(1)} %copy-done.2, s32[2]{0:T(128)S(1)} %copy-done.4, f32[136,512]{1,0:T(8,128)S(1)} %collective-permute-done.1.packed_ref), custom_call_target="tpu_custom_call" | custom-call | flops 4096000 | bytes 983040 | tf_op jit(solution)/shard_map/pallas_call | solution.py:444
  19.2 0.2 compare_reduce_fusion.4
  19.3 0.3 collective-permute-done.4
  19.6 0.1 broadcast_select_fusion.1
  19.7 0.1 collective-permute-start.5
  19.8 1.3 %collective-permute-done.5 = f32[3,16,640]{2,1,0:T(8,128)S(1)} collective-permute-done((f32[3,16,640]{2,1,0:T(8,128)S(1)}, f32[3,16,640]{2,1,0:T(8,128)S(1)}, u32[]{:S(2)}, u32[]{:S(2)}) %collective-permute-start.5) | collective-permute-done | bytes 122912 | tf_op jit(solution)/shard_map/ppermute | solution.py:482
  21.1 10.9 %shard_map.67 = f32[3,32,640]{2,1,0:T(8,128)S(1)} custom-call(f32[2,2,2,5,32,128]{5,4,3,2,1,0:T(8,128)S(1)} %get-tuple-element.13.own_ref, f32[2,4,6,8,128]{4,3,2,1,0:T(8,128)S(1)} %get-tuple-element.14.own_taps_ref, f32[2,8,128]{2,1,0:T(8,128)S(1)} %get-tuple-element.15.own_rate_ref, f32[2,2,2,5,32,128]{5,4,3,2,1,0:T(8,128)S(1)} %get-tuple-element.16.near_ref, ...), custom_call_target="tpu_custom_call" | custom-call | tf_op jit(solution)/shard_map/pallas_call | solution.py:464
  32.1 0.2 collective-permute-start.6
  32.3 1.2 %collective-permute-done.6 = f32[3,16,512]{2,1,0:T(8,128)S(1)} collective-permute-done((f32[3,16,512]{2,1,0:T(8,128)S(1)}, f32[3,16,512]{2,1,0:T(8,128)S(1)}, u32[]{:S(2)}, u32[]{:S(2)}) %collective-permute-start.6) | collective-permute-done | bytes 98336 | tf_op jit(solution)/shard_map/ppermute | solution.py:482
  33.5 1.2 %collective-permute-start.7 = (f32[3,16,512]{2,1,0:T(8,128)S(1)}, f32[3,16,512]{2,1,0:T(8,128)S(1)}, u32[]{:S(2)}, u32[]{:S(2)}) collective-permute-start(f32[3,16,512]{2,1,0:T(8,128)S(1)} %select_add_fusion), channel_id=1, source_target_pairs={{0,4},{1,5},{2,6},{3,7},{4,0},{5,1},{6,2},{7,3},{8,12},{9,13},{10,... | collective-permute-start | bytes 294920 | tf_op jit(solution)/shard_map/ppermute | solution.py:482
  34.7 3.7 %collective-permute-done.7 = f32[3,16,512]{2,1,0:T(8,128)S(1)} collective-permute-done((f32[3,16,512]{2,1,0:T(8,128)S(1)}, f32[3,16,512]{2,1,0:T(8,128)S(1)}, u32[]{:S(2)}, u32[]{:S(2)}) %collective-permute-start.7) | collective-permute-done | bytes 98336 | tf_op jit(solution)/shard_map/ppermute | solution.py:482
  38.4 3.7 %collective-permute-start.8 = (f32[3,16,512]{2,1,0:T(8,128)S(1)}, f32[3,16,512]{2,1,0:T(8,128)S(1)}, u32[]{:S(2)}, u32[]{:S(2)}) collective-permute-start(f32[3,16,512]{2,1,0:T(8,128)S(1)} %add.10), channel_id=1, source_target_pairs={{0,12},{1,13},{2,14},{3,15},{4,8},{5,9},{6,10},{7,11},{8,4},{9,5},... | collective-permute-start | bytes 294920 | tf_op jit(solution)/shard_map/ppermute | solution.py:482
  42.2 2.8 %collective-permute-done.8 = f32[3,16,512]{2,1,0:T(8,128)S(1)} collective-permute-done((f32[3,16,512]{2,1,0:T(8,128)S(1)}, f32[3,16,512]{2,1,0:T(8,128)S(1)}, u32[]{:S(2)}, u32[]{:S(2)}) %collective-permute-start.8) | collective-permute-done | bytes 98336 | tf_op jit(solution)/shard_map/ppermute | solution.py:482
  45.0 0.1 select_reduce_fusion.3
  45.1 1.7 %collective-permute-start.9 = (f32[2,16,512]{2,1,0:T(8,128)S(1)}, f32[2,16,512]{2,1,0:T(8,128)S(1)}, u32[]{:S(2)}, u32[]{:S(2)}) collective-permute-start(f32[2,16,512]{2,1,0:T(8,128)S(1)} %pad_maximum_fusion.1), channel_id=1, source_target_pairs={{0,2},{1,3},{2,0},{3,1},{4,6},{5,7},{6,4},{7,5},{8,10},{9,11},{10,... | collective-permute-start | bytes 196616 | tf_op jit(solution)/shard_map/ppermute | solution.py:482
  46.8 2.6 %collective-permute-done.9 = f32[2,16,512]{2,1,0:T(8,128)S(1)} collective-permute-done((f32[2,16,512]{2,1,0:T(8,128)S(1)}, f32[2,16,512]{2,1,0:T(8,128)S(1)}, u32[]{:S(2)}, u32[]{:S(2)}) %collective-permute-start.9) | collective-permute-done | bytes 65568 | tf_op jit(solution)/shard_map/ppermute | solution.py:482
  49.5 0.1 collective-permute-start.10
  49.5 1.2 %collective-permute-done.10 = f32[16,1024]{1,0:T(8,128)S(1)} collective-permute-done((f32[16,1024]{1,0:T(8,128)S(1)}, f32[16,1024]{1,0:T(8,128)S(1)}, u32[]{:S(2)}, u32[]{:S(2)}) %collective-permute-start.10) | collective-permute-done | bytes 65568 | tf_op jit(solution)/shard_map/ppermute | solution.py:482
  50.8 0.7 %maximum_select_fusion.2 = f32[1,32,1024]{2,1,0:T(8,128)} fusion(f32[1,16,1024]{2,1,0:T(8,128)S(1)} %get-tuple-element.30, f32[1,16,1024]{2,1,0:T(8,128)S(1)} %bitcast.23, pred[]{:T(512)S(6)} %ne.8), kind=kLoop, calls=%fused_computation.5 | loop fusion | flops 98304 | bytes 262145 | tf_op jit(solution)/shard_map/jit(_where)/select_n | solution.py:506
  (13 shorter events, 0.2 us)
Async XLA Ops:
  0.0 4.7 %copy-start = (f32[2,2,32,1024]{3,2,1,0:T(8,128)S(1)}, f32[2,2,32,1024]{3,2,1,0:T(8,128)}, u32[]{:S(2)}) copy-start(f32[2,2,32,1024]{3,2,1,0:T(8,128)} %receiver_ref.3) | copy-start | bytes 1572868
  0.0 1.6 %collective-permute-start = (f32[32,1024]{1,0:T(8,128)}, f32[32,1024]{1,0:T(8,128)S(1)}, u32[]{:S(2)}, u32[]{:S(2)}) collective-permute-start(f32[32,1024]{1,0:T(8,128)} %bitcast.18), channel_id=1, source_target_pairs={{0,1},{1,0},{2,3},{3,2},{4,5},{5,4},{6,7},{7,6},{8,9},{9,8},{10,11... | collective-permute-start | bytes 393224 | tf_op jit(solution)/shard_map/ppermute | solution.py:482
  1.7 3.0 %copy-start.1 = (f32[2,4,6]{2,1,0:T(4,128)S(1)}, f32[2,4,6]{2,1,0:T(4,128)}, u32[]{:S(2)}) copy-start(f32[2,4,6]{2,1,0:T(4,128)} %taps_ref.3) | copy-start | bytes 580
  1.7 3.0 %copy-start.3 = (f32[2,2]{1,0:T(2,128)S(1)}, f32[2,2]{1,0:T(2,128)}, u32[]{:S(2)}) copy-start(f32[2,2]{1,0:T(2,128)} %spectrum_ref.3) | copy-start | bytes 52
  1.7 3.8 %copy-start.2 = (s32[3]{0:T(128)S(1)}, s32[3]{0:T(128)}, u32[]{:S(2)}) copy-start(s32[3]{0:T(128)} %owner_ref.3) | copy-start | bytes 40
  1.7 3.8 %copy-start.4 = (s32[2]{0:T(128)S(1)}, s32[2]{0:T(128)}, u32[]{:S(2)}) copy-start(s32[2]{0:T(128)} %position_ref.3) | copy-start | bytes 28
  1.8 5.7 %collective-permute-start.2 = (f32[2,16,640]{2,1,0:T(8,128)S(1)}, f32[2,16,640]{2,1,0:T(8,128)S(1)}, u32[]{:S(2)}, u32[]{:S(2)}) collective-permute-start(f32[2,16,640]{2,1,0:T(8,128)S(1)} %get-tuple-element.31), channel_id=1, source_target_pairs={{0,2},{1,3},{2,0},{3,1},{4,6},{5,7},{6,4},{7,5},{8,10},{9,11},{10,... | collective-permute-start | bytes 245768 | tf_op jit(solution)/shard_map/ppermute | solution.py:482
  7.6 5.1 %collective-permute-start.3 = (f32[3,16,640]{2,1,0:T(8,128)S(1)}, f32[3,16,640]{2,1,0:T(8,128)S(1)}, u32[]{:S(2)}, u32[]{:S(2)}) collective-permute-start(f32[3,16,640]{2,1,0:T(8,128)S(1)} %select_select_fusion), channel_id=1, source_target_pairs={{0,4},{1,5},{2,6},{3,7},{4,0},{5,1},{6,2},{7,3},{8,12},{9,13},{10,... | collective-permute-start | bytes 368648 | tf_op jit(solution)/shard_map/ppermute | solution.py:482
  9.4 7.9 %collective-permute-start.1 = (f32[136,512]{1,0:T(8,128)S(1)}, f32[136,512]{1,0:T(8,128)S(1)}, u32[]{:S(2)}, u32[]{:S(2)}) collective-permute-start(f32[136,512]{1,0:T(8,128)S(1)} %shard_map.64.packed_ref), channel_id=1, source_target_pairs={{0,2},{1,3},{2,0},{3,1},{4,6},{5,7},{6,4},{7,5},{8,10},{9,11},{10,... | collective-permute-start | bytes 835592 | tf_op jit(solution)/shard_map/ppermute | solution.py:482
  12.8 6.8 %collective-permute-start.4 = (f32[3,16,640]{2,1,0:T(8,128)S(1)}, f32[3,16,640]{2,1,0:T(8,128)S(1)}, u32[]{:S(2)}, u32[]{:S(2)}) collective-permute-start(f32[3,16,640]{2,1,0:T(8,128)S(1)} %broadcast_select_fusion), channel_id=1, source_target_pairs={{0,12},{1,13},{2,14},{3,15},{4,8},{5,9},{6,10},{7,11},{8,4},{9,5},... | collective-permute-start | bytes 368648 | tf_op jit(solution)/shard_map/ppermute | solution.py:482
  19.7 1.4 %collective-permute-start.5 = (f32[3,16,640]{2,1,0:T(8,128)S(1)}, f32[3,16,640]{2,1,0:T(8,128)S(1)}, u32[]{:S(2)}, u32[]{:S(2)}) collective-permute-start(f32[3,16,640]{2,1,0:T(8,128)S(1)} %broadcast_select_fusion.1), channel_id=1, source_target_pairs={{0,1},{1,0},{2,3},{3,2},{4,5},{5,4},{6,7},{7,6},{8,9},{9,8},{10,11... | collective-permute-start | bytes 368648 | tf_op jit(solution)/shard_map/ppermute | solution.py:482
  32.1 1.4 %collective-permute-start.6 = (f32[3,16,512]{2,1,0:T(8,128)S(1)}, f32[3,16,512]{2,1,0:T(8,128)S(1)}, u32[]{:S(2)}, u32[]{:S(2)}) collective-permute-start(f32[3,16,512]{2,1,0:T(8,128)S(1)} %slice_select_fusion.1), channel_id=1, source_target_pairs={{0,1},{1,0},{2,3},{3,2},{4,5},{5,4},{6,7},{7,6},{8,9},{9,8},{10,11... | collective-permute-start | bytes 294920 | tf_op jit(solution)/shard_map/ppermute | solution.py:482
  33.5 4.9 %collective-permute-start.7 = (f32[3,16,512]{2,1,0:T(8,128)S(1)}, f32[3,16,512]{2,1,0:T(8,128)S(1)}, u32[]{:S(2)}, u32[]{:S(2)}) collective-permute-start(f32[3,16,512]{2,1,0:T(8,128)S(1)} %select_add_fusion), channel_id=1, source_target_pairs={{0,4},{1,5},{2,6},{3,7},{4,0},{5,1},{6,2},{7,3},{8,12},{9,13},{10,... | collective-permute-start | bytes 294920 | tf_op jit(solution)/shard_map/ppermute | solution.py:482
  38.4 6.5 %collective-permute-start.8 = (f32[3,16,512]{2,1,0:T(8,128)S(1)}, f32[3,16,512]{2,1,0:T(8,128)S(1)}, u32[]{:S(2)}, u32[]{:S(2)}) collective-permute-start(f32[3,16,512]{2,1,0:T(8,128)S(1)} %add.10), channel_id=1, source_target_pairs={{0,12},{1,13},{2,14},{3,15},{4,8},{5,9},{6,10},{7,11},{8,4},{9,5},... | collective-permute-start | bytes 294920 | tf_op jit(solution)/shard_map/ppermute | solution.py:482
  45.1 4.3 %collective-permute-start.9 = (f32[2,16,512]{2,1,0:T(8,128)S(1)}, f32[2,16,512]{2,1,0:T(8,128)S(1)}, u32[]{:S(2)}, u32[]{:S(2)}) collective-permute-start(f32[2,16,512]{2,1,0:T(8,128)S(1)} %pad_maximum_fusion.1), channel_id=1, source_target_pairs={{0,2},{1,3},{2,0},{3,1},{4,6},{5,7},{6,4},{7,5},{8,10},{9,11},{10,... | collective-permute-start | bytes 196616 | tf_op jit(solution)/shard_map/ppermute | solution.py:482
  49.5 1.3 %collective-permute-start.10 = (f32[16,1024]{1,0:T(8,128)S(1)}, f32[16,1024]{1,0:T(8,128)S(1)}, u32[]{:S(2)}, u32[]{:S(2)}) collective-permute-start(f32[16,1024]{1,0:T(8,128)S(1)} %get-tuple-element.29), channel_id=1, source_target_pairs={{0,1},{1,0},{2,3},{3,2},{4,5},{5,4},{6,7},{7,6},{8,9},{9,8},{10,11... | collective-permute-start | bytes 196616 | tf_op jit(solution)/shard_map/ppermute | solution.py:482

commit v7 on v6

--- a/solution.py
+++ b/solution.py
@@ -14,6 +14,7 @@
 directions = ((1, 0), (0, 1), (1, 1), (1, -1))
 LANES = 128
 SUB = 8
+UNROLL = 2
 REACH = 2
 NEAR_ROWS = 1
 NEAR_COLUMNS = 2
@@ -355,12 +356,13 @@
         re, im = at(0, 0), at(1, 0)
         p1r, p1i = at(0, 1) + at(0, -1), at(1, 1) + at(1, -1)
         p2r, p2i = at(0, 2) + at(0, -2), at(1, 2) + at(1, -2)
-        out_re = (re * c0r - im * c0i) + (p1r * c1r - p1i * c1i) + (p2r * c2r - p2i * c2i)
-        out_im = (re * c0i + im * c0r) + (p1r * c1i + p1i * c1r) + (p2r * c2i + p2i * c2r)
-        return out_re, out_im
+        both = (re + im) * c0r + (p1r + p1i) * c1r + (p2r + p2i) * c2r
+        from_re = re * (c0i - c0r) + p1r * (c1i - c1r) + p2r * (c2i - c2r)
+        from_im = im * (c0r + c0i) + p1i * (c1r + c1i) + p2i * (c2r + c2i)
+        return both - from_im, both + from_re
 
     def sweep(src, dst, d, work=None, level=None):
-        @pl.loop(0, freq_local)
+        @pl.loop(0, freq_local, unroll=UNROLL)
         def _(f):
             taps = [taps_ref[f, d, i] for i in range(6)]
             if work is not None:
@@ -378,7 +380,7 @@
                                 store(dst, f, field, part, b - blocks, g, edge)
 
     def last_sweep(src, dst, d, t):
-        @pl.loop(0, freq_local)
+        @pl.loop(0, freq_local, unroll=UNROLL)
         def _(f):
             taps = [taps_ref[f, d, i] for i in range(6)]
             for g in range(groups):

time: 51.6 us -> 50 us (0.969)
  Pallas kernels: 15.2 us -> 13.6 us
    pallas_call x1, Pallas kernels: 10.9 us -> 9.36 us  [migrate(): pl.pallas_call(functools.partial(migrate_kernel, freq_total), out_shape=j...]
where the time goes in v7:
time: 50 us; the launch traced here: 49.9 us
  starting transfers between devices  17.5 us (35%)
  waiting for transfers between devices  16.1 us (32%)
  Pallas kernels  13.6 us (27%)
  other arithmetic  2.51 us (5%)
    ppermute x11, starting transfers between devices, exchange(): return lax.ppermute(value, 'freq', [(i, i ^ mask) for i in range(size)])  17.5 us
    ppermute x11, waiting for transfers between devices, exchange(): return lax.ppermute(value, 'freq', [(i, i ^ mask) for i in range(size)])  16.1 us
    pallas_call x1, Pallas kernels, migrate(): pl.pallas_call(functools.partial(migrate_kernel, freq_total), out_shape=j...  9.36 us
    pallas_call x2, Pallas kernels, prepared(): pl.pallas_call(kernel, out_shape=(jax.ShapeDtypeStruct((freq_local, 2, 2,...  3.41 us
  transfers between devices with their start and end apart: 11, of which 11 were waited for; matrix products, arithmetic and copies ran while one was open for 3% of the time, Pallas kernels for 8%

profile of v7, /device:TPU:0, one launch (start us, length us, event | category | flops | bytes accessed | tf_op | source)
XLA Modules:
  0.0 49.9 jit_solution(11571081778332547897)
XLA Ops:
  0.0 0.0 copy-start
  0.0 0.5 collective-permute-start
  0.5 0.9 %slice_select_fusion.3 = f32[1,16,1024]{2,1,0:T(8,128)S(1)} fusion(f32[1,32,1024]{2,1,0:T(8,128)} %param.9, pred[]{:T(512)S(6)} %ne.8), kind=kLoop, calls=%fused_computation.19 | loop fusion | flops 16384 | bytes 196609 | tf_op jit(solution)/shard_map/jit(_where)/select_n | solution.py:499
  1.3 0.3 collective-permute-done.slab_ref
  1.7 0.0 copy-start.1
  1.7 0.0 copy-start.3
  1.7 0.0 copy-start.2
  1.7 0.0 copy-start.4
  1.8 2.9 %collective-permute-start.2 = (f32[2,16,640]{2,1,0:T(8,128)S(1)}, f32[2,16,640]{2,1,0:T(8,128)S(1)}, u32[]{:S(2)}, u32[]{:S(2)}) collective-permute-start(f32[2,16,640]{2,1,0:T(8,128)S(1)} %get-tuple-element.31), channel_id=1, source_target_pairs={{0,2},{1,3},{2,0},{3,1},{4,6},{5,7},{6,4},{7,5},{8,10},{9,11},{10,... | collective-permute-start | bytes 245768 | tf_op jit(solution)/shard_map/ppermute | solution.py:484
  4.7 0.0 copy-done
  4.7 0.0 copy-done.1
  4.7 0.0 copy-done.3
  4.7 0.8 %shard_map.64.packed_ref = f32[136,512]{1,0:T(8,128)S(1)} custom-call(f32[2,4,6]{2,1,0:T(4,128)S(1)} %copy-done.1, f32[2,2]{1,0:T(2,128)S(1)} %copy-done.3, f32[2,2,32,1024]{3,2,1,0:T(8,128)S(1)} %copy-done, f32[32,1024]{1,0:T(8,128)S(1)} %collective-permute-done.slab_ref), custom_call_target="tpu_custom_call" | custom-call | bytes 557056 | tf_op jit(solution)/shard_map/pallas_call | solution.py:433
  5.5 0.0 copy-done.2
  5.5 0.0 copy-done.4
  5.5 1.5 %shard_map.65 = (f32[2,2,2,5,32,128]{5,4,3,2,1,0:T(8,128)S(1)}, f32[2,4,6,8,128]{4,3,2,1,0:T(8,128)S(1)}, f32[2,8,128]{2,1,0:T(8,128)S(1)}, s32[3,8,128]{2,1,0:T(8,128)S(1)}) custom-call(s32[3]{0:T(128)S(1)} %copy-done.2, s32[2]{0:T(128)S(1)} %copy-done.4, f32[2,4,6]{2,1,0:T(4,128)S(1)} %copy-done.1, f32[2,2]{1,0:T(2,128)S(1)} %copy-done.3, ...), custom_call_target="tpu_custom_call" | custom-call | flops 4096000 | bytes 983040 | tf_op jit(solution)/shard_map/pallas_call | solution.py:446
  7.1 0.3 compare_reduce_fusion.3
  7.4 0.1 collective-permute-done.2
  7.5 0.1 select_select_fusion
  7.6 1.9 %collective-permute-start.3 = (f32[3,16,640]{2,1,0:T(8,128)S(1)}, f32[3,16,640]{2,1,0:T(8,128)S(1)}, u32[]{:S(2)}, u32[]{:S(2)}) collective-permute-start(f32[3,16,640]{2,1,0:T(8,128)S(1)} %select_select_fusion), channel_id=1, source_target_pairs={{0,4},{1,5},{2,6},{3,7},{4,0},{5,1},{6,2},{7,3},{8,12},{9,13},{10,... | collective-permute-start | bytes 368648 | tf_op jit(solution)/shard_map/ppermute | solution.py:484
  9.4 1.5 %collective-permute-start.1 = (f32[136,512]{1,0:T(8,128)S(1)}, f32[136,512]{1,0:T(8,128)S(1)}, u32[]{:S(2)}, u32[]{:S(2)}) collective-permute-start(f32[136,512]{1,0:T(8,128)S(1)} %shard_map.64.packed_ref), channel_id=1, source_target_pairs={{0,2},{1,3},{2,0},{3,1},{4,6},{5,7},{6,4},{7,5},{8,10},{9,11},{10,... | collective-permute-start | bytes 835592 | tf_op jit(solution)/shard_map/ppermute | solution.py:484
  10.9 1.7 %collective-permute-done.3 = f32[3,16,640]{2,1,0:T(8,128)S(1)} collective-permute-done((f32[3,16,640]{2,1,0:T(8,128)S(1)}, f32[3,16,640]{2,1,0:T(8,128)S(1)}, u32[]{:S(2)}, u32[]{:S(2)}) %collective-permute-start.3) | collective-permute-done | bytes 122912 | tf_op jit(solution)/shard_map/ppermute | solution.py:484
  12.7 0.1 broadcast_select_fusion
  12.8 3.7 %collective-permute-start.4 = (f32[3,16,640]{2,1,0:T(8,128)S(1)}, f32[3,16,640]{2,1,0:T(8,128)S(1)}, u32[]{:S(2)}, u32[]{:S(2)}) collective-permute-start(f32[3,16,640]{2,1,0:T(8,128)S(1)} %broadcast_select_fusion), channel_id=1, source_target_pairs={{0,12},{1,13},{2,14},{3,15},{4,8},{5,9},{6,10},{7,11},{8,4},{9,5},... | collective-permute-start | bytes 368648 | tf_op jit(solution)/shard_map/ppermute | solution.py:484
  16.5 0.8 %collective-permute-done.1.packed_ref = f32[136,512]{1,0:T(8,128)S(1)} collective-permute-done((f32[136,512]{1,0:T(8,128)S(1)}, f32[136,512]{1,0:T(8,128)S(1)}, u32[]{:S(2)}, u32[]{:S(2)}) %collective-permute-start.1) | collective-permute-done | bytes 278560 | tf_op jit(solution)/shard_map/ppermute | solution.py:484
  17.3 1.9 %shard_map.66 = (f32[2,2,2,5,32,128]{5,4,3,2,1,0:T(8,128)S(1)}, f32[2,4,6,8,128]{4,3,2,1,0:T(8,128)S(1)}, f32[2,8,128]{2,1,0:T(8,128)S(1)}, s32[3,8,128]{2,1,0:T(8,128)S(1)}) custom-call(s32[3]{0:T(128)S(1)} %copy-done.2, s32[2]{0:T(128)S(1)} %copy-done.4, f32[136,512]{1,0:T(8,128)S(1)} %collective-permute-done.1.packed_ref), custom_call_target="tpu_custom_call" | custom-call | flops 4096000 | bytes 983040 | tf_op jit(solution)/shard_map/pallas_call | solution.py:446
  19.2 0.2 compare_reduce_fusion.4
  19.3 0.3 collective-permute-done.4
  19.6 0.1 broadcast_select_fusion.1
  19.7 0.1 collective-permute-start.5
  19.8 1.3 %collective-permute-done.5 = f32[3,16,640]{2,1,0:T(8,128)S(1)} collective-permute-done((f32[3,16,640]{2,1,0:T(8,128)S(1)}, f32[3,16,640]{2,1,0:T(8,128)S(1)}, u32[]{:S(2)}, u32[]{:S(2)}) %collective-permute-start.5) | collective-permute-done | bytes 122912 | tf_op jit(solution)/shard_map/ppermute | solution.py:484
  21.1 9.4 %shard_map.67 = f32[3,32,640]{2,1,0:T(8,128)S(1)} custom-call(f32[2,2,2,5,32,128]{5,4,3,2,1,0:T(8,128)S(1)} %get-tuple-element.13.own_ref, f32[2,4,6,8,128]{4,3,2,1,0:T(8,128)S(1)} %get-tuple-element.14.own_taps_ref, f32[2,8,128]{2,1,0:T(8,128)S(1)} %get-tuple-element.15.own_rate_ref, f32[2,2,2,5,32,128]{5,4,3,2,1,0:T(8,128)S(1)} %get-tuple-element.16.near_ref, ...), custom_call_target="tpu_custom_call" | custom-call | tf_op jit(solution)/shard_map/pallas_call | solution.py:466
  30.5 0.2 collective-permute-start.6
  30.7 1.2 %collective-permute-done.6 = f32[3,16,512]{2,1,0:T(8,128)S(1)} collective-permute-done((f32[3,16,512]{2,1,0:T(8,128)S(1)}, f32[3,16,512]{2,1,0:T(8,128)S(1)}, u32[]{:S(2)}, u32[]{:S(2)}) %collective-permute-start.6) | collective-permute-done | bytes 98336 | tf_op jit(solution)/shard_map/ppermute | solution.py:484
  31.9 1.2 %collective-permute-start.7 = (f32[3,16,512]{2,1,0:T(8,128)S(1)}, f32[3,16,512]{2,1,0:T(8,128)S(1)}, u32[]{:S(2)}, u32[]{:S(2)}) collective-permute-start(f32[3,16,512]{2,1,0:T(8,128)S(1)} %select_add_fusion), channel_id=1, source_target_pairs={{0,4},{1,5},{2,6},{3,7},{4,0},{5,1},{6,2},{7,3},{8,12},{9,13},{10,... | collective-permute-start | bytes 294920 | tf_op jit(solution)/shard_map/ppermute | solution.py:484
  33.1 3.7 %collective-permute-done.7 = f32[3,16,512]{2,1,0:T(8,128)S(1)} collective-permute-done((f32[3,16,512]{2,1,0:T(8,128)S(1)}, f32[3,16,512]{2,1,0:T(8,128)S(1)}, u32[]{:S(2)}, u32[]{:S(2)}) %collective-permute-start.7) | collective-permute-done | bytes 98336 | tf_op jit(solution)/shard_map/ppermute | solution.py:484
  36.9 3.7 %collective-permute-start.8 = (f32[3,16,512]{2,1,0:T(8,128)S(1)}, f32[3,16,512]{2,1,0:T(8,128)S(1)}, u32[]{:S(2)}, u32[]{:S(2)}) collective-permute-start(f32[3,16,512]{2,1,0:T(8,128)S(1)} %add.10), channel_id=1, source_target_pairs={{0,12},{1,13},{2,14},{3,15},{4,8},{5,9},{6,10},{7,11},{8,4},{9,5},... | collective-permute-start | bytes 294920 | tf_op jit(solution)/shard_map/ppermute | solution.py:484
  40.6 2.8 %collective-permute-done.8 = f32[3,16,512]{2,1,0:T(8,128)S(1)} collective-permute-done((f32[3,16,512]{2,1,0:T(8,128)S(1)}, f32[3,16,512]{2,1,0:T(8,128)S(1)}, u32[]{:S(2)}, u32[]{:S(2)}) %collective-permute-start.8) | collective-permute-done | bytes 98336 | tf_op jit(solution)/shard_map/ppermute | solution.py:484
  43.4 0.1 select_reduce_fusion.3
  43.5 1.7 %collective-permute-start.9 = (f32[2,16,512]{2,1,0:T(8,128)S(1)}, f32[2,16,512]{2,1,0:T(8,128)S(1)}, u32[]{:S(2)}, u32[]{:S(2)}) collective-permute-start(f32[2,16,512]{2,1,0:T(8,128)S(1)} %pad_maximum_fusion.1), channel_id=1, source_target_pairs={{0,2},{1,3},{2,0},{3,1},{4,6},{5,7},{6,4},{7,5},{8,10},{9,11},{10,... | collective-permute-start | bytes 196616 | tf_op jit(solution)/shard_map/ppermute | solution.py:484
  45.2 2.6 %collective-permute-done.9 = f32[2,16,512]{2,1,0:T(8,128)S(1)} collective-permute-done((f32[2,16,512]{2,1,0:T(8,128)S(1)}, f32[2,16,512]{2,1,0:T(8,128)S(1)}, u32[]{:S(2)}, u32[]{:S(2)}) %collective-permute-start.9) | collective-permute-done | bytes 65568 | tf_op jit(solution)/shard_map/ppermute | solution.py:484
  47.9 0.1 collective-permute-start.10
  48.0 1.2 %collective-permute-done.10 = f32[16,1024]{1,0:T(8,128)S(1)} collective-permute-done((f32[16,1024]{1,0:T(8,128)S(1)}, f32[16,1024]{1,0:T(8,128)S(1)}, u32[]{:S(2)}, u32[]{:S(2)}) %collective-permute-start.10) | collective-permute-done | bytes 65568 | tf_op jit(solution)/shard_map/ppermute | solution.py:484
  49.2 0.7 %maximum_select_fusion.2 = f32[1,32,1024]{2,1,0:T(8,128)} fusion(f32[1,16,1024]{2,1,0:T(8,128)S(1)} %get-tuple-element.30, f32[1,16,1024]{2,1,0:T(8,128)S(1)} %bitcast.23, pred[]{:T(512)S(6)} %ne.8), kind=kLoop, calls=%fused_computation.5 | loop fusion | flops 98304 | bytes 262145 | tf_op jit(solution)/shard_map/jit(_where)/select_n | solution.py:508
  (13 shorter events, 0.2 us)
Async XLA Ops:
  0.0 4.7 %copy-start = (f32[2,2,32,1024]{3,2,1,0:T(8,128)S(1)}, f32[2,2,32,1024]{3,2,1,0:T(8,128)}, u32[]{:S(2)}) copy-start(f32[2,2,32,1024]{3,2,1,0:T(8,128)} %receiver_ref.3) | copy-start | bytes 1572868
  0.0 1.6 %collective-permute-start = (f32[32,1024]{1,0:T(8,128)}, f32[32,1024]{1,0:T(8,128)S(1)}, u32[]{:S(2)}, u32[]{:S(2)}) collective-permute-start(f32[32,1024]{1,0:T(8,128)} %bitcast.18), channel_id=1, source_target_pairs={{0,1},{1,0},{2,3},{3,2},{4,5},{5,4},{6,7},{7,6},{8,9},{9,8},{10,11... | collective-permute-start | bytes 393224 | tf_op jit(solution)/shard_map/ppermute | solution.py:484
  1.7 3.0 %copy-start.1 = (f32[2,4,6]{2,1,0:T(4,128)S(1)}, f32[2,4,6]{2,1,0:T(4,128)}, u32[]{:S(2)}) copy-start(f32[2,4,6]{2,1,0:T(4,128)} %taps_ref.3) | copy-start | bytes 580
  1.7 3.0 %copy-start.3 = (f32[2,2]{1,0:T(2,128)S(1)}, f32[2,2]{1,0:T(2,128)}, u32[]{:S(2)}) copy-start(f32[2,2]{1,0:T(2,128)} %spectrum_ref.3) | copy-start | bytes 52
  1.7 3.8 %copy-start.2 = (s32[3]{0:T(128)S(1)}, s32[3]{0:T(128)}, u32[]{:S(2)}) copy-start(s32[3]{0:T(128)} %owner_ref.3) | copy-start | bytes 40
  1.7 3.8 %copy-start.4 = (s32[2]{0:T(128)S(1)}, s32[2]{0:T(128)}, u32[]{:S(2)}) copy-start(s32[2]{0:T(128)} %position_ref.3) | copy-start | bytes 28
  1.8 5.7 %collective-permute-start.2 = (f32[2,16,640]{2,1,0:T(8,128)S(1)}, f32[2,16,640]{2,1,0:T(8,128)S(1)}, u32[]{:S(2)}, u32[]{:S(2)}) collective-permute-start(f32[2,16,640]{2,1,0:T(8,128)S(1)} %get-tuple-element.31), channel_id=1, source_target_pairs={{0,2},{1,3},{2,0},{3,1},{4,6},{5,7},{6,4},{7,5},{8,10},{9,11},{10,... | collective-permute-start | bytes 245768 | tf_op jit(solution)/shard_map/ppermute | solution.py:484
  7.6 5.1 %collective-permute-start.3 = (f32[3,16,640]{2,1,0:T(8,128)S(1)}, f32[3,16,640]{2,1,0:T(8,128)S(1)}, u32[]{:S(2)}, u32[]{:S(2)}) collective-permute-start(f32[3,16,640]{2,1,0:T(8,128)S(1)} %select_select_fusion), channel_id=1, source_target_pairs={{0,4},{1,5},{2,6},{3,7},{4,0},{5,1},{6,2},{7,3},{8,12},{9,13},{10,... | collective-permute-start | bytes 368648 | tf_op jit(solution)/shard_map/ppermute | solution.py:484
  9.4 7.9 %collective-permute-start.1 = (f32[136,512]{1,0:T(8,128)S(1)}, f32[136,512]{1,0:T(8,128)S(1)}, u32[]{:S(2)}, u32[]{:S(2)}) collective-permute-start(f32[136,512]{1,0:T(8,128)S(1)} %shard_map.64.packed_ref), channel_id=1, source_target_pairs={{0,2},{1,3},{2,0},{3,1},{4,6},{5,7},{6,4},{7,5},{8,10},{9,11},{10,... | collective-permute-start | bytes 835592 | tf_op jit(solution)/shard_map/ppermute | solution.py:484
  12.8 6.8 %collective-permute-start.4 = (f32[3,16,640]{2,1,0:T(8,128)S(1)}, f32[3,16,640]{2,1,0:T(8,128)S(1)}, u32[]{:S(2)}, u32[]{:S(2)}) collective-permute-start(f32[3,16,640]{2,1,0:T(8,128)S(1)} %broadcast_select_fusion), channel_id=1, source_target_pairs={{0,12},{1,13},{2,14},{3,15},{4,8},{5,9},{6,10},{7,11},{8,4},{9,5},... | collective-permute-start | bytes 368648 | tf_op jit(solution)/shard_map/ppermute | solution.py:484
  19.7 1.4 %collective-permute-start.5 = (f32[3,16,640]{2,1,0:T(8,128)S(1)}, f32[3,16,640]{2,1,0:T(8,128)S(1)}, u32[]{:S(2)}, u32[]{:S(2)}) collective-permute-start(f32[3,16,640]{2,1,0:T(8,128)S(1)} %broadcast_select_fusion.1), channel_id=1, source_target_pairs={{0,1},{1,0},{2,3},{3,2},{4,5},{5,4},{6,7},{7,6},{8,9},{9,8},{10,11... | collective-permute-start | bytes 368648 | tf_op jit(solution)/shard_map/ppermute | solution.py:484
  30.5 1.4 %collective-permute-start.6 = (f32[3,16,512]{2,1,0:T(8,128)S(1)}, f32[3,16,512]{2,1,0:T(8,128)S(1)}, u32[]{:S(2)}, u32[]{:S(2)}) collective-permute-start(f32[3,16,512]{2,1,0:T(8,128)S(1)} %slice_select_fusion.1), channel_id=1, source_target_pairs={{0,1},{1,0},{2,3},{3,2},{4,5},{5,4},{6,7},{7,6},{8,9},{9,8},{10,11... | collective-permute-start | bytes 294920 | tf_op jit(solution)/shard_map/ppermute | solution.py:484
  31.9 4.9 %collective-permute-start.7 = (f32[3,16,512]{2,1,0:T(8,128)S(1)}, f32[3,16,512]{2,1,0:T(8,128)S(1)}, u32[]{:S(2)}, u32[]{:S(2)}) collective-permute-start(f32[3,16,512]{2,1,0:T(8,128)S(1)} %select_add_fusion), channel_id=1, source_target_pairs={{0,4},{1,5},{2,6},{3,7},{4,0},{5,1},{6,2},{7,3},{8,12},{9,13},{10,... | collective-permute-start | bytes 294920 | tf_op jit(solution)/shard_map/ppermute | solution.py:484
  36.9 6.5 %collective-permute-start.8 = (f32[3,16,512]{2,1,0:T(8,128)S(1)}, f32[3,16,512]{2,1,0:T(8,128)S(1)}, u32[]{:S(2)}, u32[]{:S(2)}) collective-permute-start(f32[3,16,512]{2,1,0:T(8,128)S(1)} %add.10), channel_id=1, source_target_pairs={{0,12},{1,13},{2,14},{3,15},{4,8},{5,9},{6,10},{7,11},{8,4},{9,5},... | collective-permute-start | bytes 294920 | tf_op jit(solution)/shard_map/ppermute | solution.py:484
  43.5 4.3 %collective-permute-start.9 = (f32[2,16,512]{2,1,0:T(8,128)S(1)}, f32[2,16,512]{2,1,0:T(8,128)S(1)}, u32[]{:S(2)}, u32[]{:S(2)}) collective-permute-start(f32[2,16,512]{2,1,0:T(8,128)S(1)} %pad_maximum_fusion.1), channel_id=1, source_target_pairs={{0,2},{1,3},{2,0},{3,1},{4,6},{5,7},{6,4},{7,5},{8,10},{9,11},{10,... | collective-permute-start | bytes 196616 | tf_op jit(solution)/shard_map/ppermute | solution.py:484
  47.9 1.3 %collective-permute-start.10 = (f32[16,1024]{1,0:T(8,128)S(1)}, f32[16,1024]{1,0:T(8,128)S(1)}, u32[]{:S(2)}, u32[]{:S(2)}) collective-permute-start(f32[16,1024]{1,0:T(8,128)S(1)} %get-tuple-element.29), channel_id=1, source_target_pairs={{0,1},{1,0},{2,3},{3,2},{4,5},{5,4},{6,7},{7,6},{8,9},{9,8},{10,11... | collective-permute-start | bytes 196616 | tf_op jit(solution)/shard_map/ppermute | solution.py:484

commit v8 on v7

--- a/solution.py
+++ b/solution.py
@@ -326,25 +326,35 @@
     for g in range(groups):
         take_slab(0, g)
 
-    def lens(t, get, first):
+    def lens(t, get):
         step_rate = lens_rate / freq_total
         step = small_cos_sin if step_rate * greatest_slowness < math.pi / 4.0 else cos_sin
+        apart = NEAR_COLUMNS * freq_own
+        side = jnp.where((lax.axis_index("freq") & NEAR_COLUMNS) != 0, -1.0, 1.0)
+
+        def plus(one, other):
+            return one[0] * other[0] - one[1] * other[1], one[1] * other[0] + one[0] * other[1]
+
         for g in range(groups):
             for b in range(blocks):
                 slow = v_ref[t, b, SUB * g : SUB * (g + 1), :]
-                cos_value, sin_value = cos_sin(rate_ref[first] * slow)
-                if freq_own > 1:
-                    cos_step, sin_step = step(step_rate * slow)
-                for f in range(freq_own):
-                    if f:
-                        cos_value, sin_value = (
-                            cos_value * cos_step - sin_value * sin_step,
-                            sin_value * cos_step + cos_value * sin_step,
-                        )
+                by_one = step(step_rate * slow)
+                far = by_one
+                if apart & (apart - 1) == 0:
+                    for _ in range(apart.bit_length() - 1):
+                        far = far[0] * far[0] - far[1] * far[1], 2.0 * far[0] * far[1]
+                else:
+                    far = cos_sin(apart * step_rate * slow)
+                own = [cos_sin(rate_ref[0] * slow)]
+                near = [plus(own[0], (far[0], side * far[1]))]
+                for _ in range(1, freq_own):
+                    own.append(plus(own[-1], by_one))
+                    near.append(plus(near[-1], by_one))
+                for f, (cos_value, sin_value) in enumerate(own + near):
                     for field in range(2):
-                        re, im = get(first + f, field, 0, b, g), get(first + f, field, 1, b, g)
-                        store(a_ref, first + f, field, 0, b, g, re * cos_value + im * sin_value)
-                        store(a_ref, first + f, field, 1, b, g, im * cos_value - re * sin_value)
+                        re, im = get(f, field, 0, b, g), get(f, field, 1, b, g)
+                        store(a_ref, f, field, 0, b, g, re * cos_value + im * sin_value)
+                        store(a_ref, f, field, 1, b, g, im * cos_value - re * sin_value)
 
     def filtered(src, f, field, b, g, d, taps):
         step_x, step_y = directions[d]
@@ -401,21 +411,17 @@
         sweep(a_ref, b_ref, 2)
         last_sweep(b_ref, a_ref, 3, t)
 
-    for side, ref in enumerate((own_ref, near_ref)):
-        first = side * freq_own
-
-        def surface(f, field, part, b, g, ref=ref, first=first):
-            return tile(ref, f - first, field, part, b, g)[...]
-
-        lens(0, surface, first)
+    def surface(f, field, part, b, g):
+        ref = own_ref if f < freq_own else near_ref
+        return tile(ref, f % freq_own, field, part, b, g)[...]
+
+    lens(0, surface)
 
     @pl.loop(0, levels)
     def _(t):
         @pl.when(t > 0)
         def _():
-            @pl.loop(0, 2)
-            def _(side):
-                lens(t, lambda f, field, part, b, g: load(a_ref, f, field, part, b, g), side * freq_own)
+            lens(t, lambda f, field, part, b, g: load(a_ref, f, field, part, b, g))
 
         depth_step(t)
 

time: 50 us -> 49.7 us (level)
  transfers between devices with their start and end apart: 11 -> 11, of which waited for: 11 -> 11; matrix products, arithmetic and copies ran while one was open for 3% -> 3% of each run, Pallas kernels for 8% -> 9%
where the time goes in v8:
time: 49.7 us; the launch traced here: 49.6 us
  starting transfers between devices  17.5 us (35%)
  waiting for transfers between devices  16.1 us (32%)
  Pallas kernels  13.3 us (27%)
  other arithmetic  2.51 us (5%)
    ppermute x11, starting transfers between devices, exchange(): return lax.ppermute(value, 'freq', [(i, i ^ mask) for i in range(size)])  17.5 us
    ppermute x11, waiting for transfers between devices, exchange(): return lax.ppermute(value, 'freq', [(i, i ^ mask) for i in range(size)])  16.1 us
    pallas_call x1, Pallas kernels, migrate(): pl.pallas_call(functools.partial(migrate_kernel, freq_total), out_shape=j...  9.07 us
    pallas_call x2, Pallas kernels, prepared(): pl.pallas_call(kernel, out_shape=(jax.ShapeDtypeStruct((freq_local, 2, 2,...  3.41 us
  transfers between devices with their start and end apart: 11, of which 11 were waited for; matrix products, arithmetic and copies ran while one was open for 3% of the time, Pallas kernels for 9%

profile of v8, /device:TPU:0, one launch (start us, length us, event | category | flops | bytes accessed | tf_op | source)
XLA Modules:
  0.0 49.6 jit_solution(6365115458542950928)
XLA Ops:
  0.0 0.0 copy-start
  0.0 0.5 collective-permute-start
  0.5 0.9 %slice_select_fusion.3 = f32[1,16,1024]{2,1,0:T(8,128)S(1)} fusion(f32[1,32,1024]{2,1,0:T(8,128)} %param.9, pred[]{:T(512)S(6)} %ne.8), kind=kLoop, calls=%fused_computation.19 | loop fusion | flops 16384 | bytes 196609 | tf_op jit(solution)/shard_map/jit(_where)/select_n | solution.py:505
  1.3 0.3 collective-permute-done.slab_ref
  1.7 0.0 copy-start.1
  1.7 0.0 copy-start.3
  1.7 0.0 copy-start.2
  1.7 0.0 copy-start.4
  1.8 2.9 %collective-permute-start.2 = (f32[2,16,640]{2,1,0:T(8,128)S(1)}, f32[2,16,640]{2,1,0:T(8,128)S(1)}, u32[]{:S(2)}, u32[]{:S(2)}) collective-permute-start(f32[2,16,640]{2,1,0:T(8,128)S(1)} %get-tuple-element.31), channel_id=1, source_target_pairs={{0,2},{1,3},{2,0},{3,1},{4,6},{5,7},{6,4},{7,5},{8,10},{9,11},{10,... | collective-permute-start | bytes 245768 | tf_op jit(solution)/shard_map/ppermute | solution.py:490
  4.7 0.0 copy-done
  4.7 0.0 copy-done.1
  4.7 0.0 copy-done.3
  4.7 0.8 %shard_map.64.packed_ref = f32[136,512]{1,0:T(8,128)S(1)} custom-call(f32[2,4,6]{2,1,0:T(4,128)S(1)} %copy-done.1, f32[2,2]{1,0:T(2,128)S(1)} %copy-done.3, f32[2,2,32,1024]{3,2,1,0:T(8,128)S(1)} %copy-done, f32[32,1024]{1,0:T(8,128)S(1)} %collective-permute-done.slab_ref), custom_call_target="tpu_custom_call" | custom-call | bytes 557056 | tf_op jit(solution)/shard_map/pallas_call | solution.py:439
  5.5 0.0 copy-done.2
  5.5 0.0 copy-done.4
  5.5 1.5 %shard_map.65 = (f32[2,2,2,5,32,128]{5,4,3,2,1,0:T(8,128)S(1)}, f32[2,4,6,8,128]{4,3,2,1,0:T(8,128)S(1)}, f32[2,8,128]{2,1,0:T(8,128)S(1)}, s32[3,8,128]{2,1,0:T(8,128)S(1)}) custom-call(s32[3]{0:T(128)S(1)} %copy-done.2, s32[2]{0:T(128)S(1)} %copy-done.4, f32[2,4,6]{2,1,0:T(4,128)S(1)} %copy-done.1, f32[2,2]{1,0:T(2,128)S(1)} %copy-done.3, ...), custom_call_target="tpu_custom_call" | custom-call | flops 4096000 | bytes 983040 | tf_op jit(solution)/shard_map/pallas_call | solution.py:452
  7.1 0.3 compare_reduce_fusion.3
  7.4 0.1 collective-permute-done.2
  7.5 0.1 select_select_fusion
  7.6 1.9 %collective-permute-start.3 = (f32[3,16,640]{2,1,0:T(8,128)S(1)}, f32[3,16,640]{2,1,0:T(8,128)S(1)}, u32[]{:S(2)}, u32[]{:S(2)}) collective-permute-start(f32[3,16,640]{2,1,0:T(8,128)S(1)} %select_select_fusion), channel_id=1, source_target_pairs={{0,4},{1,5},{2,6},{3,7},{4,0},{5,1},{6,2},{7,3},{8,12},{9,13},{10,... | collective-permute-start | bytes 368648 | tf_op jit(solution)/shard_map/ppermute | solution.py:490
  9.4 1.5 %collective-permute-start.1 = (f32[136,512]{1,0:T(8,128)S(1)}, f32[136,512]{1,0:T(8,128)S(1)}, u32[]{:S(2)}, u32[]{:S(2)}) collective-permute-start(f32[136,512]{1,0:T(8,128)S(1)} %shard_map.64.packed_ref), channel_id=1, source_target_pairs={{0,2},{1,3},{2,0},{3,1},{4,6},{5,7},{6,4},{7,5},{8,10},{9,11},{10,... | collective-permute-start | bytes 835592 | tf_op jit(solution)/shard_map/ppermute | solution.py:490
  10.9 1.7 %collective-permute-done.3 = f32[3,16,640]{2,1,0:T(8,128)S(1)} collective-permute-done((f32[3,16,640]{2,1,0:T(8,128)S(1)}, f32[3,16,640]{2,1,0:T(8,128)S(1)}, u32[]{:S(2)}, u32[]{:S(2)}) %collective-permute-start.3) | collective-permute-done | bytes 122912 | tf_op jit(solution)/shard_map/ppermute | solution.py:490
  12.7 0.1 broadcast_select_fusion
  12.8 3.7 %collective-permute-start.4 = (f32[3,16,640]{2,1,0:T(8,128)S(1)}, f32[3,16,640]{2,1,0:T(8,128)S(1)}, u32[]{:S(2)}, u32[]{:S(2)}) collective-permute-start(f32[3,16,640]{2,1,0:T(8,128)S(1)} %broadcast_select_fusion), channel_id=1, source_target_pairs={{0,12},{1,13},{2,14},{3,15},{4,8},{5,9},{6,10},{7,11},{8,4},{9,5},... | collective-permute-start | bytes 368648 | tf_op jit(solution)/shard_map/ppermute | solution.py:490
  16.5 0.8 %collective-permute-done.1.packed_ref = f32[136,512]{1,0:T(8,128)S(1)} collective-permute-done((f32[136,512]{1,0:T(8,128)S(1)}, f32[136,512]{1,0:T(8,128)S(1)}, u32[]{:S(2)}, u32[]{:S(2)}) %collective-permute-start.1) | collective-permute-done | bytes 278560 | tf_op jit(solution)/shard_map/ppermute | solution.py:490
  17.3 1.9 %shard_map.66 = (f32[2,2,2,5,32,128]{5,4,3,2,1,0:T(8,128)S(1)}, f32[2,4,6,8,128]{4,3,2,1,0:T(8,128)S(1)}, f32[2,8,128]{2,1,0:T(8,128)S(1)}, s32[3,8,128]{2,1,0:T(8,128)S(1)}) custom-call(s32[3]{0:T(128)S(1)} %copy-done.2, s32[2]{0:T(128)S(1)} %copy-done.4, f32[136,512]{1,0:T(8,128)S(1)} %collective-permute-done.1.packed_ref), custom_call_target="tpu_custom_call" | custom-call | flops 4096000 | bytes 983040 | tf_op jit(solution)/shard_map/pallas_call | solution.py:452
  19.2 0.2 compare_reduce_fusion.4
  19.3 0.3 collective-permute-done.4
  19.6 0.1 broadcast_select_fusion.1
  19.7 0.1 collective-permute-start.5
  19.8 1.3 %collective-permute-done.5 = f32[3,16,640]{2,1,0:T(8,128)S(1)} collective-permute-done((f32[3,16,640]{2,1,0:T(8,128)S(1)}, f32[3,16,640]{2,1,0:T(8,128)S(1)}, u32[]{:S(2)}, u32[]{:S(2)}) %collective-permute-start.5) | collective-permute-done | bytes 122912 | tf_op jit(solution)/shard_map/ppermute | solution.py:490
  21.1 9.1 %shard_map.67 = f32[3,32,640]{2,1,0:T(8,128)S(1)} custom-call(f32[2,2,2,5,32,128]{5,4,3,2,1,0:T(8,128)S(1)} %get-tuple-element.13.own_ref, f32[2,4,6,8,128]{4,3,2,1,0:T(8,128)S(1)} %get-tuple-element.14.own_taps_ref, f32[2,8,128]{2,1,0:T(8,128)S(1)} %get-tuple-element.15.own_rate_ref, f32[2,2,2,5,32,128]{5,4,3,2,1,0:T(8,128)S(1)} %get-tuple-element.16.near_ref, ...), custom_call_target="tpu_custom_call" | custom-call | tf_op jit(solution)/shard_map/pallas_call | solution.py:472
  30.2 0.2 collective-permute-start.6
  30.5 1.2 %collective-permute-done.6 = f32[3,16,512]{2,1,0:T(8,128)S(1)} collective-permute-done((f32[3,16,512]{2,1,0:T(8,128)S(1)}, f32[3,16,512]{2,1,0:T(8,128)S(1)}, u32[]{:S(2)}, u32[]{:S(2)}) %collective-permute-start.6) | collective-permute-done | bytes 98336 | tf_op jit(solution)/shard_map/ppermute | solution.py:490
  31.6 1.2 %collective-permute-start.7 = (f32[3,16,512]{2,1,0:T(8,128)S(1)}, f32[3,16,512]{2,1,0:T(8,128)S(1)}, u32[]{:S(2)}, u32[]{:S(2)}) collective-permute-start(f32[3,16,512]{2,1,0:T(8,128)S(1)} %select_add_fusion), channel_id=1, source_target_pairs={{0,4},{1,5},{2,6},{3,7},{4,0},{5,1},{6,2},{7,3},{8,12},{9,13},{10,... | collective-permute-start | bytes 294920 | tf_op jit(solution)/shard_map/ppermute | solution.py:490
  32.9 3.7 %collective-permute-done.7 = f32[3,16,512]{2,1,0:T(8,128)S(1)} collective-permute-done((f32[3,16,512]{2,1,0:T(8,128)S(1)}, f32[3,16,512]{2,1,0:T(8,128)S(1)}, u32[]{:S(2)}, u32[]{:S(2)}) %collective-permute-start.7) | collective-permute-done | bytes 98336 | tf_op jit(solution)/shard_map/ppermute | solution.py:490
  36.6 3.7 %collective-permute-start.8 = (f32[3,16,512]{2,1,0:T(8,128)S(1)}, f32[3,16,512]{2,1,0:T(8,128)S(1)}, u32[]{:S(2)}, u32[]{:S(2)}) collective-permute-start(f32[3,16,512]{2,1,0:T(8,128)S(1)} %add.10), channel_id=1, source_target_pairs={{0,12},{1,13},{2,14},{3,15},{4,8},{5,9},{6,10},{7,11},{8,4},{9,5},... | collective-permute-start | bytes 294920 | tf_op jit(solution)/shard_map/ppermute | solution.py:490
  40.3 2.8 %collective-permute-done.8 = f32[3,16,512]{2,1,0:T(8,128)S(1)} collective-permute-done((f32[3,16,512]{2,1,0:T(8,128)S(1)}, f32[3,16,512]{2,1,0:T(8,128)S(1)}, u32[]{:S(2)}, u32[]{:S(2)}) %collective-permute-start.8) | collective-permute-done | bytes 98336 | tf_op jit(solution)/shard_map/ppermute | solution.py:490
  43.1 0.1 select_reduce_fusion.3
  43.2 1.7 %collective-permute-start.9 = (f32[2,16,512]{2,1,0:T(8,128)S(1)}, f32[2,16,512]{2,1,0:T(8,128)S(1)}, u32[]{:S(2)}, u32[]{:S(2)}) collective-permute-start(f32[2,16,512]{2,1,0:T(8,128)S(1)} %pad_maximum_fusion.1), channel_id=1, source_target_pairs={{0,2},{1,3},{2,0},{3,1},{4,6},{5,7},{6,4},{7,5},{8,10},{9,11},{10,... | collective-permute-start | bytes 196616 | tf_op jit(solution)/shard_map/ppermute | solution.py:490
  44.9 2.6 %collective-permute-done.9 = f32[2,16,512]{2,1,0:T(8,128)S(1)} collective-permute-done((f32[2,16,512]{2,1,0:T(8,128)S(1)}, f32[2,16,512]{2,1,0:T(8,128)S(1)}, u32[]{:S(2)}, u32[]{:S(2)}) %collective-permute-start.9) | collective-permute-done | bytes 65568 | tf_op jit(solution)/shard_map/ppermute | solution.py:490
  47.6 0.1 collective-permute-start.10
  47.7 1.2 %collective-permute-done.10 = f32[16,1024]{1,0:T(8,128)S(1)} collective-permute-done((f32[16,1024]{1,0:T(8,128)S(1)}, f32[16,1024]{1,0:T(8,128)S(1)}, u32[]{:S(2)}, u32[]{:S(2)}) %collective-permute-start.10) | collective-permute-done | bytes 65568 | tf_op jit(solution)/shard_map/ppermute | solution.py:490
  48.9 0.7 %maximum_select_fusion.2 = f32[1,32,1024]{2,1,0:T(8,128)} fusion(f32[1,16,1024]{2,1,0:T(8,128)S(1)} %get-tuple-element.30, f32[1,16,1024]{2,1,0:T(8,128)S(1)} %bitcast.23, pred[]{:T(512)S(6)} %ne.8), kind=kLoop, calls=%fused_computation.5 | loop fusion | flops 98304 | bytes 262145 | tf_op jit(solution)/shard_map/jit(_where)/select_n | solution.py:514
  (13 shorter events, 0.2 us)
Async XLA Ops:
  0.0 4.7 %copy-start = (f32[2,2,32,1024]{3,2,1,0:T(8,128)S(1)}, f32[2,2,32,1024]{3,2,1,0:T(8,128)}, u32[]{:S(2)}) copy-start(f32[2,2,32,1024]{3,2,1,0:T(8,128)} %receiver_ref.3) | copy-start | bytes 1572868
  0.0 1.6 %collective-permute-start = (f32[32,1024]{1,0:T(8,128)}, f32[32,1024]{1,0:T(8,128)S(1)}, u32[]{:S(2)}, u32[]{:S(2)}) collective-permute-start(f32[32,1024]{1,0:T(8,128)} %bitcast.18), channel_id=1, source_target_pairs={{0,1},{1,0},{2,3},{3,2},{4,5},{5,4},{6,7},{7,6},{8,9},{9,8},{10,11... | collective-permute-start | bytes 393224 | tf_op jit(solution)/shard_map/ppermute | solution.py:490
  1.7 3.0 %copy-start.1 = (f32[2,4,6]{2,1,0:T(4,128)S(1)}, f32[2,4,6]{2,1,0:T(4,128)}, u32[]{:S(2)}) copy-start(f32[2,4,6]{2,1,0:T(4,128)} %taps_ref.3) | copy-start | bytes 580
  1.7 3.0 %copy-start.3 = (f32[2,2]{1,0:T(2,128)S(1)}, f32[2,2]{1,0:T(2,128)}, u32[]{:S(2)}) copy-start(f32[2,2]{1,0:T(2,128)} %spectrum_ref.3) | copy-start | bytes 52
  1.7 3.8 %copy-start.2 = (s32[3]{0:T(128)S(1)}, s32[3]{0:T(128)}, u32[]{:S(2)}) copy-start(s32[3]{0:T(128)} %owner_ref.3) | copy-start | bytes 40
  1.7 3.8 %copy-start.4 = (s32[2]{0:T(128)S(1)}, s32[2]{0:T(128)}, u32[]{:S(2)}) copy-start(s32[2]{0:T(128)} %position_ref.3) | copy-start | bytes 28
  1.8 5.7 %collective-permute-start.2 = (f32[2,16,640]{2,1,0:T(8,128)S(1)}, f32[2,16,640]{2,1,0:T(8,128)S(1)}, u32[]{:S(2)}, u32[]{:S(2)}) collective-permute-start(f32[2,16,640]{2,1,0:T(8,128)S(1)} %get-tuple-element.31), channel_id=1, source_target_pairs={{0,2},{1,3},{2,0},{3,1},{4,6},{5,7},{6,4},{7,5},{8,10},{9,11},{10,... | collective-permute-start | bytes 245768 | tf_op jit(solution)/shard_map/ppermute | solution.py:490
  7.6 5.1 %collective-permute-start.3 = (f32[3,16,640]{2,1,0:T(8,128)S(1)}, f32[3,16,640]{2,1,0:T(8,128)S(1)}, u32[]{:S(2)}, u32[]{:S(2)}) collective-permute-start(f32[3,16,640]{2,1,0:T(8,128)S(1)} %select_select_fusion), channel_id=1, source_target_pairs={{0,4},{1,5},{2,6},{3,7},{4,0},{5,1},{6,2},{7,3},{8,12},{9,13},{10,... | collective-permute-start | bytes 368648 | tf_op jit(solution)/shard_map/ppermute | solution.py:490
  9.4 7.9 %collective-permute-start.1 = (f32[136,512]{1,0:T(8,128)S(1)}, f32[136,512]{1,0:T(8,128)S(1)}, u32[]{:S(2)}, u32[]{:S(2)}) collective-permute-start(f32[136,512]{1,0:T(8,128)S(1)} %shard_map.64.packed_ref), channel_id=1, source_target_pairs={{0,2},{1,3},{2,0},{3,1},{4,6},{5,7},{6,4},{7,5},{8,10},{9,11},{10,... | collective-permute-start | bytes 835592 | tf_op jit(solution)/shard_map/ppermute | solution.py:490
  12.8 6.8 %collective-permute-start.4 = (f32[3,16,640]{2,1,0:T(8,128)S(1)}, f32[3,16,640]{2,1,0:T(8,128)S(1)}, u32[]{:S(2)}, u32[]{:S(2)}) collective-permute-start(f32[3,16,640]{2,1,0:T(8,128)S(1)} %broadcast_select_fusion), channel_id=1, source_target_pairs={{0,12},{1,13},{2,14},{3,15},{4,8},{5,9},{6,10},{7,11},{8,4},{9,5},... | collective-permute-start | bytes 368648 | tf_op jit(solution)/shard_map/ppermute | solution.py:490
  19.7 1.4 %collective-permute-start.5 = (f32[3,16,640]{2,1,0:T(8,128)S(1)}, f32[3,16,640]{2,1,0:T(8,128)S(1)}, u32[]{:S(2)}, u32[]{:S(2)}) collective-permute-start(f32[3,16,640]{2,1,0:T(8,128)S(1)} %broadcast_select_fusion.1), channel_id=1, source_target_pairs={{0,1},{1,0},{2,3},{3,2},{4,5},{5,4},{6,7},{7,6},{8,9},{9,8},{10,11... | collective-permute-start | bytes 368648 | tf_op jit(solution)/shard_map/ppermute | solution.py:490
  30.2 1.4 %collective-permute-start.6 = (f32[3,16,512]{2,1,0:T(8,128)S(1)}, f32[3,16,512]{2,1,0:T(8,128)S(1)}, u32[]{:S(2)}, u32[]{:S(2)}) collective-permute-start(f32[3,16,512]{2,1,0:T(8,128)S(1)} %slice_select_fusion.1), channel_id=1, source_target_pairs={{0,1},{1,0},{2,3},{3,2},{4,5},{5,4},{6,7},{7,6},{8,9},{9,8},{10,11... | collective-permute-start | bytes 294920 | tf_op jit(solution)/shard_map/ppermute | solution.py:490
  31.6 4.9 %collective-permute-start.7 = (f32[3,16,512]{2,1,0:T(8,128)S(1)}, f32[3,16,512]{2,1,0:T(8,128)S(1)}, u32[]{:S(2)}, u32[]{:S(2)}) collective-permute-start(f32[3,16,512]{2,1,0:T(8,128)S(1)} %select_add_fusion), channel_id=1, source_target_pairs={{0,4},{1,5},{2,6},{3,7},{4,0},{5,1},{6,2},{7,3},{8,12},{9,13},{10,... | collective-permute-start | bytes 294920 | tf_op jit(solution)/shard_map/ppermute | solution.py:490
  36.6 6.5 %collective-permute-start.8 = (f32[3,16,512]{2,1,0:T(8,128)S(1)}, f32[3,16,512]{2,1,0:T(8,128)S(1)}, u32[]{:S(2)}, u32[]{:S(2)}) collective-permute-start(f32[3,16,512]{2,1,0:T(8,128)S(1)} %add.10), channel_id=1, source_target_pairs={{0,12},{1,13},{2,14},{3,15},{4,8},{5,9},{6,10},{7,11},{8,4},{9,5},... | collective-permute-start | bytes 294920 | tf_op jit(solution)/shard_map/ppermute | solution.py:490
  43.2 4.3 %collective-permute-start.9 = (f32[2,16,512]{2,1,0:T(8,128)S(1)}, f32[2,16,512]{2,1,0:T(8,128)S(1)}, u32[]{:S(2)}, u32[]{:S(2)}) collective-permute-start(f32[2,16,512]{2,1,0:T(8,128)S(1)} %pad_maximum_fusion.1), channel_id=1, source_target_pairs={{0,2},{1,3},{2,0},{3,1},{4,6},{5,7},{6,4},{7,5},{8,10},{9,11},{10,... | collective-permute-start | bytes 196616 | tf_op jit(solution)/shard_map/ppermute | solution.py:490
  47.6 1.3 %collective-permute-start.10 = (f32[16,1024]{1,0:T(8,128)S(1)}, f32[16,1024]{1,0:T(8,128)S(1)}, u32[]{:S(2)}, u32[]{:S(2)}) collective-permute-start(f32[16,1024]{1,0:T(8,128)S(1)} %get-tuple-element.29), channel_id=1, source_target_pairs={{0,1},{1,0},{2,3},{3,2},{4,5},{5,4},{6,7},{7,6},{8,9},{9,8},{10,11... | collective-permute-start | bytes 196616 | tf_op jit(solution)/shard_map/ppermute | solution.py:490

commit v9 on v8

--- a/solution.py
+++ b/solution.py
@@ -389,27 +389,34 @@
                                 edge = jnp.where(not_first, pltpu.roll(value, 1, 1), 0.0)
                                 store(dst, f, field, part, b - blocks, g, edge)
 
-    def last_sweep(src, dst, d, t):
+    def last_sweep(src, dst, d, t, more):
         @pl.loop(0, freq_local, unroll=UNROLL)
         def _(f):
             taps = [taps_ref[f, d, i] for i in range(6)]
-            for g in range(groups):
-                for b in range(blocks):
+            for b in range(blocks):
+                for g in range(groups):
                     s_re, s_im = filtered(src, f, 0, b, g, d, taps)
                     r_re, r_im = filtered(src, f, 1, b, g, d, taps)
-                    store(dst, f, 0, 0, b, g, s_re)
-                    store(dst, f, 0, 1, b, g, s_im)
-                    store(dst, f, 1, 0, b, g, r_re)
-                    store(dst, f, 1, 1, b, g, r_im)
+                    if more:
+                        store(dst, f, 0, 0, b, g, s_re)
+                        store(dst, f, 0, 1, b, g, s_im)
+                        store(dst, f, 1, 0, b, g, r_re)
+                        store(dst, f, 1, 1, b, g, r_im)
                     term = s_re * r_re - s_im * r_im
                     at = (t, b, slice(SUB * g, SUB * (g + 1)))
                     c_ref[at] = jnp.where(f == 0, term, c_ref[at] + term)
 
-    def depth_step(t):
-        sweep(a_ref, b_ref, 0, take_slab, jnp.minimum(t + 1, levels - 1))
+    def depth_step(t, more):
+        if more:
+            sweep(a_ref, b_ref, 0, take_slab, t + 1)
+        else:
+            sweep(a_ref, b_ref, 0)
         sweep(b_ref, a_ref, 1, give_sum, jnp.maximum(t - 1, 0))
         sweep(a_ref, b_ref, 2)
-        last_sweep(b_ref, a_ref, 3, t)
+        last_sweep(b_ref, a_ref, 3, t, more)
+
+    def carried(f, field, part, b, g):
+        return load(a_ref, f, field, part, b, g)
 
     def surface(f, field, part, b, g):
         ref = own_ref if f < freq_own else near_ref
@@ -417,14 +424,17 @@
 
     lens(0, surface)
 
-    @pl.loop(0, levels)
+    @pl.loop(0, levels - 1)
     def _(t):
         @pl.when(t > 0)
         def _():
-            lens(t, lambda f, field, part, b, g: load(a_ref, f, field, part, b, g))
-
-        depth_step(t)
-
+            lens(t, carried)
+
+        depth_step(t, True)
+
+    if levels > 1:
+        lens(levels - 1, carried)
+    depth_step(levels - 1, False)
     for g in range(groups):
         give_sum(levels - 1, g)
 

time: 49.7 us -> 49.6 us (level)
  no operation moved by 1% of the time
where the time goes in v9:
time: 49.6 us; the launch traced here: 49.5 us
  starting transfers between devices  17.5 us (35%)
  waiting for transfers between devices  16.1 us (32%)
  Pallas kernels  13.2 us (27%)
  other arithmetic  2.51 us (5%)
    ppermute x11, starting transfers between devices, exchange(): return lax.ppermute(value, 'freq', [(i, i ^ mask) for i in range(size)])  17.5 us
    ppermute x11, waiting for transfers between devices, exchange(): return lax.ppermute(value, 'freq', [(i, i ^ mask) for i in range(size)])  16.1 us
    pallas_call x1, Pallas kernels, migrate(): pl.pallas_call(functools.partial(migrate_kernel, freq_total), out_shape=j...  8.99 us
    pallas_call x2, Pallas kernels, prepared(): pl.pallas_call(kernel, out_shape=(jax.ShapeDtypeStruct((freq_local, 2, 2,...  3.41 us
  transfers between devices with their start and end apart: 11, of which 11 were waited for; matrix products, arithmetic and copies ran while one was open for 3% of the time, Pallas kernels for 9%

profile of v9, /device:TPU:0, one launch (start us, length us, event | category | flops | bytes accessed | tf_op | source)
XLA Modules:
  0.0 49.5 jit_solution(6106266461853257544)
XLA Ops:
  0.0 0.0 copy-start
  0.0 0.5 collective-permute-start
  0.5 0.9 %slice_select_fusion.3 = f32[1,16,1024]{2,1,0:T(8,128)S(1)} fusion(f32[1,32,1024]{2,1,0:T(8,128)} %param.9, pred[]{:T(512)S(6)} %ne.8), kind=kLoop, calls=%fused_computation.19 | loop fusion | flops 16384 | bytes 196609 | tf_op jit(solution)/shard_map/jit(_where)/select_n | solution.py:515
  1.3 0.3 collective-permute-done.slab_ref
  1.7 0.0 copy-start.1
  1.7 0.0 copy-start.3
  1.7 0.0 copy-start.2
  1.7 0.0 copy-start.4
  1.8 2.9 %collective-permute-start.2 = (f32[2,16,640]{2,1,0:T(8,128)S(1)}, f32[2,16,640]{2,1,0:T(8,128)S(1)}, u32[]{:S(2)}, u32[]{:S(2)}) collective-permute-start(f32[2,16,640]{2,1,0:T(8,128)S(1)} %get-tuple-element.31), channel_id=1, source_target_pairs={{0,2},{1,3},{2,0},{3,1},{4,6},{5,7},{6,4},{7,5},{8,10},{9,11},{10,... | collective-permute-start | bytes 245768 | tf_op jit(solution)/shard_map/ppermute | solution.py:500
  4.7 0.0 copy-done
  4.7 0.0 copy-done.1
  4.7 0.0 copy-done.3
  4.7 0.8 %shard_map.64.packed_ref = f32[136,512]{1,0:T(8,128)S(1)} custom-call(f32[2,4,6]{2,1,0:T(4,128)S(1)} %copy-done.1, f32[2,2]{1,0:T(2,128)S(1)} %copy-done.3, f32[2,2,32,1024]{3,2,1,0:T(8,128)S(1)} %copy-done, f32[32,1024]{1,0:T(8,128)S(1)} %collective-permute-done.slab_ref), custom_call_target="tpu_custom_call" | custom-call | bytes 557056 | tf_op jit(solution)/shard_map/pallas_call | solution.py:449
  5.5 0.0 copy-done.2
  5.5 0.0 copy-done.4
  5.5 1.5 %shard_map.65 = (f32[2,2,2,5,32,128]{5,4,3,2,1,0:T(8,128)S(1)}, f32[2,4,6,8,128]{4,3,2,1,0:T(8,128)S(1)}, f32[2,8,128]{2,1,0:T(8,128)S(1)}, s32[3,8,128]{2,1,0:T(8,128)S(1)}) custom-call(s32[3]{0:T(128)S(1)} %copy-done.2, s32[2]{0:T(128)S(1)} %copy-done.4, f32[2,4,6]{2,1,0:T(4,128)S(1)} %copy-done.1, f32[2,2]{1,0:T(2,128)S(1)} %copy-done.3, ...), custom_call_target="tpu_custom_call" | custom-call | flops 4096000 | bytes 983040 | tf_op jit(solution)/shard_map/pallas_call | solution.py:462
  7.1 0.3 compare_reduce_fusion.3
  7.4 0.1 collective-permute-done.2
  7.5 0.1 select_select_fusion
  7.6 1.9 %collective-permute-start.3 = (f32[3,16,640]{2,1,0:T(8,128)S(1)}, f32[3,16,640]{2,1,0:T(8,128)S(1)}, u32[]{:S(2)}, u32[]{:S(2)}) collective-permute-start(f32[3,16,640]{2,1,0:T(8,128)S(1)} %select_select_fusion), channel_id=1, source_target_pairs={{0,4},{1,5},{2,6},{3,7},{4,0},{5,1},{6,2},{7,3},{8,12},{9,13},{10,... | collective-permute-start | bytes 368648 | tf_op jit(solution)/shard_map/ppermute | solution.py:500
  9.4 1.5 %collective-permute-start.1 = (f32[136,512]{1,0:T(8,128)S(1)}, f32[136,512]{1,0:T(8,128)S(1)}, u32[]{:S(2)}, u32[]{:S(2)}) collective-permute-start(f32[136,512]{1,0:T(8,128)S(1)} %shard_map.64.packed_ref), channel_id=1, source_target_pairs={{0,2},{1,3},{2,0},{3,1},{4,6},{5,7},{6,4},{7,5},{8,10},{9,11},{10,... | collective-permute-start | bytes 835592 | tf_op jit(solution)/shard_map/ppermute | solution.py:500
  10.9 1.7 %collective-permute-done.3 = f32[3,16,640]{2,1,0:T(8,128)S(1)} collective-permute-done((f32[3,16,640]{2,1,0:T(8,128)S(1)}, f32[3,16,640]{2,1,0:T(8,128)S(1)}, u32[]{:S(2)}, u32[]{:S(2)}) %collective-permute-start.3) | collective-permute-done | bytes 122912 | tf_op jit(solution)/shard_map/ppermute | solution.py:500
  12.7 0.1 broadcast_select_fusion
  12.8 3.7 %collective-permute-start.4 = (f32[3,16,640]{2,1,0:T(8,128)S(1)}, f32[3,16,640]{2,1,0:T(8,128)S(1)}, u32[]{:S(2)}, u32[]{:S(2)}) collective-permute-start(f32[3,16,640]{2,1,0:T(8,128)S(1)} %broadcast_select_fusion), channel_id=1, source_target_pairs={{0,12},{1,13},{2,14},{3,15},{4,8},{5,9},{6,10},{7,11},{8,4},{9,5},... | collective-permute-start | bytes 368648 | tf_op jit(solution)/shard_map/ppermute | solution.py:500
  16.5 0.8 %collective-permute-done.1.packed_ref = f32[136,512]{1,0:T(8,128)S(1)} collective-permute-done((f32[136,512]{1,0:T(8,128)S(1)}, f32[136,512]{1,0:T(8,128)S(1)}, u32[]{:S(2)}, u32[]{:S(2)}) %collective-permute-start.1) | collective-permute-done | bytes 278560 | tf_op jit(solution)/shard_map/ppermute | solution.py:500
  17.3 1.9 %shard_map.66 = (f32[2,2,2,5,32,128]{5,4,3,2,1,0:T(8,128)S(1)}, f32[2,4,6,8,128]{4,3,2,1,0:T(8,128)S(1)}, f32[2,8,128]{2,1,0:T(8,128)S(1)}, s32[3,8,128]{2,1,0:T(8,128)S(1)}) custom-call(s32[3]{0:T(128)S(1)} %copy-done.2, s32[2]{0:T(128)S(1)} %copy-done.4, f32[136,512]{1,0:T(8,128)S(1)} %collective-permute-done.1.packed_ref), custom_call_target="tpu_custom_call" | custom-call | flops 4096000 | bytes 983040 | tf_op jit(solution)/shard_map/pallas_call | solution.py:462
  19.2 0.2 compare_reduce_fusion.4
  19.3 0.3 collective-permute-done.4
  19.6 0.1 broadcast_select_fusion.1
  19.7 0.1 collective-permute-start.5
  19.8 1.3 %collective-permute-done.5 = f32[3,16,640]{2,1,0:T(8,128)S(1)} collective-permute-done((f32[3,16,640]{2,1,0:T(8,128)S(1)}, f32[3,16,640]{2,1,0:T(8,128)S(1)}, u32[]{:S(2)}, u32[]{:S(2)}) %collective-permute-start.5) | collective-permute-done | bytes 122912 | tf_op jit(solution)/shard_map/ppermute | solution.py:500
  21.1 9.0 %shard_map.67 = f32[3,32,640]{2,1,0:T(8,128)S(1)} custom-call(f32[2,2,2,5,32,128]{5,4,3,2,1,0:T(8,128)S(1)} %get-tuple-element.13.own_ref, f32[2,4,6,8,128]{4,3,2,1,0:T(8,128)S(1)} %get-tuple-element.14.own_taps_ref, f32[2,8,128]{2,1,0:T(8,128)S(1)} %get-tuple-element.15.own_rate_ref, f32[2,2,2,5,32,128]{5,4,3,2,1,0:T(8,128)S(1)} %get-tuple-element.16.near_ref, ...), custom_call_target="tpu_custom_call" | custom-call | tf_op jit(solution)/shard_map/pallas_call | solution.py:482
  30.2 0.2 collective-permute-start.6
  30.4 1.2 %collective-permute-done.6 = f32[3,16,512]{2,1,0:T(8,128)S(1)} collective-permute-done((f32[3,16,512]{2,1,0:T(8,128)S(1)}, f32[3,16,512]{2,1,0:T(8,128)S(1)}, u32[]{:S(2)}, u32[]{:S(2)}) %collective-permute-start.6) | collective-permute-done | bytes 98336 | tf_op jit(solution)/shard_map/ppermute | solution.py:500
  31.5 1.2 %collective-permute-start.7 = (f32[3,16,512]{2,1,0:T(8,128)S(1)}, f32[3,16,512]{2,1,0:T(8,128)S(1)}, u32[]{:S(2)}, u32[]{:S(2)}) collective-permute-start(f32[3,16,512]{2,1,0:T(8,128)S(1)} %select_add_fusion), channel_id=1, source_target_pairs={{0,4},{1,5},{2,6},{3,7},{4,0},{5,1},{6,2},{7,3},{8,12},{9,13},{10,... | collective-permute-start | bytes 294920 | tf_op jit(solution)/shard_map/ppermute | solution.py:500
  32.8 3.7 %collective-permute-done.7 = f32[3,16,512]{2,1,0:T(8,128)S(1)} collective-permute-done((f32[3,16,512]{2,1,0:T(8,128)S(1)}, f32[3,16,512]{2,1,0:T(8,128)S(1)}, u32[]{:S(2)}, u32[]{:S(2)}) %collective-permute-start.7) | collective-permute-done | bytes 98336 | tf_op jit(solution)/shard_map/ppermute | solution.py:500
  36.5 3.7 %collective-permute-start.8 = (f32[3,16,512]{2,1,0:T(8,128)S(1)}, f32[3,16,512]{2,1,0:T(8,128)S(1)}, u32[]{:S(2)}, u32[]{:S(2)}) collective-permute-start(f32[3,16,512]{2,1,0:T(8,128)S(1)} %add.10), channel_id=1, source_target_pairs={{0,12},{1,13},{2,14},{3,15},{4,8},{5,9},{6,10},{7,11},{8,4},{9,5},... | collective-permute-start | bytes 294920 | tf_op jit(solution)/shard_map/ppermute | solution.py:500
  40.2 2.8 %collective-permute-done.8 = f32[3,16,512]{2,1,0:T(8,128)S(1)} collective-permute-done((f32[3,16,512]{2,1,0:T(8,128)S(1)}, f32[3,16,512]{2,1,0:T(8,128)S(1)}, u32[]{:S(2)}, u32[]{:S(2)}) %collective-permute-start.8) | collective-permute-done | bytes 98336 | tf_op jit(solution)/shard_map/ppermute | solution.py:500
  43.0 0.1 select_reduce_fusion.3
  43.1 1.7 %collective-permute-start.9 = (f32[2,16,512]{2,1,0:T(8,128)S(1)}, f32[2,16,512]{2,1,0:T(8,128)S(1)}, u32[]{:S(2)}, u32[]{:S(2)}) collective-permute-start(f32[2,16,512]{2,1,0:T(8,128)S(1)} %pad_maximum_fusion.1), channel_id=1, source_target_pairs={{0,2},{1,3},{2,0},{3,1},{4,6},{5,7},{6,4},{7,5},{8,10},{9,11},{10,... | collective-permute-start | bytes 196616 | tf_op jit(solution)/shard_map/ppermute | solution.py:500
  44.8 2.6 %collective-permute-done.9 = f32[2,16,512]{2,1,0:T(8,128)S(1)} collective-permute-done((f32[2,16,512]{2,1,0:T(8,128)S(1)}, f32[2,16,512]{2,1,0:T(8,128)S(1)}, u32[]{:S(2)}, u32[]{:S(2)}) %collective-permute-start.9) | collective-permute-done | bytes 65568 | tf_op jit(solution)/shard_map/ppermute | solution.py:500
  47.5 0.1 collective-permute-start.10
  47.6 1.2 %collective-permute-done.10 = f32[16,1024]{1,0:T(8,128)S(1)} collective-permute-done((f32[16,1024]{1,0:T(8,128)S(1)}, f32[16,1024]{1,0:T(8,128)S(1)}, u32[]{:S(2)}, u32[]{:S(2)}) %collective-permute-start.10) | collective-permute-done | bytes 65568 | tf_op jit(solution)/shard_map/ppermute | solution.py:500
  48.8 0.7 %maximum_select_fusion.2 = f32[1,32,1024]{2,1,0:T(8,128)} fusion(f32[1,16,1024]{2,1,0:T(8,128)S(1)} %get-tuple-element.30, f32[1,16,1024]{2,1,0:T(8,128)S(1)} %bitcast.23, pred[]{:T(512)S(6)} %ne.8), kind=kLoop, calls=%fused_computation.5 | loop fusion | flops 98304 | bytes 262145 | tf_op jit(solution)/shard_map/jit(_where)/select_n | solution.py:524
  (13 shorter events, 0.2 us)
Async XLA Ops:
  0.0 4.7 %copy-start = (f32[2,2,32,1024]{3,2,1,0:T(8,128)S(1)}, f32[2,2,32,1024]{3,2,1,0:T(8,128)}, u32[]{:S(2)}) copy-start(f32[2,2,32,1024]{3,2,1,0:T(8,128)} %receiver_ref.3) | copy-start | bytes 1572868
  0.0 1.6 %collective-permute-start = (f32[32,1024]{1,0:T(8,128)}, f32[32,1024]{1,0:T(8,128)S(1)}, u32[]{:S(2)}, u32[]{:S(2)}) collective-permute-start(f32[32,1024]{1,0:T(8,128)} %bitcast.18), channel_id=1, source_target_pairs={{0,1},{1,0},{2,3},{3,2},{4,5},{5,4},{6,7},{7,6},{8,9},{9,8},{10,11... | collective-permute-start | bytes 393224 | tf_op jit(solution)/shard_map/ppermute | solution.py:500
  1.7 3.0 %copy-start.1 = (f32[2,4,6]{2,1,0:T(4,128)S(1)}, f32[2,4,6]{2,1,0:T(4,128)}, u32[]{:S(2)}) copy-start(f32[2,4,6]{2,1,0:T(4,128)} %taps_ref.3) | copy-start | bytes 580
  1.7 3.0 %copy-start.3 = (f32[2,2]{1,0:T(2,128)S(1)}, f32[2,2]{1,0:T(2,128)}, u32[]{:S(2)}) copy-start(f32[2,2]{1,0:T(2,128)} %spectrum_ref.3) | copy-start | bytes 52
  1.7 3.8 %copy-start.2 = (s32[3]{0:T(128)S(1)}, s32[3]{0:T(128)}, u32[]{:S(2)}) copy-start(s32[3]{0:T(128)} %owner_ref.3) | copy-start | bytes 40
  1.7 3.8 %copy-start.4 = (s32[2]{0:T(128)S(1)}, s32[2]{0:T(128)}, u32[]{:S(2)}) copy-start(s32[2]{0:T(128)} %position_ref.3) | copy-start | bytes 28
  1.8 5.7 %collective-permute-start.2 = (f32[2,16,640]{2,1,0:T(8,128)S(1)}, f32[2,16,640]{2,1,0:T(8,128)S(1)}, u32[]{:S(2)}, u32[]{:S(2)}) collective-permute-start(f32[2,16,640]{2,1,0:T(8,128)S(1)} %get-tuple-element.31), channel_id=1, source_target_pairs={{0,2},{1,3},{2,0},{3,1},{4,6},{5,7},{6,4},{7,5},{8,10},{9,11},{10,... | collective-permute-start | bytes 245768 | tf_op jit(solution)/shard_map/ppermute | solution.py:500
  7.6 5.1 %collective-permute-start.3 = (f32[3,16,640]{2,1,0:T(8,128)S(1)}, f32[3,16,640]{2,1,0:T(8,128)S(1)}, u32[]{:S(2)}, u32[]{:S(2)}) collective-permute-start(f32[3,16,640]{2,1,0:T(8,128)S(1)} %select_select_fusion), channel_id=1, source_target_pairs={{0,4},{1,5},{2,6},{3,7},{4,0},{5,1},{6,2},{7,3},{8,12},{9,13},{10,... | collective-permute-start | bytes 368648 | tf_op jit(solution)/shard_map/ppermute | solution.py:500
  9.4 7.9 %collective-permute-start.1 = (f32[136,512]{1,0:T(8,128)S(1)}, f32[136,512]{1,0:T(8,128)S(1)}, u32[]{:S(2)}, u32[]{:S(2)}) collective-permute-start(f32[136,512]{1,0:T(8,128)S(1)} %shard_map.64.packed_ref), channel_id=1, source_target_pairs={{0,2},{1,3},{2,0},{3,1},{4,6},{5,7},{6,4},{7,5},{8,10},{9,11},{10,... | collective-permute-start | bytes 835592 | tf_op jit(solution)/shard_map/ppermute | solution.py:500
  12.8 6.8 %collective-permute-start.4 = (f32[3,16,640]{2,1,0:T(8,128)S(1)}, f32[3,16,640]{2,1,0:T(8,128)S(1)}, u32[]{:S(2)}, u32[]{:S(2)}) collective-permute-start(f32[3,16,640]{2,1,0:T(8,128)S(1)} %broadcast_select_fusion), channel_id=1, source_target_pairs={{0,12},{1,13},{2,14},{3,15},{4,8},{5,9},{6,10},{7,11},{8,4},{9,5},... | collective-permute-start | bytes 368648 | tf_op jit(solution)/shard_map/ppermute | solution.py:500
  19.7 1.4 %collective-permute-start.5 = (f32[3,16,640]{2,1,0:T(8,128)S(1)}, f32[3,16,640]{2,1,0:T(8,128)S(1)}, u32[]{:S(2)}, u32[]{:S(2)}) collective-permute-start(f32[3,16,640]{2,1,0:T(8,128)S(1)} %broadcast_select_fusion.1), channel_id=1, source_target_pairs={{0,1},{1,0},{2,3},{3,2},{4,5},{5,4},{6,7},{7,6},{8,9},{9,8},{10,11... | collective-permute-start | bytes 368648 | tf_op jit(solution)/shard_map/ppermute | solution.py:500
  30.2 1.4 %collective-permute-start.6 = (f32[3,16,512]{2,1,0:T(8,128)S(1)}, f32[3,16,512]{2,1,0:T(8,128)S(1)}, u32[]{:S(2)}, u32[]{:S(2)}) collective-permute-start(f32[3,16,512]{2,1,0:T(8,128)S(1)} %slice_select_fusion.1), channel_id=1, source_target_pairs={{0,1},{1,0},{2,3},{3,2},{4,5},{5,4},{6,7},{7,6},{8,9},{9,8},{10,11... | collective-permute-start | bytes 294920 | tf_op jit(solution)/shard_map/ppermute | solution.py:500
  31.5 4.9 %collective-permute-start.7 = (f32[3,16,512]{2,1,0:T(8,128)S(1)}, f32[3,16,512]{2,1,0:T(8,128)S(1)}, u32[]{:S(2)}, u32[]{:S(2)}) collective-permute-start(f32[3,16,512]{2,1,0:T(8,128)S(1)} %select_add_fusion), channel_id=1, source_target_pairs={{0,4},{1,5},{2,6},{3,7},{4,0},{5,1},{6,2},{7,3},{8,12},{9,13},{10,... | collective-permute-start | bytes 294920 | tf_op jit(solution)/shard_map/ppermute | solution.py:500
  36.5 6.5 %collective-permute-start.8 = (f32[3,16,512]{2,1,0:T(8,128)S(1)}, f32[3,16,512]{2,1,0:T(8,128)S(1)}, u32[]{:S(2)}, u32[]{:S(2)}) collective-permute-start(f32[3,16,512]{2,1,0:T(8,128)S(1)} %add.10), channel_id=1, source_target_pairs={{0,12},{1,13},{2,14},{3,15},{4,8},{5,9},{6,10},{7,11},{8,4},{9,5},... | collective-permute-start | bytes 294920 | tf_op jit(solution)/shard_map/ppermute | solution.py:500
  43.1 4.3 %collective-permute-start.9 = (f32[2,16,512]{2,1,0:T(8,128)S(1)}, f32[2,16,512]{2,1,0:T(8,128)S(1)}, u32[]{:S(2)}, u32[]{:S(2)}) collective-permute-start(f32[2,16,512]{2,1,0:T(8,128)S(1)} %pad_maximum_fusion.1), channel_id=1, source_target_pairs={{0,2},{1,3},{2,0},{3,1},{4,6},{5,7},{6,4},{7,5},{8,10},{9,11},{10,... | collective-permute-start | bytes 196616 | tf_op jit(solution)/shard_map/ppermute | solution.py:500
  47.5 1.3 %collective-permute-start.10 = (f32[16,1024]{1,0:T(8,128)S(1)}, f32[16,1024]{1,0:T(8,128)S(1)}, u32[]{:S(2)}, u32[]{:S(2)}) collective-permute-start(f32[16,1024]{1,0:T(8,128)S(1)} %get-tuple-element.29), channel_id=1, source_target_pairs={{0,1},{1,0},{2,3},{3,2},{4,5},{5,4},{6,7},{7,6},{8,9},{9,8},{10,11... | collective-permute-start | bytes 196616 | tf_op jit(solution)/shard_map/ppermute | solution.py:500
